TPU v7x, 32 devices: a whole 2x2x4 slice. The times are simulated.
32 devices in a mesh: dev: 32 (over z, y, x, core).
Axes of the slice: x: 2, y: 2, z: 4, core: 2. Of those that a mesh axis runs over, the one named last changes fastest.
Arguments:
- tile_lists: int32 [768, 512], P('dev'), may hold values from -1 to 2047, as said below
- send_rows: int32 [32, 2048], P('dev'), may hold values from -1 to 2047, as said below
- centres: float32 [2, 65536], P(None, 'dev'), may hold values from -12 to 12
- conic: float32 [2, 65536], P(None, 'dev'), may hold values from 0.015625 to 0.25
- rho: float32 [1, 65536], P(None, 'dev'), may hold values from -0.6 to 0.6
- opacity: float32 [1, 65536], P(None, 'dev'), may hold values from 0.002 to 0.03
- colors: float32 [3, 65536], P(None, 'dev'), may hold values from 0 to 1
- target: float32 [3, 512, 384], P(None, 'dev'), may hold values from 0 to 1
Outputs:
- rendered: float32 [3, 512, 384], P(None, 'dev')
- grads: float32 [9, 65536], P(None, 'dev')
Inputs may be any that keep to these rules, and one draw needn't show every extreme that they name: `tile_lists`: row t belongs to strip t // 24. An entry is -1 only after all live entries of its row; a live entry s * 64 + m names a slot m that owner s fills for that strip. Some row has no -1. `send_rows`: entry [s, r * 64 + m] is the local index on owner s of the Gaussian in slot m for strip r, or -1 for an unused slot. The used slots of an owner and strip come first, are distinct, and number at least 32; some owner fills all 64 slots for some strip.
All inputs are finite; a program needn't handle non-finite values.
Results may differ from a plain program's by a relative error of at most 0.0003.
Values sent between devices are 32-bit elements; how exact they have to be, the bound alone decides.
No kernel may reach another device: no remote copies, remote signals or barrier semaphores. Data moves between devices by JAX's collectives and lax.ppermute only.
A program may use at most 256 MiB of HBM per device.

v0:
```python
import jax
import jax.numpy as jnp
from jax import lax
from jax.sharding import PartitionSpec as P


def with_halo(value, sides, width):
    for axis, dim in sides:
        size, length = (lax.axis_size(axis), value.shape[dim])
        up = [(i, (i + 1) % size) for i in range(size - 1)]
        down = [(j, i) for i, j in up]
        last = lax.slice_in_dim(value, length - width, length, axis=dim)
        first = lax.slice_in_dim(value, 0, width, axis=dim)
        before = lax.ppermute(last, axis, up)
        after = lax.ppermute(first, axis, down)
        value = jnp.concatenate([before, value, after], axis=dim)
    return value


def filter_taps():
    offsets = jnp.arange(11).astype(jnp.float32) - 5.0
    taps = jnp.exp(-offsets * offsets / 4.5)
    return taps / jnp.sum(taps)


def blur_strip(values):
    taps = filter_taps()
    count = values.shape[1] - 10
    width = values.shape[2]
    rows_done = taps[0] * values[:, 0:count]
    for shift in range(1, 11):
        rows_done = rows_done + taps[shift] * values[:, shift : shift + count]
    padded = jnp.pad(rows_done, ((0, 0), (0, 0), (5, 5)))
    result = taps[0] * padded[:, :, 0:width]
    for shift in range(1, 11):
        result = result + taps[shift] * padded[:, :, shift : shift + width]
    return result


def local_loss(render_pad, target_pad):
    mean_r = blur_strip(render_pad)
    mean_t = blur_strip(target_pad)
    var_r = blur_strip(render_pad * render_pad) - mean_r * mean_r
    var_t = blur_strip(target_pad * target_pad) - mean_t * mean_t
    covar = blur_strip(render_pad * target_pad) - mean_r * mean_t
    ssim = (
        (2.0 * mean_r * mean_t + 0.0001)
        * (2.0 * covar + 0.0009)
        / ((mean_r * mean_r + mean_t * mean_t + 0.0001) * (var_r + var_t + 0.0009))
    )
    centre_r = render_pad[:, 5:-5]
    centre_t = target_pad[:, 5:-5]
    diff = centre_r - centre_t
    return jnp.sum(0.8 * diff * diff + 0.2 * (1.0 - ssim))


def composite(params, live, tile, lower):
    count = tile * tile
    pixel = jnp.arange(count)
    vert = (pixel // tile).astype(jnp.float32) - (tile - 1) / 2.0
    horiz = (pixel % tile).astype(jnp.float32) - (tile - 1) / 2.0
    delta_x = horiz[None, :] - params[0][:, None]
    delta_y = vert[None, :] - params[1][:, None]
    cross = params[4] * jnp.sqrt(params[2] * params[3])
    quad = (
        params[2][:, None] * delta_x * delta_x
        + 2.0 * cross[:, None] * delta_x * delta_y
        + params[3][:, None] * delta_y * delta_y
    )
    alpha = jnp.where(live[:, None], params[5][:, None] * jnp.exp(-0.5 * quad), 0.0)
    logs = jnp.log1p(-alpha)
    before = jnp.dot(
        lower, logs, precision=lax.Precision.HIGHEST, preferred_element_type=jnp.float32
    )
    weight = alpha * jnp.exp(before)
    return jnp.dot(
        params[6:9], weight, precision=lax.Precision.HIGHEST, preferred_element_type=jnp.float32
    )


def shards(tile_lists, send_rows, centres, conic, rho, opacity, colors, target):
    slot_count = send_rows.shape[1]
    owned_count = centres.shape[1]
    tile = target.shape[1]
    strip_tiles = tile_lists.shape[0]
    list_len = tile_lists.shape[1]
    local_params = jnp.concatenate([centres, conic, rho, opacity, colors], axis=0)
    nine = local_params.shape[0]
    owned = send_rows[0]
    taken = jnp.take(local_params, jnp.maximum(owned, 0), axis=1)
    packed = jnp.where(owned[None, :] >= 0, taken, 0.0)
    received = lax.all_to_all(packed, "dev", split_axis=1, concat_axis=1, tiled=True)
    live = tile_lists >= 0
    entry = jnp.maximum(tile_lists, 0)
    gathered = jnp.take(received, entry, axis=1).transpose(1, 0, 2)
    steps_idx = jnp.arange(list_len)
    lower = (steps_idx[:, None] > steps_idx[None, :]).astype(jnp.float32)

    def render_tile(args):
        return composite(args[0], args[1], tile, lower)

    colour_tiles = lax.map(render_tile, (gathered, live))
    image = (
        colour_tiles.reshape(strip_tiles, 3, tile, tile)
        .transpose(1, 2, 0, 3)
        .reshape(3, tile, strip_tiles * tile)
    )
    stacked = jnp.concatenate([image, target], axis=0)
    padded = with_halo(stacked, (("dev", 1),), 5)
    target_pad = padded[3:]
    loss_value, pull = jax.vjp(lambda rend: local_loss(rend, target_pad), padded[:3])
    grad_pad = pull(jnp.ones_like(loss_value))[0]
    rims = jnp.concatenate([grad_pad[:, :5], grad_pad[:, -5:]], axis=1)
    arrived = with_halo(rims, (("dev", 1),), 5)
    pixel_grad = grad_pad[:, 5:-5]
    pixel_grad = pixel_grad + jnp.pad(arrived[:, :5], ((0, 0), (0, tile - 5), (0, 0)))
    pixel_grad = pixel_grad + jnp.pad(arrived[:, -5:], ((0, 0), (tile - 5, 0), (0, 0)))
    cot_tiles = (
        pixel_grad.reshape(3, tile, strip_tiles, tile)
        .transpose(2, 0, 1, 3)
        .reshape(strip_tiles, 3, tile * tile)
    )

    def back_tile(args):
        params_tile, mask, cotangent = args
        _, back = jax.vjp(lambda chosen: composite(chosen, mask, tile, lower), params_tile)
        return jnp.where(mask[None, :], back(cotangent)[0], 0.0)

    entry_grads = lax.map(back_tile, (gathered, live, cot_tiles))
    flat_grads = entry_grads.transpose(1, 0, 2).reshape(nine, strip_tiles * list_len)
    target_slot = jnp.where(live, tile_lists, slot_count).reshape(strip_tiles * list_len)
    slot_grads = (
        jnp.zeros((nine, slot_count), jnp.float32).at[:, target_slot].add(flat_grads, mode="drop")
    )
    returned = lax.all_to_all(slot_grads, "dev", split_axis=1, concat_axis=1, tiled=True)
    home = jnp.where(owned >= 0, owned, owned_count)
    grads = jnp.zeros((nine, owned_count), jnp.float32).at[:, home].add(returned, mode="drop")
    return (image, grads)


def solution(mesh):
    return jax.shard_map(
        shards,
        mesh=mesh,
        in_specs=(
            P("dev", None),
            P("dev", None),
            P(None, "dev"),
            P(None, "dev"),
            P(None, "dev"),
            P(None, "dev"),
            P(None, "dev"),
            P(None, "dev", None),
        ),
        out_specs=(P(None, "dev", None), P(None, "dev")),
        check_vma=False,
    )
```

profile of v0, /device:TPU:0, one launch (start us, length us, event | category | flops | bytes accessed | tf_op | source)
XLA Modules:
  0.0 457.9 jit_solution(2985860970634943561)
XLA Ops:
  2.1 1.7 concatenate.33
  4.2 5.5 %gather_fusion = f32[2048,9]{1,0:T(8,128)S(1)} fusion(f32[9,2048]{0,1:T(8,128)S(1)} %copy.44, s32[2048]{0:T(1024)S(1)} %broadcast_clamp_fusion.1), kind=kCustom, calls=%fused_computation | custom fusion | bytes 155648 | tf_op jit(solution)/shard_map/jit(_take)/gather | solution.py:90
  11.1 7.3 %all-to-all-start = ((f32[32,1,576]{2,1,0:T(1,128)}), f32[32,1,576]{2,1,0:T(1,128)S(1)}, u32[]{:S(2)}, u32[]{:S(2)}) async-start(f32[32,1,576]{2,1,0:T(1,128)} %reshape.524), calls=%async_computation | async-start | bytes 163840 | tf_op jit(solution)/shard_map/all_to_all | solution.py:92
  21.4 4.5 all-to-all-done
  27.8 41.0 %gather_fusion.1 = f32[12288,9]{1,0:T(8,128)} fusion(f32[9,2048]{0,1:T(8,128)S(1)} %bitcast.182, s32[12288]{0:T(1024)S(1)} %broadcast_clamp_fusion), kind=kCustom, calls=%fused_computation.1 | custom fusion | bytes 933888 | tf_op jit(solution)/shard_map/jit(_take)/gather | solution.py:95
  68.8 4.4 copy.47
  73.4 55.9 %while.29 = (s32[]{:T(128)}, f32[24,3,256]{2,0,1:T(8,128)S(1)}, f32[24,9,512]{2,1,0:T(8,128)S(1)}, pred[24,512]{1,0:T(8,128)(4,1)S(1)}, s32[]{:T(128)}, /*index=...) while((s32[]{:T(128)}, f32[24,3,256]{2,0,1:T(8,128)S(1)}, ...), condition=%wide.region_1.2_spmd.clone, body=%wide.region_0.1_spmd.clone.sunk | while | flops 814224896 | bytes 1123045 | solution.py:102
  82.8 1.6 fusion.361
  85.2 1.6 fusion.361
  89.8 1.6 fusion.361
  92.2 1.6 fusion.361
  96.8 1.6 fusion.361
  99.1 1.6 fusion.361
  103.8 1.6 fusion.361
  106.1 1.6 fusion.361
  110.8 1.6 fusion.361
  113.1 1.6 fusion.361
  117.8 1.6 fusion.361
  120.1 1.6 fusion.361
  130.0 2.0 collective-permute-start
  141.1 6.9 %fusion.312 = f32[3,16,384]{2,1,0:T(8,128)S(1)} fusion(f32[3,26,384]{2,1,0:T(8,128)S(1)} %get-tuple-element.331, f32[]{:T(128)} %bitcast.20, f32[]{:T(128)} %bitcast.19, f32[]{:T(128)} %bitcast.18, f32[]{:T(128)} %bitcast.17, f32[]{:T(128)} %bitcast.16, f32[]{:T(128)} %bitcast.15, f32[]{:T(128)} %bitcast.14, f32[]{:T(128)} %bitcast.13, f32[]{:T(128)} %bitcast.12, ...), kind=kLoop, calls=%fused_computation.495 | loop fusion | flops 387072 | bytes 884780 | tf_op jit(solution)/shard_map/jvp()/add | solution.py:32
  148.0 6.9 %fusion.302 = f32[3,16,384]{2,1,0:T(8,128)S(1)} fusion(f32[3,26,384]{2,1,0:T(8,128)S(1)} %get-tuple-element.330, f32[]{:T(128)} %bitcast.20, f32[]{:T(128)} %bitcast.19, f32[]{:T(128)} %bitcast.18, f32[]{:T(128)} %bitcast.17, f32[]{:T(128)} %bitcast.16, f32[]{:T(128)} %bitcast.15, f32[]{:T(128)} %bitcast.14, f32[]{:T(128)} %bitcast.13, f32[]{:T(128)} %bitcast.12, ...), kind=kLoop, calls=%fused_computation.474 | loop fusion | flops 387072 | bytes 884780 | tf_op jit(solution)/shard_map/jvp()/add | solution.py:32
  155.0 6.9 %fusion.292 = f32[3,16,384]{2,1,0:T(8,128)S(1)} fusion(f32[3,26,384]{2,1,0:T(8,128)S(1)} %get-tuple-element.329, f32[]{:T(128)} %bitcast.20, f32[]{:T(128)} %bitcast.19, f32[]{:T(128)} %bitcast.18, f32[]{:T(128)} %bitcast.17, f32[]{:T(128)} %bitcast.16, f32[]{:T(128)} %bitcast.15, f32[]{:T(128)} %bitcast.14, f32[]{:T(128)} %bitcast.13, f32[]{:T(128)} %bitcast.12, ...), kind=kLoop, calls=%fused_computation.447 | loop fusion | flops 387072 | bytes 884780 | tf_op jit(solution)/shard_map/jvp()/add | solution.py:32
  161.9 7.0 %fusion.245 = f32[3,16,384]{2,1,0:T(8,128)S(1)} fusion(f32[6,16,384]{2,1,0:T(8,128)S(1)} %get-tuple-element.337, f32[6,5,384]{2,1,0:T(8,128)S(1)} %collective-permute-done.1, f32[6,5,384]{2,1,0:T(8,128)S(1)} %collective-permute-done, f32[3,16,384]{2,1,0:T(8,128)S(1)} %reshape.476, f32[]{:T(128)} %bitcast.20, f32[]{:T(128)} %bitcast.19, f32[]{:T(128)} %bitcast.18, ...), kind=kLoop, calls=%fused_computation.386 | loop fusion | flops 571392 | bytes 387116 | tf_op jit(solution)/shard_map/jvp()/add | solution.py:32
  168.9 7.0 %fusion.238 = f32[3,16,384]{2,1,0:T(8,128)S(1)} fusion(f32[6,16,384]{2,1,0:T(8,128)S(1)} %get-tuple-element.337, f32[6,5,384]{2,1,0:T(8,128)S(1)} %collective-permute-done.1, f32[6,5,384]{2,1,0:T(8,128)S(1)} %collective-permute-done, f32[3,16,384]{2,1,0:T(8,128)S(1)} %copy-done.1, f32[]{:T(128)} %bitcast.20, f32[]{:T(128)} %bitcast.19, f32[]{:T(128)} %bitcast.18, ...), kind=kLoop, calls=%fused_computation.379 | loop fusion | flops 571392 | bytes 387116 | tf_op jit(solution)/shard_map/jvp()/add | solution.py:32
  175.9 7.7 %broadcast_multiply_fusion.11 = (f32[3,16,384]{2,1,0:T(8,128)S(1)}, f32[3,16,384]{2,1,0:T(8,128)S(1)}, f32[3,16,384]{2,1,0:T(8,128)S(1)}, f32[3,16,384]{2,1,0:T(8,128)S(1)}, f32[3,16,384]{2,1,0:T(8,128)S(1)}) fusion(f32[]{:T(128)S(6)} %mul.1560, f32[3,16,384]{2,1,0:T(8,128)S(1)} %fusion.302, f32[]{:T(128)} %bitcast.10, f32[]{:T(128)} %bitcast.20, ...), kind=kLoop, calls=%fused_computation.543 | loop fusion | flops 1824768 | bytes 663600 | tf_op jit(solution)/shard_map/transpose(jvp())/mul | solution.py:36
  183.6 7.1 %broadcast_multiply_fusion.64 = (f32[3,16,384]{2,1,0:T(8,128)S(1)}, f32[3,16,384]{2,1,0:T(8,128)S(1)}, f32[3,16,384]{2,1,0:T(8,128)S(1)}) fusion(f32[]{:T(128)} %bitcast.10, f32[3,16,384]{2,1,0:T(8,128)S(1)} %get-tuple-element.301, f32[3,16,384]{2,1,0:T(8,128)S(1)} %get-tuple-element.302, f32[3,16,384]{2,1,0:T(8,128)S(1)} %get-tuple-element.300, ...), kind=kLoop, calls=%fused_computation.596 | loop fusion | flops 755712 | bytes 516140 | tf_op jit(solution)/shard_map/transpose(jvp())/mul | solution.py:36
  190.7 5.1 %broadcast_multiply_fusion.24 = (f32[3,16,384]{2,1,0:T(8,128)S(1)}, f32[3,16,384]{2,1,0:T(8,128)S(1)}, f32[3,16,384]{2,1,0:T(8,128)S(1)}, f32[3,16,384]{2,1,0:T(...) fusion(f32[3,16,384]{2,1,0:T(8,128)S(1)} %get-tuple-element.306, ...), kind=kLoop, calls=%fused_computation.556 | loop fusion | flops 147456 | bytes 663584 | tf_op jit(solution)/shard_map/transpose(jvp())/mul | solution.py:36
  195.8 1.9 broadcast_multiply_fusion.10
  199.0 6.3 %broadcast_multiply_fusion.15 = (f32[3,16,384]{2,1,0:T(8,128)S(1)}, f32[3,16,384]{2,1,0:T(8,128)S(1)}, f32[3,16,384]{2,1,0:T(8,128)S(1)}, f32[3,16,384]{2,1,0:T(...) fusion(f32[3,16,384]{2,1,0:T(8,128)S(1)} %get-tuple-element.418, ...), kind=kLoop, calls=%fused_computation.547 | loop fusion | flops 184320 | bytes 811048 | tf_op jit(solution)/shard_map/transpose(jvp())/mul | solution.py:32
  205.3 6.3 %broadcast_multiply_fusion.13 = (f32[3,16,384]{2,1,0:T(8,128)S(1)}, f32[3,16,384]{2,1,0:T(8,128)S(1)}, f32[3,16,384]{2,1,0:T(8,128)S(1)}, f32[3,16,384]{2,1,0:T(...) fusion(f32[3,16,384]{2,1,0:T(8,128)S(1)} %get-tuple-element.304, ...), kind=kLoop, calls=%fused_computation.545 | loop fusion | flops 184320 | bytes 811048 | tf_op jit(solution)/shard_map/transpose(jvp())/mul | solution.py:32
  211.6 6.3 %broadcast_multiply_fusion.12 = (f32[3,16,384]{2,1,0:T(8,128)S(1)}, f32[3,16,384]{2,1,0:T(8,128)S(1)}, f32[3,16,384]{2,1,0:T(8,128)S(1)}, f32[3,16,384]{2,1,0:T(...) fusion(f32[3,16,384]{2,1,0:T(8,128)S(1)} %get-tuple-element.359, ...), kind=kLoop, calls=%fused_computation.544 | loop fusion | flops 184320 | bytes 811048 | tf_op jit(solution)/shard_map/transpose(jvp())/mul | solution.py:36
  218.9 6.3 %broadcast_multiply_fusion.16 = (f32[3,16,384]{2,1,0:T(8,128)S(1)}, f32[3,16,384]{2,1,0:T(8,128)S(1)}, f32[3,16,384]{2,1,0:T(8,128)S(1)}, f32[3,16,384]{2,1,0:T(...) fusion(f32[3,16,384]{2,1,0:T(8,128)S(1)} %get-tuple-element.309, ...), kind=kLoop, calls=%fused_computation.548 | loop fusion | flops 184320 | bytes 811048 | tf_op jit(solution)/shard_map/transpose(jvp())/mul | solution.py:32
  225.6 3.0 collective-permute-start.2
  230.2 2.7 collective-permute-done.3
  233.6 121.9 %while.30 = (s32[]{:T(128)}, f32[24,9,512]{2,1,0:T(8,128)S(1)}, pred[24,512]{1,0:T(8,128)(4,1)S(1)}, f32[24,3,256]{2,1,0:T(4,128)S(1)}, f32[24,9,512]{2,1,0:T(8,...) while((s32[]{:T(128)}, f32[24,9,512]{2,1,0:T(8,128)S(1)}, ...), condition=%wide.region_10.11_spmd.clone.clone, body=%wide.region_3.10_spmd.clone.clone.sunk | while | flops 1632681984 | bytes 2828525 | solution.py:129
  235.7 2.1 fusion.370
  240.8 2.1 fusion.370
  245.9 2.1 fusion.370
  251.0 2.1 fusion.370
  256.0 2.1 fusion.370
  261.1 2.1 fusion.370
  266.2 2.1 fusion.370
  271.3 2.1 fusion.370
  276.4 2.1 fusion.370
  281.4 2.1 fusion.370
  286.5 2.1 fusion.370
  291.6 2.1 fusion.370
  296.7 2.1 fusion.370
  301.8 2.1 fusion.370
  306.8 2.1 fusion.370
  311.9 2.1 fusion.370
  317.0 2.1 fusion.370
  322.1 2.1 fusion.370
  327.2 2.1 fusion.370
  332.2 2.1 fusion.370
  337.3 2.1 fusion.370
  342.4 2.1 fusion.370
  347.5 2.1 fusion.370
  352.6 2.1 fusion.370
  356.3 4.0 copy.53
  360.3 66.2 %scatter_custom_fusion = f32[9,2048]{0,1:T(8,128)S(1)} fusion(s32[12288]{0:T(1024)S(1)} %bitcast.229, f32[12288,9]{1,0:T(8,128)} %copy.53, f32[]{:T(128)} %constant.243.clone.1), kind=kCustom, calls=%fused_computation.177 | custom fusion | flops 110592 | bytes 74240 | tf_op jit(solution)/shard_map/scatter-add | solution.py:133
  427.1 16.6 %all_to_all.21 = f32[32,1,576]{2,1,0:T(1,128)S(1)} all-to-all(f32[32,1,576]{2,1,0:T(1,128)S(1)} %reshape.526), channel_id=1, replica_groups=mesh['dev'=32] {'dev'}, dimensions={0} | all-to-all | bytes 147456 | tf_op jit(solution)/shard_map/all_to_all | solution.py:135
  445.1 11.7 %scatter_custom_fusion.1 = f32[9,2048]{0,1:T(8,128)S(1)} fusion(s32[2048]{0:T(1024)S(1)} %bitcast.231, f32[2048,9]{1,0:T(8,128)S(1)} %copy.56, f32[]{:T(128)} %constant.243.clone.1), kind=kCustom, calls=%fused_computation.175 | custom fusion | flops 18432 | bytes 73732 | tf_op jit(solution)/shard_map/scatter-add | solution.py:137
  (556 shorter events, 125.0 us)
Async XLA Ops:
  11.1 14.9 %all-to-all-start = ((f32[32,1,576]{2,1,0:T(1,128)}), f32[32,1,576]{2,1,0:T(1,128)S(1)}, u32[]{:S(2)}, u32[]{:S(2)}) async-start(f32[32,1,576]{2,1,0:T(1,128)} %reshape.524), calls=%async_computation | async-start | bytes 163840 | tf_op jit(solution)/shard_map/all_to_all | solution.py:92
  73.4 56.6 %copy-start.1 = (f32[3,16,384]{2,1,0:T(8,128)S(1)}, f32[3,16,384]{2,1,0:T(8,128)}, u32[]{:S(2)}) copy-start(f32[3,16,384]{2,1,0:T(8,128)} %param.19) | copy-start | bytes 221188
  130.0 81.6 %copy-start = (f32[3,16,384]{2,1,0:T(8,128)}, f32[3,16,384]{2,1,0:T(8,128)S(1)}, u32[]{:S(2)}) copy-start(f32[3,16,384]{2,1,0:T(8,128)S(1)} %reshape.476) | copy-start | bytes 221188
  130.0 10.9 %collective-permute-start = (f32[6,5,384]{2,1,0:T(8,128)S(1)}, f32[6,5,384]{2,1,0:T(8,128)S(1)}, u32[]{:S(2)}, u32[]{:S(2)}) collective-permute-start(f32[6,5,384]{2,1,0:T(8,128)S(1)} %get-tuple-element.334), channel_id=1, source_target_pairs={{0,1},{1,2},{2,3},{3,4},{4,5},{5,6},{6,7},{7,8},{8,9},{9,10},{10,1... | collective-permute-start | bytes 138248 | tf_op jit(solution)/shard_map/ppermute | solution.py:14
  132.1 8.9 %collective-permute-start.1 = (f32[6,5,384]{2,1,0:T(8,128)S(1)}, f32[6,5,384]{2,1,0:T(8,128)S(1)}, u32[]{:S(2)}, u32[]{:S(2)}) collective-permute-start(f32[6,5,384]{2,1,0:T(8,128)S(1)} %get-tuple-element.335), channel_id=1, source_target_pairs={{1,0},{2,1},{3,2},{4,3},{5,4},{6,5},{7,6},{8,7},{9,8},{10,9},{11,1... | collective-permute-start | bytes 138248 | tf_op jit(solution)/shard_map/ppermute | solution.py:15
  225.6 4.6 %collective-permute-start.2 = (f32[3,5,384]{2,1,0:T(8,128)S(1)}, f32[3,5,384]{2,1,0:T(8,128)S(1)}, u32[]{:S(2)}, u32[]{:S(2)}) collective-permute-start(f32[3,5,384]{2,1,0:T(8,128)S(1)} %get-tuple-element.332), channel_id=1, source_target_pairs={{0,1},{1,2},{2,3},{3,4},{4,5},{5,6},{6,7},{7,8},{8,9},{9,10},{10,1... | collective-permute-start | bytes 69128 | tf_op jit(solution)/shard_map/ppermute | solution.py:14
  228.6 4.2 collective-permute-start.3
where the time goes:
time: 460 us; the launch traced here: 458 us
  other arithmetic  171 us (37%)
  matrix products  167 us (36%)
  local copies, waits for them, and re-layouts  68.9 us (15%)
  blocking collectives  16.6 us (4%)
  starting transfers between devices  15.1 us (3%)
  between operations  7.98 us (2%)
  waiting for transfers between devices  7.22 us (2%)
    dot_general x72, matrix products, composite(): jnp.dot(lower, logs, precision=lax.Precision.HIGHEST, preferred_element_t...  123 us
    scatter-add x1, other arithmetic, shards(): jnp.zeros((nine, slot_count), jnp.float32).at[:, target_slot]  66.2 us
    gather x2, local copies, waits for them, and re-layouts, shards(): gathered = jnp.take(received, entry, axis=1).transpose(1, 0, 2)  45.5 us
    dot_general x72, matrix products, composite(): jnp.dot(params[6:9], weight, precision=lax.Precision.HIGHEST, preferred_e...  44.3 us
    add x5, other arithmetic, blur_strip(): rows_done = rows_done + taps[shift] * values[:, shift:shift + count]  34.8 us
    mul x5, other arithmetic, blur_strip(): result = result + taps[shift] * padded[:, :, shift:shift + width]  28.1 us
    mul x5, other arithmetic, blur_strip(): rows_done = rows_done + taps[shift] * values[:, shift:shift + count]  20.6 us
    all_to_all x1, blocking collectives, shards(): lax.all_to_all(slot_grads, 'dev', split_axis=1, concat_axis=1, tiled=True)  16.6 us
  transfers between devices with their start and end apart: 5, of which 2 were waited for; matrix products, arithmetic and copies ran while one was open for 1% of the time, Pallas kernels for 0%

commit v1 on v0

v1 whole, which is shorter than its diff:
```python
import functools

import jax
import jax.numpy as jnp
import numpy as np
from jax import lax
from jax.experimental import pallas as pl
from jax.experimental.pallas import tpu as pltpu
from jax.sharding import PartitionSpec as P

LANES = 128
SUB = 8
RIM = 5
HALO = 2 * RIM
LOG2E = 1.4426950408889634
F32 = jnp.float32
BF16 = jnp.bfloat16
NT = (((1,), (1,)), ((), ()))
TN = (((0,), (0,)), ((), ()))


def dot(a, b, dims):
    return lax.dot_general(a, b, dims, preferred_element_type=F32)


def pieces(x, count):
    out = []
    for _ in range(count - 1):
        top = x.astype(BF16)
        out.append(top)
        x = x - top.astype(F32)
    out.append(x.astype(BF16))
    return out


def lanes_of(shape):
    return lax.broadcasted_iota(jnp.int32, shape, len(shape) - 1)


def rows_of(shape):
    return lax.broadcasted_iota(jnp.int32, shape, len(shape) - 2)


def pick(table, last, where):
    chunks = table.shape[0]
    lane = jnp.bitwise_and(where, LANES - 1)
    chunk = jnp.right_shift(where, 7)
    lane8 = jnp.broadcast_to(lane, (SUB, LANES))
    chunk8 = jnp.broadcast_to(chunk, (SUB, LANES))
    value = jnp.zeros((SUB, LANES), F32)
    for c in range(chunks):
        got = jnp.take_along_axis(table[c], lane8, axis=1, mode="promise_in_bounds")
        value = jnp.where(chunk8 == c, got, value)
    total = jnp.zeros((SUB, LANES), F32)
    for c in range(0, chunks, SUB):
        got = jnp.take_along_axis(last[c : c + SUB], lane8, axis=1, mode="promise_in_bounds")
        total = total + jnp.where(chunk8 == rows_of((SUB, LANES)) + c, got, 0.0)
    return value, jnp.sum(total, axis=0, keepdims=True)


def pack_kernel(rows_ref, centres, conic, rho, opacity, colors, out_ref, table, last):
    chunks = table.shape[0]
    s = -0.5 * LOG2E
    for c in range(chunks):
        at = slice(c * LANES, (c + 1) * LANES)
        x, y = centres[0:1, at], centres[1:2, at]
        a, d = conic[0:1, at], conic[1:2, at]
        b = rho[0:1, at] * jnp.sqrt(a * d)
        rows = [
            jnp.log(opacity[0:1, at]) * LOG2E + s * (a * x * x + 2.0 * b * x * y + d * y * y),
            -2.0 * s * (a * x + b * y),
            -2.0 * s * (d * y + b * x),
            s * a,
            2.0 * s * b,
            s * d,
            colors[0:1, at],
            colors[1:2, at],
        ]
        table[c] = jnp.concatenate(rows, axis=0)
        last[c : c + 1] = colors[2:3, at]
    half = LANES // 2
    left = lanes_of((SUB, LANES)) < half
    for g in range(rows_ref.shape[1] // LANES):
        where = jnp.maximum(rows_ref[0:1, g * LANES : (g + 1) * LANES], 0)
        value, ninth = pick(table, last, where)
        ninth = jnp.broadcast_to(ninth, (SUB, LANES))
        out_ref[2 * g * SUB : (2 * g + 1) * SUB] = jnp.where(left, value, pltpu.roll(ninth, half, 1))
        out_ref[(2 * g + 1) * SUB : (2 * g + 2) * SUB] = jnp.where(left, pltpu.roll(value, half, 1), ninth)


def shifted(x, by):
    return pltpu.roll(x, by % SUB, 0)


def forward_kernel(recv, idx_ref, basis, img_ref, x_ref, seg_ref, table, last):
    chunks = table.shape[0]
    tiles, pixels = img_ref.shape[0], img_ref.shape[2]
    groups = x_ref.shape[2] // LANES
    half = LANES // 2
    left = lanes_of((SUB, LANES)) < half
    for c in range(chunks):
        a = recv[2 * c * SUB : (2 * c + 1) * SUB]
        b = recv[(2 * c + 1) * SUB : (2 * c + 2) * SUB]
        table[c] = jnp.where(left, a, pltpu.roll(b, half, 1))
        last[c : c + 1] = jnp.where(left, pltpu.roll(a, half, 1), b)[0:1]
    first = rows_of((SUB, LANES)) == 0

    def fetch(t, carry):
        for q in range(groups):
            idx = idx_ref[pl.ds(t * groups + q, 1), :]
            live = idx >= 0
            value, ninth = pick(table, last, jnp.maximum(idx, 0))
            live8 = jnp.broadcast_to(live, (SUB, LANES))
            value = jnp.where(live8, value, jnp.where(first, -1000.0, 0.0))
            ninth = jnp.where(live8, jnp.broadcast_to(ninth, (SUB, LANES)), 0.0)
            p0, p1, p2 = [p.astype(F32) for p in pieces(value, 3)]
            n0, n1, n2 = [p.astype(F32) for p in pieces(ninth, 3)]
            r = rows_of((SUB, LANES))
            n = jnp.where(r == 0, n0, jnp.where(r == 1, n1, jnp.where(r == 2, n2, 0.0)))
            x_ref[t, :, q * LANES : (q + 1) * LANES] = jnp.concatenate([p0, p1, p2, n], axis=0).astype(BF16)
        return carry

    lax.fori_loop(0, tiles, fetch, 0)
    row = rows_of((SUB, pixels))

    def composite(t, carry):
        trans = jnp.ones((SUB, pixels), F32)
        acc = [jnp.zeros((SUB, pixels), F32) for _ in range(3)]
        for q in range(groups):
            out = dot(x_ref[t, :, q * LANES : (q + 1) * LANES], basis[...], TN)
            for i in range(LANES // SUB):
                at = slice(i * SUB, (i + 1) * SUB)
                alpha = jnp.exp2(out[at, :pixels])
                w = alpha * trans
                trans = trans * (1.0 - alpha)
                for ch in range(3):
                    tint = out[at, pixels + ch * LANES : pixels + (ch + 1) * LANES]
                    acc[ch] = acc[ch] + jnp.concatenate([tint] * (pixels // LANES), axis=1) * w
        before = jnp.where(row >= 1, shifted(trans, 1), 1.0)
        for by in (1, 2, 4):
            before = before * jnp.where(row >= by, shifted(before, by), 1.0)
        seg_ref[t, 0:SUB] = before
        seg_ref[t, SUB : 2 * SUB] = trans
        image = []
        for ch in range(3):
            seg_ref[t, (2 + ch) * SUB : (3 + ch) * SUB] = acc[ch]
            image.append(jnp.sum(acc[ch] * before, axis=0, keepdims=True))
        img_ref[t] = jnp.concatenate(image, axis=0)
        return carry

    lax.fori_loop(0, tiles, composite, 0)


def taps_of():
    m = np.arange(-RIM, RIM + 1)
    w = np.exp(-m * m / 4.5)
    return [float(v) for v in w / w.sum()]


def blur_rows(x, count):
    taps = taps_of()
    width = x.shape[1]
    out = taps[RIM] * x[RIM : RIM + count]
    for m in range(1, RIM + 1):
        out = out + taps[RIM + m] * (x[RIM - m : RIM - m + count] + x[RIM + m : RIM + m + count])
    lane = lanes_of(out.shape)
    res = taps[RIM] * out
    for m in range(1, RIM + 1):
        up = jnp.where(lane >= m, pltpu.roll(out, m, 1), 0.0)
        down = jnp.where(lane < width - m, pltpu.roll(out, width - m, 1), 0.0)
        res = res + taps[RIM + m] * (up + down)
    return res


def ssim_kernel(edge, ren, tar, ren_b, tar_b, ren_a, tar_a, cot_ref):
    rows = ren.shape[1]
    width = ren.shape[2]
    mid = rows + HALO
    r_at = rows_of((mid, width))
    inside = jnp.logical_and(r_at >= edge[0], r_at < edge[1])
    for ch in range(ren.shape[0]):
        r = jnp.concatenate([ren_b[ch], ren[ch], ren_a[ch]], axis=0)
        t = jnp.concatenate([tar_b[ch], tar[ch], tar_a[ch]], axis=0)
        mr, mt = blur_rows(r, mid), blur_rows(t, mid)
        er, et, ert = blur_rows(r * r, mid), blur_rows(t * t, mid), blur_rows(r * t, mid)
        a1 = 2.0 * mr * mt + 0.0001
        a2 = 2.0 * (ert - mr * mt) + 0.0009
        b1 = mr * mr + mt * mt + 0.0001
        b2 = (er - mr * mr) + (et - mt * mt) + 0.0009
        i1, i2 = 1.0 / b1, 1.0 / b2
        s = a1 * a2 * i1 * i2
        d_mr = 2.0 * mt * (a2 - a1) * i1 * i2 - 2.0 * mr * s * (i1 - i2)
        d_er = -s * i2
        d_ert = 2.0 * a1 * i1 * i2
        g0, g1, g2 = [blur_rows(jnp.where(inside, d, 0.0), rows) for d in (d_mr, d_er, d_ert)]
        rc, tc = ren[ch], tar[ch]
        cot_ref[ch] = 1.6 * (rc - tc) - 0.2 * (g0 + 2.0 * rc * g1 + tc * g2)


def spread(values, where, total):
    count = where.shape[1]
    wide = total.shape[1]
    p0, p1, p2 = [p.astype(F32) for p in pieces(values, 3)]
    rows = rows_of((SUB, count))
    tail = jnp.where(rows == 0, p0[SUB:], jnp.where(rows == 1, p1[SUB:], jnp.where(rows == 2, p2[SUB:], 0.0)))
    stacked = jnp.concatenate([p0[:SUB], p1[:SUB], p2[:SUB], tail], axis=0)
    low = jnp.bitwise_and(where, wide - 1)
    high = jnp.where(where < 0, -1, jnp.right_shift(where, wide.bit_length() - 1))
    hot = (jnp.broadcast_to(low, (wide, count)) == rows_of((wide, count))).astype(F32).astype(BF16)
    parts = []
    for c in range(total.shape[0] // 32):
        parts.append(jnp.where(jnp.broadcast_to(high == c, stacked.shape), stacked, 0.0).astype(BF16))
    total[...] += dot(jnp.concatenate(parts, axis=0), hot, NT)


def nine(total, c):
    got = total[c * 32 : (c + 1) * 32]
    return (
        got[0:SUB] + got[SUB : 2 * SUB] + got[2 * SUB : 3 * SUB],
        got[24:25] + got[25:26] + got[26:27],
    )


def backward_kernel(x_ref, idx_ref, seg_ref, cot_ref, basis, phi, out_ref, alphas, weights, grads, total):
    tiles, pixels = cot_ref.shape[0], cot_ref.shape[2]
    count = x_ref.shape[2]
    groups = count // LANES
    steps = LANES // SUB
    total[...] = jnp.zeros_like(total)
    row = rows_of((SUB, pixels))
    row32 = rows_of((32, pixels))

    def tile(t, carry):
        cot = [jnp.broadcast_to(cot_ref[t, ch : ch + 1], (SUB, pixels)) for ch in range(3)]
        hi = [c.astype(BF16).astype(F32) for c in cot]
        lo = [c - h for c, h in zip(cot, hi)]

        def place(v):
            body = jnp.where(row == 6, v[0], jnp.where(row == 7, v[1], 0.0))
            return [body, body, body, jnp.where(row < 3, v[2], 0.0)]

        rhs_g = jnp.concatenate(place(hi) + place(lo), axis=0).astype(BF16)
        lhs = jnp.where(row == 6, hi[0], jnp.where(row == 7, hi[1], 0.0)) + phi[0:SUB]
        lhs2 = jnp.where(row == 0, hi[2], jnp.where(row == 1, lo[0], jnp.where(row == 2, lo[1], jnp.where(row == 3, lo[2], 0.0))))
        lhs = jnp.concatenate([lhs, lhs2], axis=0).astype(BF16)

        seg = [seg_ref[t, s * SUB : (s + 1) * SUB] for s in range(5)]
        add = cot[0] * seg[2] + cot[1] * seg[3] + cot[2] * seg[4]
        mul = seg[1]
        for by in (1, 2, 4):
            more = row < SUB - by
            add_n = jnp.where(more, shifted(add, -by), 0.0)
            mul_n = jnp.where(more, shifted(mul, -by), 1.0)
            add, mul = add + mul * add_n, mul * mul_n
        behind = jnp.where(row < SUB - 1, shifted(add, -1), 0.0)

        trans = seg[0]
        for q in range(groups):
            out = dot(x_ref[t, :, q * LANES : (q + 1) * LANES], basis[:, :pixels], TN)
            for i in range(steps):
                at = slice(q * LANES + i * SUB, q * LANES + (i + 1) * SUB)
                alpha = jnp.exp2(out[i * SUB : (i + 1) * SUB])
                alphas[at] = alpha
                weights[at] = alpha * trans
                trans = trans * (1.0 - alpha)
        for q in reversed(range(groups)):
            x = x_ref[t, :, q * LANES : (q + 1) * LANES]
            g = dot(jnp.concatenate([x, x], axis=0), rhs_g, TN)
            hs = [None] * steps
            for i in reversed(range(steps)):
                at = slice(q * LANES + i * SUB, q * LANES + (i + 1) * SUB)
                d = g[i * SUB : (i + 1) * SUB] - behind
                hs[i] = weights[at] * d
                behind = behind + alphas[at] * d
            h = jnp.concatenate(hs, axis=0)
            h0, h1 = pieces(h, 2)
            w0, w1 = pieces(weights[q * LANES : (q + 1) * LANES], 2)
            gh = dot(lhs, h0, NT) + dot(lhs, h1, NT)
            gw = dot(lhs, w0, NT) + dot(lhs, w1, NT)
            r8 = rows_of((SUB, LANES))
            low = gw[SUB:]
            top = jnp.where(r8 < 6, gh[:SUB], gw[:SUB] + pltpu.roll(low, 5, 0))
            ninth = jnp.broadcast_to((low + pltpu.roll(low, 5, 0))[0:1], (SUB, LANES))
            grads[:, q * LANES : (q + 1) * LANES] = jnp.concatenate([top, ninth], axis=0)
        where = jnp.concatenate([idx_ref[pl.ds(t * groups + q, 1), :] for q in range(groups)], axis=1)
        spread(grads[...], where, total)
        return carry

    lax.fori_loop(0, tiles, tile, 0)
    half = LANES // 2
    left = lanes_of((SUB, LANES)) < half
    per = total.shape[1] // LANES
    for c in range(total.shape[0] // 32):
        eight, ninth = nine(total, c)
        for j in range(per):
            e = eight[:, j * LANES : (j + 1) * LANES]
            n = jnp.broadcast_to(ninth[:, j * LANES : (j + 1) * LANES], (SUB, LANES))
            at = (c * per + j) * 2 * SUB
            out_ref[at : at + SUB] = jnp.where(left, e, pltpu.roll(n, half, 1))
            out_ref[at + SUB : at + 2 * SUB] = jnp.where(left, pltpu.roll(e, half, 1), n)


def home_kernel(recv, rows_ref, centres, conic, rho, opacity, out_ref, total):
    half = LANES // 2
    left = lanes_of((SUB, LANES)) < half
    total[...] = jnp.zeros_like(total)
    step = 4
    for g in range(0, rows_ref.shape[1] // LANES, step):
        eights, ninths = [], []
        for k in range(g, g + step):
            a = recv[2 * k * SUB : (2 * k + 1) * SUB]
            b = recv[(2 * k + 1) * SUB : (2 * k + 2) * SUB]
            eights.append(jnp.where(left, a, pltpu.roll(b, half, 1)))
            n = jnp.where(left, pltpu.roll(a, half, 1), b)
            ninths.append(jnp.broadcast_to(n[0:1], (SUB, LANES)))
        values = jnp.concatenate([jnp.concatenate(eights, axis=1), jnp.concatenate(ninths, axis=1)], axis=0)
        spread(values, rows_ref[0:1, g * LANES : (g + step) * LANES], total)
    wide = total.shape[1]
    for c in range(total.shape[0] // 32):
        m, col2 = nine(total, c)
        at = slice(c * wide, (c + 1) * wide)
        x, y = centres[0:1, at], centres[1:2, at]
        a, d = conic[0:1, at], conic[1:2, at]
        root = jnp.sqrt(a * d)
        b = rho[0:1, at] * root
        m1, mu, mv, muu, muv, mvv = [m[i : i + 1] for i in range(6)]
        dx, dy = mu - x * m1, mv - y * m1
        dxx = muu - 2.0 * x * mu + x * x * m1
        dxy = muv - x * mv - y * mu + x * y * m1
        dyy = mvv - 2.0 * y * mv + y * y * m1
        rows = [
            a * dx + b * dy,
            b * dx + d * dy,
            -0.5 * (dxx + b / a * dxy),
            -0.5 * (dyy + b / d * dxy),
            -root * dxy,
            m1 / opacity[0:1, at],
            m[6:7],
            m[7:8],
            col2,
        ]
        for i, v in enumerate(rows):
            out_ref[i : i + 1, at] = v


def tables(tile):
    pixels = tile * tile
    p = np.arange(pixels)
    v = (p // tile) - (tile - 1) / 2.0
    u = (p % tile) - (tile - 1) / 2.0
    six = np.stack([np.ones(pixels), u, v, u * u, u * v, v * v])
    basis = np.zeros((32, pixels + 3 * LANES), np.float32)
    for k in range(3):
        basis[8 * k : 8 * k + 6, :pixels] = six
        basis[8 * k + 6, pixels : pixels + LANES] = 1.0
        basis[8 * k + 7, pixels + LANES : pixels + 2 * LANES] = 1.0
        basis[24 + k, pixels + 2 * LANES :] = 1.0
    phi = np.zeros((8, pixels), np.float32)
    phi[:6] = six
    return jnp.asarray(basis, BF16), jnp.asarray(phi)


def call(kernel, out_shape, scratch=(), smem=0):
    n_vmem = pl.BlockSpec()

    def run(*args):
        specs = [pl.BlockSpec(memory_space=pltpu.SMEM) if i < smem else n_vmem for i in range(len(args))]
        return pl.pallas_call(
            kernel,
            out_shape=out_shape,
            in_specs=specs,
            out_specs=jax.tree.map(lambda _: n_vmem, out_shape),
            scratch_shapes=list(scratch),
            compiler_params=pltpu.CompilerParams(vmem_limit_bytes=48 * 1024 * 1024),
        )(*args)

    return run


def swap_edges(value):
    size = lax.axis_size("dev")
    me = lax.axis_index("dev")
    first, last = value[:, :HALO], value[:, -HALO:]
    odd = (me % 2) == 1
    inner = [(i, i ^ 1) for i in range(size)]
    outer = [(i, i + 1) for i in range(1, size - 1, 2)]
    outer = outer + [(j, i) for i, j in outer]
    got_in = lax.ppermute(jnp.where(odd, first, last), "dev", inner)
    got_out = lax.ppermute(jnp.where(odd, last, first), "dev", outer)
    return jnp.where(odd, got_in, got_out), jnp.where(odd, got_out, got_in)


def shards(tile_lists, send_rows, centres, conic, rho, opacity, colors, target):
    slot_count = send_rows.shape[1]
    owned_count = centres.shape[1]
    channels, tile, width = target.shape
    strip_tiles, list_len = tile_lists.shape
    size = lax.axis_size("dev")
    me = lax.axis_index("dev")
    pixels = tile * tile
    chunks = slot_count // LANES
    wide = 2 * LANES
    basis, phi = tables(tile)
    sds = jax.ShapeDtypeStruct

    packed = call(
        pack_kernel,
        sds((size * SUB, LANES), F32),
        [pltpu.VMEM((owned_count // LANES, SUB, LANES), F32), pltpu.VMEM((owned_count // LANES, LANES), F32)],
    )(send_rows, centres, conic, rho, opacity, colors)
    received = lax.all_to_all(packed, "dev", split_axis=0, concat_axis=0, tiled=True)

    order = tile_lists.reshape(strip_tiles, SUB, list_len // SUB).transpose(0, 2, 1)
    order = order.reshape(strip_tiles * list_len // LANES, LANES)
    tar_b, tar_a = swap_edges(target)

    colour_tiles, coefs, segments = call(
        forward_kernel,
        (
            sds((strip_tiles, channels, pixels), F32),
            sds((strip_tiles, 32, list_len), BF16),
            sds((strip_tiles, 5 * SUB, pixels), F32),
        ),
        [pltpu.VMEM((chunks, SUB, LANES), F32), pltpu.VMEM((chunks, LANES), F32)],
    )(received, order, basis)
    image = (
        colour_tiles.reshape(strip_tiles, channels, tile, tile).transpose(1, 2, 0, 3).reshape(channels, tile, width)
    )
    ren_b, ren_a = swap_edges(image)
    edge = jnp.stack([jnp.where(me == 0, RIM, 0), jnp.where(me == size - 1, tile + RIM, tile + HALO)]).astype(jnp.int32)
    cot = call(ssim_kernel, sds((channels, tile, width), F32), smem=1)(
        edge, image, target, ren_b, tar_b, ren_a, tar_a
    )
    cot_tiles = (
        cot.reshape(channels, tile, strip_tiles, tile).transpose(2, 0, 1, 3).reshape(strip_tiles, channels, pixels)
    )
    slot_sums = call(
        backward_kernel,
        sds((size * SUB, LANES), F32),
        [
            pltpu.VMEM((list_len, pixels), F32),
            pltpu.VMEM((list_len, pixels), F32),
            pltpu.VMEM((2 * SUB, list_len), F32),
            pltpu.VMEM((slot_count // wide * 32, wide), F32),
        ],
    )(coefs, order, segments, cot_tiles, basis, phi)
    returned = lax.all_to_all(slot_sums, "dev", split_axis=0, concat_axis=0, tiled=True)
    grads = call(
        home_kernel,
        sds((9, owned_count), F32),
        [pltpu.VMEM((owned_count // wide * 32, wide), F32)],
    )(returned, send_rows, centres, conic, rho, opacity)
    return (image, grads)


def solution(mesh):
    return jax.shard_map(
        shards,
        mesh=mesh,
        in_specs=(
            P("dev", None),
            P("dev", None),
            P(None, "dev"),
            P(None, "dev"),
            P(None, "dev"),
            P(None, "dev"),
            P(None, "dev"),
            P(None, "dev", None),
        ),
        out_specs=(P(None, "dev", None), P(None, "dev")),
        check_vma=False,
    )
```

time: 460 us -> 98.3 us (0.21)
  other arithmetic: 171 us -> 0.76 us
  matrix products: 167 us -> 0 us
  local copies, waits for them, and re-layouts: 68.9 us -> 6.69 us
  Pallas kernels: 0 us -> 58.1 us
  between operations: 7.98 us -> 0.9 us
    dot_general x144 -> x0, matrix products: 167 us -> none  [the longest x72 123 us: composite(): jnp.dot(lower, logs, precision=lax.Precision.HIGHEST, preferred_element_t...]
    scatter-add x2 -> x0, other arithmetic: 77.9 us -> none  [the longest x1 66.2 us: shards(): jnp.zeros((nine, slot_count), jnp.float32).at[:, target_slot]]
    pallas_call x0 -> x5, Pallas kernels: none -> 58.1 us  [run(): pl.pallas_call(kernel, out_shape=out_shape, in_specs=specs, out_specs=jax...]
    gather x4 -> x0, local copies, waits for them, and re-layouts: 51.3 us -> none  [the longest x2 45.5 us: shards(): gathered = jnp.take(received, entry, axis=1).transpose(1, 0, 2)]
    mul x131 -> x0, other arithmetic: 49.7 us -> none  [the longest x5 28.1 us: blur_strip(): result = result + taps[shift] * padded[:, :, shift:shift + width]]
    add x6 -> x0, other arithmetic: 34.8 us -> none  [the longest x5 34.8 us: blur_strip(): rows_done = rows_done + taps[shift] * values[:, shift:shift + count]]
  transfers between devices with their start and end apart: 5 -> 5, of which waited for: 2 -> 2; matrix products, arithmetic and copies ran while one was open for 1% -> 2% of each run, Pallas kernels for 0% -> 14%
where the time goes in v1:
time: 98.3 us; the launch traced here: 97.7 us
  Pallas kernels  58.1 us (59%)
  blocking collectives  13.8 us (14%)
  starting transfers between devices  13.7 us (14%)
  local copies, waits for them, and re-layouts  6.69 us (7%)
  waiting for transfers between devices  3.76 us (4%)
    pallas_call x5, Pallas kernels, run(): pl.pallas_call(kernel, out_shape=out_shape, in_specs=specs, out_specs=jax...  58.1 us
    all_to_all x1, blocking collectives, shards(): lax.all_to_all(slot_sums, 'dev', split_axis=0, concat_axis=0, tiled=True)  13.8 us
    all_to_all x1, starting transfers between devices, shards(): lax.all_to_all(packed, 'dev', split_axis=0, concat_axis=0, tiled=True)  7.3 us
    ppermute x2, starting transfers between devices, swap_edges(): got_in = lax.ppermute(jnp.where(odd, first, last), 'dev', inner)  5.05 us
    unnamed x32, local copies, waits for them, and re-layouts  4.71 us
    all_to_all x1, waiting for transfers between devices, shards(): lax.all_to_all(packed, 'dev', split_axis=0, concat_axis=0, tiled=True)  2.88 us
  transfers between devices with their start and end apart: 5, of which 2 were waited for; matrix products, arithmetic and copies ran while one was open for 2% of the time, Pallas kernels for 14%

profile of v1, /device:TPU:0, one launch (start us, length us, event | category | flops | bytes accessed | tf_op | source)
XLA Modules:
  0.0 97.7 jit_solution(4228668354616195104)
XLA Ops:
  0.6 0.0 copy-start.3
  0.6 0.7 copy-done.3
  1.4 0.0 copy-start.5
  1.4 0.7 copy-done.5
  2.1 0.0 copy-start.7
  2.1 0.7 copy-done.7
  2.8 0.0 copy-start.9
  2.8 0.7 copy-done.9
  3.5 0.0 copy-start.11
  3.5 0.7 copy-done.11
  4.2 0.0 copy-start.13
  4.2 0.8 copy-done.13
  4.9 2.1 %shard_map.113 = f32[256,128]{1,0:T(8,128)} custom-call(s32[1,2048]{1,0:T(1,128)S(1)} %copy-done.7, f32[2,2048]{1,0:T(2,128)S(1)} %copy-done.3, f32[2,2048]{1,0:T(2,128)S(1)} %copy-done.5, f32[1,2048]{1,0:T(1,128)S(1)} %copy-done.9, f32[1,2048]{1,0:T(1,128)S(1)} %copy-done.11, f32[3,2048]{1,0:T(4,128)S(1)} %copy-done.13), custom_call_target="tpu_custom_call" | custom-call | tf_op jit(solution)/shard_map/pallas_call | solution.py:368
  7.0 0.0 copy-start.1
  7.0 7.3 %all-to-all-start = ((f32[32,8,128]{2,1,0:T(8,128)}), f32[32,8,128]{2,1,0:T(8,128)S(1)}, u32[]{:S(2)}, u32[]{:S(2)}) async-start(f32[32,8,128]{2,1,0:T(8,128)} %bitcast), calls=%async_computation | async-start | bytes 262144 | tf_op jit(solution)/shard_map/all_to_all | solution.py:411
  14.3 0.0 copy-done.1
  14.3 0.0 copy-start.15
  14.3 0.6 slice_select_fusion.2
  15.0 0.7 collective-permute-start.3
  15.6 3.2 %collective-permute-start.2 = (f32[3,10,384]{2,1,0:T(8,128)S(1)}, f32[3,10,384]{2,1,0:T(8,128)S(1)}, u32[]{:S(2)}, u32[]{:S(2)}) collective-permute-start(f32[3,10,384]{2,1,0:T(8,128)S(1)} %get-tuple-element.13), channel_id=1, source_target_pairs={{0,1},{1,0},{2,3},{3,2},{4,5},{5,4},{6,7},{7,6},{8,9},{9,8},{10,11... | collective-permute-start | bytes 138248 | tf_op jit(solution)/shard_map/ppermute | solution.py:388
  18.8 0.0 copy-done.15
  18.8 0.1 reshape.26
  18.9 0.3 copy.15
  19.2 0.0 copy-start.2
  19.2 0.4 reshape.27.idx_ref
  19.6 0.1 pad_add_fusion.edge
  19.6 2.9 %all-to-all-done = f32[32,8,128]{2,1,0:T(8,128)S(1)} async-done(((f32[32,8,128]{2,1,0:T(8,128)}), f32[32,8,128]{2,1,0:T(8,128)S(1)}, u32[]{:S(2)}, u32[]{:S(2)}) %all-to-all-start) | async-done | bytes 131104 | tf_op jit(solution)/shard_map/all_to_all | solution.py:411
  22.5 0.0 copy-done.2
  22.5 13.7 %shard_map.114 = (f32[24,3,256]{2,1,0:T(4,128)S(1)}, bf16[24,32,512]{2,1,0:T(8,128)(2,1)S(1)}, f32[24,40,256]{2,1,0:T(8,128)S(1)}) custom-call(f32[256,128]{1,0:T(8,128)S(1)} %bitcast.16, s32[96,128]{1,0:T(8,128)S(1)} %reshape.27.idx_ref, bf16[32,640]{1,0:T(8,128)(2,1)S(1)} %copy-done.2), custom_call_target="tpu_custom_call" | custom-call | tf_op jit(solution)/shard_map/pallas_call | solution.py:368
  36.2 0.2 reshape.28
  36.4 0.2 copy.17
  36.6 0.2 reshape.29.ren
  36.8 0.0 copy-start
  36.9 0.7 collective-permute-start.1
  37.6 1.9 %collective-permute-start = (f32[3,10,384]{2,1,0:T(8,128)S(1)}, f32[3,10,384]{2,1,0:T(8,128)S(1)}, u32[]{:S(2)}, u32[]{:S(2)}) collective-permute-start(f32[3,10,384]{2,1,0:T(8,128)S(1)} %get-tuple-element.15), channel_id=1, source_target_pairs={{0,1},{1,0},{2,3},{3,2},{4,5},{5,4},{6,7},{7,6},{8,9},{9,8},{10,11... | collective-permute-start | bytes 138248 | tf_op jit(solution)/shard_map/ppermute | solution.py:388
  39.4 0.0 collective-permute-done.3
  39.4 0.0 collective-permute-done.2
  39.4 0.0 collective-permute-done.1
  39.4 0.9 collective-permute-done
  40.3 0.0 copy-done
  40.4 4.0 %shard_map.115 = f32[3,16,384]{2,1,0:T(8,128)S(1)} custom-call(s32[2]{0:T(128)S(1)} %pad_add_fusion.edge, f32[3,16,384]{2,1,0:T(8,128)S(1)} %reshape.29.ren, f32[3,16,384]{2,1,0:T(8,128)S(1)} %copy-done.1, f32[3,10,384]{2,1,0:T(8,128)S(1)} %get-tuple-element.11.ren_b, f32[3,10,384]{2,1,0:T(8,128)S(1)} %get-tuple-element.9.tar_b, ...), custom_call_target="tpu_custom_call" | custom-call | tf_op jit(solution)/shard_map/pallas_call | solution.py:368
  44.3 0.2 reshape.30
  44.5 0.1 copy.20
  44.7 0.0 copy-start.14
  44.7 0.3 reshape.32.cot_ref
  45.0 0.4 copy-done.14
  45.4 37.2 %shard_map.116 = f32[256,128]{1,0:T(8,128)S(1)} custom-call(bf16[24,32,512]{2,1,0:T(8,128)(2,1)S(1)} %get-tuple-element.6.x_ref, s32[96,128]{1,0:T(8,128)S(1)} %reshape.27.idx_ref, f32[24,40,256]{2,1,0:T(8,128)S(1)} %get-tuple-element.7.seg_ref, f32[24,3,256]{2,1,0:T(4,128)S(1)} %reshape.32.cot_ref, bf16[32,640]{1,0:T(8,128)(2,1)S(1)} %copy-done.2, ...), custom_call_target="tpu_custom_call" | custom-call | tf_op jit(solution)/shard_map/pallas_call | solution.py:368
  82.5 0.0 copy-start.4
  82.6 0.0 copy-start.6
  82.6 0.0 copy-start.8
  82.6 0.0 copy-start.10
  82.6 0.0 copy-start.12
  82.6 13.8 %all_to_all.22 = f32[32,8,128]{2,1,0:T(8,128)S(1)} all-to-all(f32[32,8,128]{2,1,0:T(8,128)S(1)} %bitcast.15), channel_id=1, replica_groups=mesh['dev'=32] {'dev'}, dimensions={0} | all-to-all | bytes 262144 | tf_op jit(solution)/shard_map/all_to_all | solution.py:447
  96.4 0.0 copy-done.4
  96.4 0.0 copy-done.6
  96.4 0.0 copy-done.8
  96.4 0.0 copy-done.10
  96.4 0.0 copy-done.12
  96.4 1.3 %shard_map.117 = f32[9,2048]{1,0:T(8,128)} custom-call(f32[256,128]{1,0:T(8,128)S(1)} %bitcast.17, s32[1,2048]{1,0:T(1,128)S(1)} %copy-done.8, f32[2,2048]{1,0:T(2,128)S(1)} %copy-done.4, f32[2,2048]{1,0:T(2,128)S(1)} %copy-done.6, f32[1,2048]{1,0:T(1,128)S(1)} %copy-done.10, f32[1,2048]{1,0:T(1,128)S(1)} %copy-done.12), custom_call_target="tpu_custom_call" | custom-call | tf_op jit(solution)/shard_map/pallas_call | solution.py:368
  (4 shorter events, 0.1 us)
Async XLA Ops:
  0.6 0.7 copy-start.3
  1.4 0.7 copy-start.5
  2.1 0.7 copy-start.7
  2.8 0.7 copy-start.9
  3.5 0.7 copy-start.11
  4.2 0.8 copy-start.13
  7.0 7.3 %copy-start.1 = (f32[3,16,384]{2,1,0:T(8,128)S(1)}, f32[3,16,384]{2,1,0:T(8,128)}, u32[]{:S(2)}) copy-start(f32[3,16,384]{2,1,0:T(8,128)} %tar.1) | copy-start | bytes 221188
  7.0 15.5 %all-to-all-start = ((f32[32,8,128]{2,1,0:T(8,128)}), f32[32,8,128]{2,1,0:T(8,128)S(1)}, u32[]{:S(2)}, u32[]{:S(2)}) async-start(f32[32,8,128]{2,1,0:T(8,128)} %bitcast), calls=%async_computation | async-start | bytes 262144 | tf_op jit(solution)/shard_map/all_to_all | solution.py:411
  14.3 4.5 %copy-start.15 = (s32[24,512]{1,0:T(8,128)S(1)}, s32[24,512]{1,0:T(8,128)}, u32[]{:S(2)}) copy-start(s32[24,512]{1,0:T(8,128)} %param.10) | copy-start | bytes 147460
  15.0 24.4 %collective-permute-start.3 = (f32[3,10,384]{2,1,0:T(8,128)}, f32[3,10,384]{2,1,0:T(8,128)S(1)}, u32[]{:S(2)}, u32[]{:S(2)}) collective-permute-start(f32[3,10,384]{2,1,0:T(8,128)} %get-tuple-element.12), channel_id=1, source_target_pairs={{1,2},{3,4},{5,6},{7,8},{9,10},{11,12},{13,14},{15,16},{17,18},{19... | collective-permute-start | bytes 138248 | tf_op jit(solution)/shard_map/ppermute | solution.py:389
  15.6 23.8 %collective-permute-start.2 = (f32[3,10,384]{2,1,0:T(8,128)S(1)}, f32[3,10,384]{2,1,0:T(8,128)S(1)}, u32[]{:S(2)}, u32[]{:S(2)}) collective-permute-start(f32[3,10,384]{2,1,0:T(8,128)S(1)} %get-tuple-element.13), channel_id=1, source_target_pairs={{0,1},{1,0},{2,3},{3,2},{4,5},{5,4},{6,7},{7,6},{8,9},{9,8},{10,11... | collective-permute-start | bytes 138248 | tf_op jit(solution)/shard_map/ppermute | solution.py:388
  19.2 3.3 %copy-start.2 = (bf16[32,640]{1,0:T(8,128)(2,1)S(1)}, bf16[32,640]{1,0:T(8,128)(2,1)}, u32[]{:S(2)}) copy-start(bf16[32,640]{1,0:T(8,128)(2,1)} %constant.33.clone.basis) | copy-start | bytes 122884
  36.8 3.5 %copy-start = (f32[3,16,384]{2,1,0:T(8,128)}, f32[3,16,384]{2,1,0:T(8,128)S(1)}, u32[]{:S(2)}) copy-start(f32[3,16,384]{2,1,0:T(8,128)S(1)} %reshape.29.ren) | copy-start | bytes 221188
  36.9 2.6 %collective-permute-start.1 = (f32[3,10,384]{2,1,0:T(8,128)S(1)}, f32[3,10,384]{2,1,0:T(8,128)S(1)}, u32[]{:S(2)}, u32[]{:S(2)}) collective-permute-start(f32[3,10,384]{2,1,0:T(8,128)S(1)} %get-tuple-element.14), channel_id=1, source_target_pairs={{1,2},{3,4},{5,6},{7,8},{9,10},{11,12},{13,14},{15,16},{17,18},{19... | collective-permute-start | bytes 138248 | tf_op jit(solution)/shard_map/ppermute | solution.py:389
  37.6 2.8 %collective-permute-start = (f32[3,10,384]{2,1,0:T(8,128)S(1)}, f32[3,10,384]{2,1,0:T(8,128)S(1)}, u32[]{:S(2)}, u32[]{:S(2)}) collective-permute-start(f32[3,10,384]{2,1,0:T(8,128)S(1)} %get-tuple-element.15), channel_id=1, source_target_pairs={{0,1},{1,0},{2,3},{3,2},{4,5},{5,4},{6,7},{7,6},{8,9},{9,8},{10,11... | collective-permute-start | bytes 138248 | tf_op jit(solution)/shard_map/ppermute | solution.py:388
  44.7 0.7 copy-start.14
  82.5 13.8 %copy-start.4 = (f32[2,2048]{1,0:T(2,128)S(1)}, f32[2,2048]{1,0:T(2,128)}, u32[]{:S(2)}) copy-start(f32[2,2048]{1,0:T(2,128)} %centres.3) | copy-start | bytes 49156
  82.6 13.8 %copy-start.6 = (f32[2,2048]{1,0:T(2,128)S(1)}, f32[2,2048]{1,0:T(2,128)}, u32[]{:S(2)}) copy-start(f32[2,2048]{1,0:T(2,128)} %conic.3) | copy-start | bytes 49156
  82.6 13.8 %copy-start.8 = (s32[1,2048]{1,0:T(1,128)S(1)}, s32[1,2048]{1,0:T(1,128)}, u32[]{:S(2)}) copy-start(s32[1,2048]{1,0:T(1,128)} %rows_ref.3) | copy-start | bytes 24580
  82.6 13.8 %copy-start.10 = (f32[1,2048]{1,0:T(1,128)S(1)}, f32[1,2048]{1,0:T(1,128)}, u32[]{:S(2)}) copy-start(f32[1,2048]{1,0:T(1,128)} %rho.3) | copy-start | bytes 24580
  82.6 13.8 %copy-start.12 = (f32[1,2048]{1,0:T(1,128)S(1)}, f32[1,2048]{1,0:T(1,128)}, u32[]{:S(2)}) copy-start(f32[1,2048]{1,0:T(1,128)} %opacity.3) | copy-start | bytes 24580

commit v2 on v1

--- a/solution.py
+++ b/solution.py
@@ -15,6 +15,7 @@
 LOG2E = 1.4426950408889634
 F32 = jnp.float32
 BF16 = jnp.bfloat16
+NN = (((1,), (0,)), ((), ()))
 NT = (((1,), (1,)), ((), ()))
 TN = (((0,), (0,)), ((), ()))
 
@@ -105,29 +106,30 @@
         last[c : c + 1] = jnp.where(left, pltpu.roll(a, half, 1), b)[0:1]
     first = rows_of((SUB, LANES)) == 0
 
-    def fetch(t, carry):
-        for q in range(groups):
-            idx = idx_ref[pl.ds(t * groups + q, 1), :]
-            live = idx >= 0
-            value, ninth = pick(table, last, jnp.maximum(idx, 0))
-            live8 = jnp.broadcast_to(live, (SUB, LANES))
-            value = jnp.where(live8, value, jnp.where(first, -1000.0, 0.0))
-            ninth = jnp.where(live8, jnp.broadcast_to(ninth, (SUB, LANES)), 0.0)
-            p0, p1, p2 = [p.astype(F32) for p in pieces(value, 3)]
-            n0, n1, n2 = [p.astype(F32) for p in pieces(ninth, 3)]
-            r = rows_of((SUB, LANES))
-            n = jnp.where(r == 0, n0, jnp.where(r == 1, n1, jnp.where(r == 2, n2, 0.0)))
-            x_ref[t, :, q * LANES : (q + 1) * LANES] = jnp.concatenate([p0, p1, p2, n], axis=0).astype(BF16)
-        return carry
-
-    lax.fori_loop(0, tiles, fetch, 0)
     row = rows_of((SUB, pixels))
 
-    def composite(t, carry):
+    def fetch(t, q):
+        idx = idx_ref[pl.ds(t * groups + q, 1), :]
+        live = idx >= 0
+        value, ninth = pick(table, last, jnp.maximum(idx, 0))
+        live8 = jnp.broadcast_to(live, (SUB, LANES))
+        value = jnp.where(live8, value, jnp.where(first, -1000.0, 0.0))
+        ninth = jnp.where(live8, jnp.broadcast_to(ninth, (SUB, LANES)), 0.0)
+        p0, p1, p2 = [p.astype(F32) for p in pieces(value, 3)]
+        n0, n1, n2 = [p.astype(F32) for p in pieces(ninth, 3)]
+        r = rows_of((SUB, LANES))
+        n = jnp.where(r == 0, n0, jnp.where(r == 1, n1, jnp.where(r == 2, n2, 0.0)))
+        chunk = jnp.broadcast_to(jnp.where(live, jnp.right_shift(idx, 8), -1).astype(F32), (SUB, LANES))
+        n = jnp.where(r == 3, chunk, jnp.where(r == 4, 1.0, n))
+        return jnp.concatenate([p0, p1, p2, n], axis=0).astype(BF16)
+
+    def composite(t):
         trans = jnp.ones((SUB, pixels), F32)
         acc = [jnp.zeros((SUB, pixels), F32) for _ in range(3)]
         for q in range(groups):
-            out = dot(x_ref[t, :, q * LANES : (q + 1) * LANES], basis[...], TN)
+            x = fetch(t, q)
+            x_ref[t, :, q * LANES : (q + 1) * LANES] = x
+            out = dot(x, basis[...], TN)
             for i in range(LANES // SUB):
                 at = slice(i * SUB, (i + 1) * SUB)
                 alpha = jnp.exp2(out[at, :pixels])
@@ -146,9 +148,14 @@
             seg_ref[t, (2 + ch) * SUB : (3 + ch) * SUB] = acc[ch]
             image.append(jnp.sum(acc[ch] * before, axis=0, keepdims=True))
         img_ref[t] = jnp.concatenate(image, axis=0)
+
+    def body(i, carry):
+        for k in range(par):
+            composite(i * par + k)
         return carry
 
-    lax.fori_loop(0, tiles, composite, 0)
+    par = 4
+    lax.fori_loop(0, tiles // par, body, 0)
 
 
 def taps_of():
@@ -221,16 +228,36 @@
     )
 
 
-def backward_kernel(x_ref, idx_ref, seg_ref, cot_ref, basis, phi, out_ref, alphas, weights, grads, total):
+BLOCK = 16
+
+
+def backward_kernel(x_ref, idx_ref, seg_ref, cot_ref, basis, phi, out_ref, total, *buffers):
     tiles, pixels = cot_ref.shape[0], cot_ref.shape[2]
     count = x_ref.shape[2]
     groups = count // LANES
     steps = LANES // SUB
+    wide = 2 * LANES
     total[...] = jnp.zeros_like(total)
     row = rows_of((SUB, pixels))
-    row32 = rows_of((32, pixels))
-
-    def tile(t, carry):
+    each = 6
+    par = len(buffers) // each
+    columns = total.shape[1] // 2
+    field_lane = jnp.bitwise_and(lanes_of((2 * SUB, LANES)), BLOCK - 1)
+    select = (field_lane == rows_of((2 * SUB, LANES)) + 6).astype(F32).astype(BF16)
+
+    def first_pass(t, alphas, weights, factors, rhs, offs, split):
+        trans = seg_ref[t, 0:SUB]
+        for q in range(groups):
+            out = dot(x_ref[t, :, q * LANES : (q + 1) * LANES], basis[...], TN)
+            offs[q * LANES : (q + 1) * LANES] = out[:, pixels:]
+            for i in range(steps):
+                at = slice(q * LANES + i * SUB, q * LANES + (i + 1) * SUB)
+                alpha = jnp.exp2(out[i * SUB : (i + 1) * SUB, :pixels])
+                alphas[at] = alpha
+                weights[at] = alpha * trans
+                trans = trans * (1.0 - alpha)
+
+    def second_pass(t, alphas, weights, factors, rhs, offs, split):
         cot = [jnp.broadcast_to(cot_ref[t, ch : ch + 1], (SUB, pixels)) for ch in range(3)]
         hi = [c.astype(BF16).astype(F32) for c in cot]
         lo = [c - h for c, h in zip(cot, hi)]
@@ -240,9 +267,13 @@
             return [body, body, body, jnp.where(row < 3, v[2], 0.0)]
 
         rhs_g = jnp.concatenate(place(hi) + place(lo), axis=0).astype(BF16)
-        lhs = jnp.where(row == 6, hi[0], jnp.where(row == 7, hi[1], 0.0)) + phi[0:SUB]
-        lhs2 = jnp.where(row == 0, hi[2], jnp.where(row == 1, lo[0], jnp.where(row == 2, lo[1], jnp.where(row == 3, lo[2], 0.0))))
-        lhs = jnp.concatenate([lhs, lhs2], axis=0).astype(BF16)
+        six = jnp.zeros((SUB, pixels), F32)
+        for k, v in enumerate(hi + lo):
+            six = jnp.where(row == k, v, six)
+        six = jnp.concatenate([six, jnp.zeros((SUB, pixels), F32)], axis=0).astype(BF16)
+        six = dot(six, select, TN).astype(BF16)
+        rhs[2 * pixels : 3 * pixels] = six
+        rhs[3 * pixels :] = six
 
         seg = [seg_ref[t, s * SUB : (s + 1) * SUB] for s in range(5)]
         add = cot[0] * seg[2] + cot[1] * seg[3] + cot[2] * seg[4]
@@ -253,49 +284,58 @@
             mul_n = jnp.where(more, shifted(mul, -by), 1.0)
             add, mul = add + mul * add_n, mul * mul_n
         behind = jnp.where(row < SUB - 1, shifted(add, -1), 0.0)
-
-        trans = seg[0]
-        for q in range(groups):
-            out = dot(x_ref[t, :, q * LANES : (q + 1) * LANES], basis[:, :pixels], TN)
-            for i in range(steps):
-                at = slice(q * LANES + i * SUB, q * LANES + (i + 1) * SUB)
-                alpha = jnp.exp2(out[i * SUB : (i + 1) * SUB])
-                alphas[at] = alpha
-                weights[at] = alpha * trans
-                trans = trans * (1.0 - alpha)
         for q in reversed(range(groups)):
             x = x_ref[t, :, q * LANES : (q + 1) * LANES]
             g = dot(jnp.concatenate([x, x], axis=0), rhs_g, TN)
-            hs = [None] * steps
-            for i in reversed(range(steps)):
-                at = slice(q * LANES + i * SUB, q * LANES + (i + 1) * SUB)
-                d = g[i * SUB : (i + 1) * SUB] - behind
-                hs[i] = weights[at] * d
-                behind = behind + alphas[at] * d
-            h = jnp.concatenate(hs, axis=0)
-            h0, h1 = pieces(h, 2)
-            w0, w1 = pieces(weights[q * LANES : (q + 1) * LANES], 2)
-            gh = dot(lhs, h0, NT) + dot(lhs, h1, NT)
-            gw = dot(lhs, w0, NT) + dot(lhs, w1, NT)
-            r8 = rows_of((SUB, LANES))
-            low = gw[SUB:]
-            top = jnp.where(r8 < 6, gh[:SUB], gw[:SUB] + pltpu.roll(low, 5, 0))
-            ninth = jnp.broadcast_to((low + pltpu.roll(low, 5, 0))[0:1], (SUB, LANES))
-            grads[:, q * LANES : (q + 1) * LANES] = jnp.concatenate([top, ninth], axis=0)
+            for i in reversed(range(0, steps, 2)):
+                hs, ws = [], []
+                for j in (i + 1, i):
+                    at = slice(q * LANES + j * SUB, q * LANES + (j + 1) * SUB)
+                    d = g[j * SUB : (j + 1) * SUB] - behind
+                    w = weights[at]
+                    hs.insert(0, w * d)
+                    ws.insert(0, w)
+                    behind = behind + alphas[at] * d
+                at = slice(q * LANES + i * SUB, q * LANES + (i + 2) * SUB)
+                parts = pieces(jnp.concatenate(hs, axis=0), 2) + pieces(jnp.concatenate(ws, axis=0), 2)
+                for k, v in enumerate(parts):
+                    factors[at, k * pixels : (k + 1) * pixels] = v
+
+    def sums(t, alphas, weights, factors, rhs, offs, split):
+        got = dot(factors[...], rhs[...], NN)
         where = jnp.concatenate([idx_ref[pl.ds(t * groups + q, 1), :] for q in range(groups)], axis=1)
-        spread(grads[...], where, total)
+        low = jnp.bitwise_and(where, wide - 1)
+        hot = (jnp.broadcast_to(low, (wide, count)) == rows_of((wide, count))).astype(F32).astype(BF16)
+        for base in range(0, columns, LANES):
+            kept = jnp.where(offs[:, base : base + LANES] == 0.0, got, 0.0)
+            top, rest = pieces(kept, 2)
+            split[:, base : base + LANES] = top
+            split[:, columns + base : columns + base + LANES] = rest
+        total[...] += dot(hot, split[...], NN)
+
+    def body(i, carry):
+        for stage in (first_pass, second_pass, sums):
+            for k in range(par):
+                stage(i * par + k, *buffers[each * k : each * (k + 1)])
         return carry
 
-    lax.fori_loop(0, tiles, tile, 0)
+    for k in range(par):
+        buffers[each * k + 3][: 2 * pixels] = phi[...]
+    lax.fori_loop(0, tiles // par, body, 0)
     half = LANES // 2
     left = lanes_of((SUB, LANES)) < half
-    per = total.shape[1] // LANES
-    for c in range(total.shape[0] // 32):
-        eight, ninth = nine(total, c)
-        for j in range(per):
+    for c in range(columns // BLOCK):
+        if c % SUB == 0:
+            at = c // SUB * LANES
+            both = total[:, at : at + LANES] + total[:, columns + at : columns + at + LANES]
+            turned = jnp.concatenate([jnp.transpose(both[:LANES]), jnp.transpose(both[LANES:])], axis=1)
+        got = turned[c % SUB * BLOCK : (c % SUB + 1) * BLOCK]
+        eight = jnp.concatenate([got[:6], got[6:8] + got[9:11]], axis=0)
+        ninth = got[8:9] + got[11:12]
+        for j in range(2):
             e = eight[:, j * LANES : (j + 1) * LANES]
             n = jnp.broadcast_to(ninth[:, j * LANES : (j + 1) * LANES], (SUB, LANES))
-            at = (c * per + j) * 2 * SUB
+            at = (c * 2 + j) * 2 * SUB
             out_ref[at : at + SUB] = jnp.where(left, e, pltpu.roll(n, half, 1))
             out_ref[at + SUB : at + 2 * SUB] = jnp.where(left, pltpu.roll(e, half, 1), n)
 
@@ -343,24 +383,47 @@
             out_ref[i : i + 1, at] = v
 
 
-def tables(tile):
+def tables(tile, slots):
     pixels = tile * tile
+    wide = 2 * LANES
     p = np.arange(pixels)
     v = (p // tile) - (tile - 1) / 2.0
     u = (p % tile) - (tile - 1) / 2.0
     six = np.stack([np.ones(pixels), u, v, u * u, u * v, v * v])
-    basis = np.zeros((32, pixels + 3 * LANES), np.float32)
+    columns = slots // wide * BLOCK
+    ahead = np.zeros((32, pixels + 3 * LANES), np.float32)
+    back = np.zeros((32, pixels + columns), np.float32)
     for k in range(3):
-        basis[8 * k : 8 * k + 6, :pixels] = six
-        basis[8 * k + 6, pixels : pixels + LANES] = 1.0
-        basis[8 * k + 7, pixels + LANES : pixels + 2 * LANES] = 1.0
-        basis[24 + k, pixels + 2 * LANES :] = 1.0
-    phi = np.zeros((8, pixels), np.float32)
-    phi[:6] = six
-    return jnp.asarray(basis, BF16), jnp.asarray(phi)
-
-
-def call(kernel, out_shape, scratch=(), smem=0):
+        ahead[8 * k : 8 * k + 6, :pixels] = six
+        back[8 * k : 8 * k + 6, :pixels] = six
+        ahead[8 * k + 6, pixels : pixels + LANES] = 1.0
+        ahead[8 * k + 7, pixels + LANES : pixels + 2 * LANES] = 1.0
+        ahead[24 + k, pixels + 2 * LANES :] = 1.0
+    back[27, pixels:] = 1.0
+    back[28, pixels:] = -(np.arange(columns) // BLOCK)
+    phi = np.zeros((2 * pixels, LANES), np.float32)
+    for lane in range(LANES):
+        field = lane % BLOCK
+        if field < 6:
+            phi[:pixels, lane] = six[field]
+            phi[pixels:, lane] = six[field]
+    return jnp.asarray(ahead, BF16), jnp.asarray(back, BF16), jnp.asarray(phi, BF16)
+
+
+def back_scratch(list_len, pixels, slots, par=4):
+    columns = slots // (2 * LANES) * BLOCK
+    one = [
+        pltpu.VMEM((list_len, pixels), F32),
+        pltpu.VMEM((list_len, pixels), F32),
+        pltpu.VMEM((list_len, 4 * pixels), BF16),
+        pltpu.VMEM((4 * pixels, LANES), BF16),
+        pltpu.VMEM((list_len, columns), F32),
+        pltpu.VMEM((list_len, 2 * columns), BF16),
+    ]
+    return [pltpu.VMEM((2 * LANES, 2 * columns), F32)] + one * par
+
+
+def call(kernel, out_shape, scratch=(), smem=0, mib=48):
     n_vmem = pl.BlockSpec()
 
     def run(*args):
@@ -371,7 +434,7 @@
             in_specs=specs,
             out_specs=jax.tree.map(lambda _: n_vmem, out_shape),
             scratch_shapes=list(scratch),
-            compiler_params=pltpu.CompilerParams(vmem_limit_bytes=48 * 1024 * 1024),
+            compiler_params=pltpu.CompilerParams(vmem_limit_bytes=mib * 1024 * 1024),
         )(*args)
 
     return run
@@ -400,13 +463,14 @@
     pixels = tile * tile
     chunks = slot_count // LANES
     wide = 2 * LANES
-    basis, phi = tables(tile)
+    basis, basis_back, phi = tables(tile, slot_count)
     sds = jax.ShapeDtypeStruct
 
     packed = call(
         pack_kernel,
         sds((size * SUB, LANES), F32),
         [pltpu.VMEM((owned_count // LANES, SUB, LANES), F32), pltpu.VMEM((owned_count // LANES, LANES), F32)],
+        mib=63,
     )(send_rows, centres, conic, rho, opacity, colors)
     received = lax.all_to_all(packed, "dev", split_axis=0, concat_axis=0, tiled=True)
 
@@ -437,13 +501,8 @@
     slot_sums = call(
         backward_kernel,
         sds((size * SUB, LANES), F32),
-        [
-            pltpu.VMEM((list_len, pixels), F32),
-            pltpu.VMEM((list_len, pixels), F32),
-            pltpu.VMEM((2 * SUB, list_len), F32),
-            pltpu.VMEM((slot_count // wide * 32, wide), F32),
-        ],
-    )(coefs, order, segments, cot_tiles, basis, phi)
+        back_scratch(list_len, pixels, slot_count),
+    )(coefs, order, segments, cot_tiles, basis_back, phi)
     returned = lax.all_to_all(slot_sums, "dev", split_axis=0, concat_axis=0, tiled=True)
     grads = call(
         home_kernel,

time: 98.3 us -> 76.5 us (0.78)
  Pallas kernels: 58.1 us -> 40.6 us
  local copies, waits for them, and re-layouts: 6.69 us -> 2.61 us
    pallas_call x5, Pallas kernels: 58.1 us -> 40.6 us  [run(): pl.pallas_call(kernel, out_shape=out_shape, in_specs=specs, out_specs=jax...]
    unnamed x32 -> x22, local copies, waits for them, and re-layouts: 4.71 us -> 0.64 us
where the time goes in v2:
time: 76.5 us; the launch traced here: 76.1 us
  Pallas kernels  40.6 us (53%)
  blocking collectives  13.8 us (18%)
  starting transfers between devices  13.7 us (18%)
  waiting for transfers between devices  4.37 us (6%)
  local copies, waits for them, and re-layouts  2.61 us (3%)
  between operations  0.91 us (1%)
    pallas_call x5, Pallas kernels, run(): pl.pallas_call(kernel, out_shape=out_shape, in_specs=specs, out_specs=jax...  40.6 us
    all_to_all x1, blocking collectives, shards(): lax.all_to_all(slot_sums, 'dev', split_axis=0, concat_axis=0, tiled=True)  13.8 us
    all_to_all x1, starting transfers between devices, shards(): lax.all_to_all(packed, 'dev', split_axis=0, concat_axis=0, tiled=True)  7.3 us
    ppermute x2, starting transfers between devices, swap_edges(): got_in = lax.ppermute(jnp.where(odd, first, last), 'dev', inner)  5.06 us
    all_to_all x1, waiting for transfers between devices, shards(): lax.all_to_all(packed, 'dev', split_axis=0, concat_axis=0, tiled=True)  3.48 us
  transfers between devices with their start and end apart: 5, of which 2 were waited for; matrix products, arithmetic and copies ran while one was open for 2% of the time, Pallas kernels for 14%

profile of v2, /device:TPU:0, one launch (start us, length us, event | category | flops | bytes accessed | tf_op | source)
XLA Modules:
  0.0 76.1 jit_solution(12731353532159495541)
XLA Ops:
  0.6 2.9 %shard_map.122 = f32[256,128]{1,0:T(8,128)} custom-call(s32[1,2048]{1,0:T(1,128)} %rows_ref.3, f32[2,2048]{1,0:T(2,128)} %centres.3, f32[2,2048]{1,0:T(2,128)} %conic.3, f32[1,2048]{1,0:T(1,128)} %rho.3, f32[1,2048]{1,0:T(1,128)} %opacity.3, f32[3,2048]{1,0:T(4,128)} %colors.1), custom_call_target="tpu_custom_call" | custom-call | tf_op jit(solution)/shard_map/pallas_call | solution.py:431
  3.5 0.0 copy-start.1
  3.5 7.3 %all-to-all-start = ((f32[32,8,128]{2,1,0:T(8,128)}), f32[32,8,128]{2,1,0:T(8,128)S(1)}, u32[]{:S(2)}, u32[]{:S(2)}) async-start(f32[32,8,128]{2,1,0:T(8,128)} %bitcast.21), calls=%async_computation | async-start | bytes 262144 | tf_op jit(solution)/shard_map/all_to_all | solution.py:475
  10.9 0.0 copy-done.1
  10.9 0.0 copy-start.10
  10.9 0.7 collective-permute-start.3
  11.6 3.2 %collective-permute-start.2 = (f32[3,10,384]{2,1,0:T(8,128)S(1)}, f32[3,10,384]{2,1,0:T(8,128)S(1)}, u32[]{:S(2)}, u32[]{:S(2)}) collective-permute-start(f32[3,10,384]{2,1,0:T(8,128)S(1)} %get-tuple-element.13), channel_id=1, source_target_pairs={{0,1},{1,0},{2,3},{3,2},{4,5},{5,4},{6,7},{7,6},{8,9},{9,8},{10,11... | collective-permute-start | bytes 138248 | tf_op jit(solution)/shard_map/ppermute | solution.py:451
  14.8 0.0 copy-done.10
  14.8 0.1 reshape.26
  14.8 0.3 copy.16
  15.1 0.0 copy-start.5
  15.1 0.4 reshape.27.idx_ref
  15.5 0.1 pad_add_fusion.edge
  15.6 3.5 %all-to-all-done = f32[32,8,128]{2,1,0:T(8,128)S(1)} async-done(((f32[32,8,128]{2,1,0:T(8,128)}), f32[32,8,128]{2,1,0:T(8,128)S(1)}, u32[]{:S(2)}, u32[]{:S(2)}) %all-to-all-start) | async-done | bytes 131104 | tf_op jit(solution)/shard_map/all_to_all | solution.py:475
  19.1 0.0 copy-done.5
  19.1 10.5 %shard_map.123 = (f32[24,3,256]{2,1,0:T(4,128)S(1)}, bf16[24,32,512]{2,1,0:T(8,128)(2,1)S(1)}, f32[24,40,256]{2,1,0:T(8,128)S(1)}) custom-call(f32[256,128]{1,0:T(8,128)S(1)} %bitcast.16, s32[96,128]{1,0:T(8,128)S(1)} %reshape.27.idx_ref, bf16[32,640]{1,0:T(8,128)(2,1)S(1)} %copy-done.5), custom_call_target="tpu_custom_call" | custom-call | tf_op jit(solution)/shard_map/pallas_call | solution.py:431
  29.6 0.2 reshape.28
  29.8 0.2 copy.18
  30.0 0.2 reshape.29.ren
  30.2 0.0 copy-start
  30.3 0.7 collective-permute-start.1
  30.9 1.9 %collective-permute-start = (f32[3,10,384]{2,1,0:T(8,128)S(1)}, f32[3,10,384]{2,1,0:T(8,128)S(1)}, u32[]{:S(2)}, u32[]{:S(2)}) collective-permute-start(f32[3,10,384]{2,1,0:T(8,128)S(1)} %get-tuple-element.15), channel_id=1, source_target_pairs={{0,1},{1,0},{2,3},{3,2},{4,5},{5,4},{6,7},{7,6},{8,9},{9,8},{10,11... | collective-permute-start | bytes 138248 | tf_op jit(solution)/shard_map/ppermute | solution.py:451
  32.8 0.0 collective-permute-done.3
  32.8 0.0 collective-permute-done.2
  32.8 0.0 collective-permute-done.1
  32.8 0.9 %collective-permute-done = f32[3,10,384]{2,1,0:T(8,128)S(1)} collective-permute-done((f32[3,10,384]{2,1,0:T(8,128)S(1)}, f32[3,10,384]{2,1,0:T(8,128)S(1)}, u32[]{:S(2)}, u32[]{:S(2)}) %collective-permute-start) | collective-permute-done | bytes 46112 | tf_op jit(solution)/shard_map/ppermute | solution.py:451
  33.7 0.0 copy-done
  33.7 4.0 %shard_map.124 = f32[3,16,384]{2,1,0:T(8,128)S(1)} custom-call(s32[2]{0:T(128)S(1)} %pad_add_fusion.edge, f32[3,16,384]{2,1,0:T(8,128)S(1)} %reshape.29.ren, f32[3,16,384]{2,1,0:T(8,128)S(1)} %copy-done.1, f32[3,10,384]{2,1,0:T(8,128)S(1)} %get-tuple-element.11.ren_b, f32[3,10,384]{2,1,0:T(8,128)S(1)} %get-tuple-element.9.tar_b, ...), custom_call_target="tpu_custom_call" | custom-call | tf_op jit(solution)/shard_map/pallas_call | solution.py:431
  37.7 0.2 reshape.30
  37.9 0.1 copy.21
  38.1 0.0 copy-start.2
  38.1 0.0 copy-start.9
  38.1 0.3 reshape.32.cot_ref
  38.4 0.6 copy-done.2
  39.0 0.0 copy-done.9
  39.0 22.0 %shard_map.125 = f32[256,128]{1,0:T(8,128)S(1)} custom-call(bf16[24,32,512]{2,1,0:T(8,128)(2,1)S(1)} %get-tuple-element.6.x_ref, s32[96,128]{1,0:T(8,128)S(1)} %reshape.27.idx_ref, f32[24,40,256]{2,1,0:T(8,128)S(1)} %get-tuple-element.7.seg_ref, f32[24,3,256]{2,1,0:T(4,128)S(1)} %reshape.32.cot_ref, bf16[32,384]{1,0:T(8,128)(2,1)S(1)} %copy-done.9, ...), custom_call_target="tpu_custom_call" | custom-call | tf_op jit(solution)/shard_map/pallas_call | solution.py:431
  61.0 0.0 copy-start.3
  61.0 0.0 copy-start.4
  61.0 0.0 copy-start.6
  61.0 0.0 copy-start.7
  61.0 0.0 copy-start.8
  61.0 13.8 %all_to_all.22 = f32[32,8,128]{2,1,0:T(8,128)S(1)} all-to-all(f32[32,8,128]{2,1,0:T(8,128)S(1)} %bitcast.15), channel_id=1, replica_groups=mesh['dev'=32] {'dev'}, dimensions={0} | all-to-all | bytes 262144 | tf_op jit(solution)/shard_map/all_to_all | solution.py:506
  74.8 0.0 copy-done.3
  74.8 0.0 copy-done.4
  74.8 0.0 copy-done.6
  74.8 0.0 copy-done.7
  74.8 0.0 copy-done.8
  74.8 1.2 %shard_map.126 = f32[9,2048]{1,0:T(8,128)} custom-call(f32[256,128]{1,0:T(8,128)S(1)} %bitcast.17, s32[1,2048]{1,0:T(1,128)S(1)} %copy-done.6, f32[2,2048]{1,0:T(2,128)S(1)} %copy-done.3, f32[2,2048]{1,0:T(2,128)S(1)} %copy-done.4, f32[1,2048]{1,0:T(1,128)S(1)} %copy-done.7, f32[1,2048]{1,0:T(1,128)S(1)} %copy-done.8), custom_call_target="tpu_custom_call" | custom-call | tf_op jit(solution)/shard_map/pallas_call | solution.py:431
  (5 shorter events, 0.1 us)
Async XLA Ops:
  3.5 7.3 %copy-start.1 = (f32[3,16,384]{2,1,0:T(8,128)S(1)}, f32[3,16,384]{2,1,0:T(8,128)}, u32[]{:S(2)}) copy-start(f32[3,16,384]{2,1,0:T(8,128)} %tar.1) | copy-start | bytes 221188
  3.5 15.5 %all-to-all-start = ((f32[32,8,128]{2,1,0:T(8,128)}), f32[32,8,128]{2,1,0:T(8,128)S(1)}, u32[]{:S(2)}, u32[]{:S(2)}) async-start(f32[32,8,128]{2,1,0:T(8,128)} %bitcast.21), calls=%async_computation | async-start | bytes 262144 | tf_op jit(solution)/shard_map/all_to_all | solution.py:475
  10.9 3.9 %copy-start.10 = (s32[24,512]{1,0:T(8,128)S(1)}, s32[24,512]{1,0:T(8,128)}, u32[]{:S(2)}) copy-start(s32[24,512]{1,0:T(8,128)} %param.11) | copy-start | bytes 147460
  10.9 21.9 %collective-permute-start.3 = (f32[3,10,384]{2,1,0:T(8,128)S(1)}, f32[3,10,384]{2,1,0:T(8,128)S(1)}, u32[]{:S(2)}, u32[]{:S(2)}) collective-permute-start(f32[3,10,384]{2,1,0:T(8,128)S(1)} %get-tuple-element.12), channel_id=1, source_target_pairs={{1,2},{3,4},{5,6},{7,8},{9,10},{11,12},{13,14},{15,16},{17,18},{19... | collective-permute-start | bytes 138248 | tf_op jit(solution)/shard_map/ppermute | solution.py:452
  11.6 21.2 %collective-permute-start.2 = (f32[3,10,384]{2,1,0:T(8,128)S(1)}, f32[3,10,384]{2,1,0:T(8,128)S(1)}, u32[]{:S(2)}, u32[]{:S(2)}) collective-permute-start(f32[3,10,384]{2,1,0:T(8,128)S(1)} %get-tuple-element.13), channel_id=1, source_target_pairs={{0,1},{1,0},{2,3},{3,2},{4,5},{5,4},{6,7},{7,6},{8,9},{9,8},{10,11... | collective-permute-start | bytes 138248 | tf_op jit(solution)/shard_map/ppermute | solution.py:451
  15.1 3.9 %copy-start.5 = (bf16[32,640]{1,0:T(8,128)(2,1)S(1)}, bf16[32,640]{1,0:T(8,128)(2,1)}, u32[]{:S(2)}) copy-start(bf16[32,640]{1,0:T(8,128)(2,1)} %constant.35.clone.basis) | copy-start | bytes 122884
  30.2 3.5 %copy-start = (f32[3,16,384]{2,1,0:T(8,128)}, f32[3,16,384]{2,1,0:T(8,128)S(1)}, u32[]{:S(2)}) copy-start(f32[3,16,384]{2,1,0:T(8,128)S(1)} %reshape.29.ren) | copy-start | bytes 221188
  30.3 2.6 %collective-permute-start.1 = (f32[3,10,384]{2,1,0:T(8,128)S(1)}, f32[3,10,384]{2,1,0:T(8,128)S(1)}, u32[]{:S(2)}, u32[]{:S(2)}) collective-permute-start(f32[3,10,384]{2,1,0:T(8,128)S(1)} %get-tuple-element.14), channel_id=1, source_target_pairs={{1,2},{3,4},{5,6},{7,8},{9,10},{11,12},{13,14},{15,16},{17,18},{19... | collective-permute-start | bytes 138248 | tf_op jit(solution)/shard_map/ppermute | solution.py:452
  30.9 2.8 %collective-permute-start = (f32[3,10,384]{2,1,0:T(8,128)S(1)}, f32[3,10,384]{2,1,0:T(8,128)S(1)}, u32[]{:S(2)}, u32[]{:S(2)}) collective-permute-start(f32[3,10,384]{2,1,0:T(8,128)S(1)} %get-tuple-element.15), channel_id=1, source_target_pairs={{0,1},{1,0},{2,3},{3,2},{4,5},{5,4},{6,7},{7,6},{8,9},{9,8},{10,11... | collective-permute-start | bytes 138248 | tf_op jit(solution)/shard_map/ppermute | solution.py:451
  38.1 0.9 %copy-start.2 = (bf16[512,128]{1,0:T(8,128)(2,1)S(1)}, bf16[512,128]{1,0:T(8,128)(2,1)}, u32[]{:S(2)}) copy-start(bf16[512,128]{1,0:T(8,128)(2,1)} %constant.37.clone.phi) | copy-start | bytes 393220
  38.1 0.9 %copy-start.9 = (bf16[32,384]{1,0:T(8,128)(2,1)S(1)}, bf16[32,384]{1,0:T(8,128)(2,1)}, u32[]{:S(2)}) copy-start(bf16[32,384]{1,0:T(8,128)(2,1)} %constant.36.clone.basis) | copy-start | bytes 73732
  61.0 13.8 %copy-start.3 = (f32[2,2048]{1,0:T(2,128)S(1)}, f32[2,2048]{1,0:T(2,128)}, u32[]{:S(2)}) copy-start(f32[2,2048]{1,0:T(2,128)} %centres.3) | copy-start | bytes 49156
  61.0 13.8 %copy-start.4 = (f32[2,2048]{1,0:T(2,128)S(1)}, f32[2,2048]{1,0:T(2,128)}, u32[]{:S(2)}) copy-start(f32[2,2048]{1,0:T(2,128)} %conic.3) | copy-start | bytes 49156
  61.0 13.8 %copy-start.6 = (s32[1,2048]{1,0:T(1,128)S(1)}, s32[1,2048]{1,0:T(1,128)}, u32[]{:S(2)}) copy-start(s32[1,2048]{1,0:T(1,128)} %rows_ref.3) | copy-start | bytes 24580
  61.0 13.8 %copy-start.7 = (f32[1,2048]{1,0:T(1,128)S(1)}, f32[1,2048]{1,0:T(1,128)}, u32[]{:S(2)}) copy-start(f32[1,2048]{1,0:T(1,128)} %rho.3) | copy-start | bytes 24580
  61.0 13.8 %copy-start.8 = (f32[1,2048]{1,0:T(1,128)S(1)}, f32[1,2048]{1,0:T(1,128)}, u32[]{:S(2)}) copy-start(f32[1,2048]{1,0:T(1,128)} %opacity.3) | copy-start | bytes 24580

commit v3 on v2

--- a/solution.py
+++ b/solution.py
@@ -89,6 +89,10 @@
         out_ref[(2 * g + 1) * SUB : (2 * g + 2) * SUB] = jnp.where(left, pltpu.roll(value, half, 1), ninth)
 
 
+def part_of(count, most):
+    return max(d for d in range(1, most + 1) if count % d == 0)
+
+
 def shifted(x, by):
     return pltpu.roll(x, by % SUB, 0)
 
@@ -119,8 +123,6 @@
         n0, n1, n2 = [p.astype(F32) for p in pieces(ninth, 3)]
         r = rows_of((SUB, LANES))
         n = jnp.where(r == 0, n0, jnp.where(r == 1, n1, jnp.where(r == 2, n2, 0.0)))
-        chunk = jnp.broadcast_to(jnp.where(live, jnp.right_shift(idx, 8), -1).astype(F32), (SUB, LANES))
-        n = jnp.where(r == 3, chunk, jnp.where(r == 4, 1.0, n))
         return jnp.concatenate([p0, p1, p2, n], axis=0).astype(BF16)
 
     def composite(t):
@@ -154,7 +156,7 @@
             composite(i * par + k)
         return carry
 
-    par = 4
+    par = part_of(tiles, 4)
     lax.fori_loop(0, tiles // par, body, 0)
 
 
@@ -239,25 +241,13 @@
     wide = 2 * LANES
     total[...] = jnp.zeros_like(total)
     row = rows_of((SUB, pixels))
-    each = 6
-    par = len(buffers) // each
+    each = 3
     columns = total.shape[1] // 2
-    field_lane = jnp.bitwise_and(lanes_of((2 * SUB, LANES)), BLOCK - 1)
-    select = (field_lane == rows_of((2 * SUB, LANES)) + 6).astype(F32).astype(BF16)
-
-    def first_pass(t, alphas, weights, factors, rhs, offs, split):
-        trans = seg_ref[t, 0:SUB]
-        for q in range(groups):
-            out = dot(x_ref[t, :, q * LANES : (q + 1) * LANES], basis[...], TN)
-            offs[q * LANES : (q + 1) * LANES] = out[:, pixels:]
-            for i in range(steps):
-                at = slice(q * LANES + i * SUB, q * LANES + (i + 1) * SUB)
-                alpha = jnp.exp2(out[i * SUB : (i + 1) * SUB, :pixels])
-                alphas[at] = alpha
-                weights[at] = alpha * trans
-                trans = trans * (1.0 - alpha)
-
-    def second_pass(t, alphas, weights, factors, rhs, offs, split):
+    field = jnp.bitwise_and(lanes_of((SUB, LANES)), BLOCK - 1)
+    moment = jnp.bitwise_and(lanes_of((count, LANES)), BLOCK - 1) < 6
+    block = jnp.right_shift(lanes_of((LANES, LANES)), BLOCK.bit_length() - 1)
+
+    def sweep(t, factors, tints_ref, split):
         cot = [jnp.broadcast_to(cot_ref[t, ch : ch + 1], (SUB, pixels)) for ch in range(3)]
         hi = [c.astype(BF16).astype(F32) for c in cot]
         lo = [c - h for c, h in zip(cot, hi)]
@@ -266,62 +256,69 @@
             body = jnp.where(row == 6, v[0], jnp.where(row == 7, v[1], 0.0))
             return [body, body, body, jnp.where(row < 3, v[2], 0.0)]
 
-        rhs_g = jnp.concatenate(place(hi) + place(lo), axis=0).astype(BF16)
-        six = jnp.zeros((SUB, pixels), F32)
-        for k, v in enumerate(hi + lo):
-            six = jnp.where(row == k, v, six)
-        six = jnp.concatenate([six, jnp.zeros((SUB, pixels), F32)], axis=0).astype(BF16)
-        six = dot(six, select, TN).astype(BF16)
-        rhs[2 * pixels : 3 * pixels] = six
-        rhs[3 * pixels :] = six
-
-        seg = [seg_ref[t, s * SUB : (s + 1) * SUB] for s in range(5)]
-        add = cot[0] * seg[2] + cot[1] * seg[3] + cot[2] * seg[4]
-        mul = seg[1]
+        rhs = jnp.concatenate(place(hi) + place(lo), axis=0).astype(BF16)
+        rhs = jnp.concatenate([basis[...], rhs], axis=1)
+        trans = seg_ref[t, 0:SUB]
+        rest = trans * (cot[0] * seg_ref[t, 2 * SUB : 3 * SUB] + cot[1] * seg_ref[t, 3 * SUB : 4 * SUB] + cot[2] * seg_ref[t, 4 * SUB : 5 * SUB])
         for by in (1, 2, 4):
-            more = row < SUB - by
-            add_n = jnp.where(more, shifted(add, -by), 0.0)
-            mul_n = jnp.where(more, shifted(mul, -by), 1.0)
-            add, mul = add + mul * add_n, mul * mul_n
-        behind = jnp.where(row < SUB - 1, shifted(add, -1), 0.0)
-        for q in reversed(range(groups)):
+            rest = rest + jnp.where(row < SUB - by, shifted(rest, -by), 0.0)
+        for q in range(groups):
             x = x_ref[t, :, q * LANES : (q + 1) * LANES]
-            g = dot(jnp.concatenate([x, x], axis=0), rhs_g, TN)
-            for i in reversed(range(0, steps, 2)):
-                hs, ws = [], []
-                for j in (i + 1, i):
+            out = dot(jnp.concatenate([x, x], axis=0), rhs, TN)
+            for i in range(0, steps, 2):
+                hs = []
+                for j in (i, i + 1):
                     at = slice(q * LANES + j * SUB, q * LANES + (j + 1) * SUB)
-                    d = g[j * SUB : (j + 1) * SUB] - behind
-                    w = weights[at]
-                    hs.insert(0, w * d)
-                    ws.insert(0, w)
-                    behind = behind + alphas[at] * d
+                    alpha = jnp.exp2(out[j * SUB : (j + 1) * SUB, :pixels])
+                    w = alpha * trans
+                    clear = 1.0 - alpha
+                    trans = trans * clear
+                    wg = w * out[j * SUB : (j + 1) * SUB, pixels:]
+                    rest = rest - wg
+                    hs.append(wg - alpha * pl.reciprocal(clear, approx=True) * rest)
+                    tints = [jnp.sum(w * c, axis=1, keepdims=True) for c in cot]
+                    tints_ref[at] = jnp.where(field == 6, tints[0], jnp.where(field == 7, tints[1], tints[2]))
                 at = slice(q * LANES + i * SUB, q * LANES + (i + 2) * SUB)
-                parts = pieces(jnp.concatenate(hs, axis=0), 2) + pieces(jnp.concatenate(ws, axis=0), 2)
-                for k, v in enumerate(parts):
-                    factors[at, k * pixels : (k + 1) * pixels] = v
-
-    def sums(t, alphas, weights, factors, rhs, offs, split):
-        got = dot(factors[...], rhs[...], NN)
+                for p, v in enumerate(pieces(jnp.concatenate(hs, axis=0), 2)):
+                    factors[at, p * pixels : (p + 1) * pixels] = v
+
+    def sums(t, factors, tints_ref, split):
+        got = jnp.where(moment, dot(factors[...], phi[...], NN), tints_ref[...])
+        where = [idx_ref[pl.ds(t * groups + q, 1), :] for q in range(groups)]
+        where = jnp.concatenate(where + [where[0]] * (SUB - groups), axis=0)
+        chunk = jnp.transpose(jnp.where(where < 0, -1, jnp.right_shift(where, 8)))
+        for q in range(groups):
+            at = slice(q * LANES, (q + 1) * LANES)
+            mine = jnp.broadcast_to(chunk[:, q : q + 1], (LANES, LANES))
+            for base in range(0, columns, LANES):
+                kept = jnp.where(mine == block + base // BLOCK, got[at], 0.0)
+                top, rest = pieces(kept, 2)
+                split[at, base : base + LANES] = top
+                split[at, columns + base : columns + base + LANES] = rest
+
+    def scatter(t, factors, tints_ref, split):
         where = jnp.concatenate([idx_ref[pl.ds(t * groups + q, 1), :] for q in range(groups)], axis=1)
         low = jnp.bitwise_and(where, wide - 1)
         hot = (jnp.broadcast_to(low, (wide, count)) == rows_of((wide, count))).astype(F32).astype(BF16)
-        for base in range(0, columns, LANES):
-            kept = jnp.where(offs[:, base : base + LANES] == 0.0, got, 0.0)
-            top, rest = pieces(kept, 2)
-            split[:, base : base + LANES] = top
-            split[:, columns + base : columns + base + LANES] = rest
         total[...] += dot(hot, split[...], NN)
 
+    par = len(buffers) // each
+
     def body(i, carry):
-        for stage in (first_pass, second_pass, sums):
-            for k in range(par):
-                stage(i * par + k, *buffers[each * k : each * (k + 1)])
+        for k in range(par):
+            now = buffers[each * k : each * (k + 1)]
+            last = buffers[each * ((k - 1) % par) :][:each]
+            t = i * par + k
+            sums(jnp.maximum(t - 1, 0), *last)
+            sweep(t, *now)
+            scatter(jnp.maximum(t - 1, 0), *last)
         return carry
 
-    for k in range(par):
-        buffers[each * k + 3][: 2 * pixels] = phi[...]
+    buffers[each * (par - 1)][...] = jnp.zeros((count, 2 * pixels), BF16)
+    buffers[each * (par - 1) + 1][...] = jnp.zeros((count, LANES), F32)
     lax.fori_loop(0, tiles // par, body, 0)
+    sums(tiles - 1, *buffers[each * (par - 1) :])
+    scatter(tiles - 1, *buffers[each * (par - 1) :])
     half = LANES // 2
     left = lanes_of((SUB, LANES)) < half
     for c in range(columns // BLOCK):
@@ -330,8 +327,7 @@
             both = total[:, at : at + LANES] + total[:, columns + at : columns + at + LANES]
             turned = jnp.concatenate([jnp.transpose(both[:LANES]), jnp.transpose(both[LANES:])], axis=1)
         got = turned[c % SUB * BLOCK : (c % SUB + 1) * BLOCK]
-        eight = jnp.concatenate([got[:6], got[6:8] + got[9:11]], axis=0)
-        ninth = got[8:9] + got[11:12]
+        eight, ninth = got[:SUB], got[SUB : SUB + 1]
         for j in range(2):
             e = eight[:, j * LANES : (j + 1) * LANES]
             n = jnp.broadcast_to(ninth[:, j * LANES : (j + 1) * LANES], (SUB, LANES))
@@ -390,17 +386,14 @@
     v = (p // tile) - (tile - 1) / 2.0
     u = (p % tile) - (tile - 1) / 2.0
     six = np.stack([np.ones(pixels), u, v, u * u, u * v, v * v])
-    columns = slots // wide * BLOCK
     ahead = np.zeros((32, pixels + 3 * LANES), np.float32)
-    back = np.zeros((32, pixels + columns), np.float32)
+    back = np.zeros((64, pixels), np.float32)
     for k in range(3):
         ahead[8 * k : 8 * k + 6, :pixels] = six
         back[8 * k : 8 * k + 6, :pixels] = six
         ahead[8 * k + 6, pixels : pixels + LANES] = 1.0
         ahead[8 * k + 7, pixels + LANES : pixels + 2 * LANES] = 1.0
         ahead[24 + k, pixels + 2 * LANES :] = 1.0
-    back[27, pixels:] = 1.0
-    back[28, pixels:] = -(np.arange(columns) // BLOCK)
     phi = np.zeros((2 * pixels, LANES), np.float32)
     for lane in range(LANES):
         field = lane % BLOCK
@@ -410,14 +403,11 @@
     return jnp.asarray(ahead, BF16), jnp.asarray(back, BF16), jnp.asarray(phi, BF16)
 
 
-def back_scratch(list_len, pixels, slots, par=4):
+def back_scratch(list_len, pixels, slots, par):
     columns = slots // (2 * LANES) * BLOCK
     one = [
-        pltpu.VMEM((list_len, pixels), F32),
-        pltpu.VMEM((list_len, pixels), F32),
-        pltpu.VMEM((list_len, 4 * pixels), BF16),
-        pltpu.VMEM((4 * pixels, LANES), BF16),
-        pltpu.VMEM((list_len, columns), F32),
+        pltpu.VMEM((list_len, 2 * pixels), BF16),
+        pltpu.VMEM((list_len, LANES), F32),
         pltpu.VMEM((list_len, 2 * columns), BF16),
     ]
     return [pltpu.VMEM((2 * LANES, 2 * columns), F32)] + one * par
@@ -501,7 +491,7 @@
     slot_sums = call(
         backward_kernel,
         sds((size * SUB, LANES), F32),
-        back_scratch(list_len, pixels, slot_count),
+        back_scratch(list_len, pixels, slot_count, part_of(strip_tiles, 6)),
     )(coefs, order, segments, cot_tiles, basis_back, phi)
     returned = lax.all_to_all(slot_sums, "dev", split_axis=0, concat_axis=0, tiled=True)
     grads = call(

time: 76.5 us -> 70.6 us (0.923)
  Pallas kernels: 40.6 us -> 34.7 us
    pallas_call x5, Pallas kernels: 40.6 us -> 34.7 us  [run(): pl.pallas_call(kernel, out_shape=out_shape, in_specs=specs, out_specs=jax...]
  transfers between devices with their start and end apart: 5 -> 5, of which waited for: 2 -> 2; matrix products, arithmetic and copies ran while one was open for 2% -> 2% of each run, Pallas kernels for 14% -> 15%
where the time goes in v3:
time: 70.6 us; the launch traced here: 70.1 us
  Pallas kernels  34.7 us (49%)
  starting transfers between devices  13.9 us (20%)
  blocking collectives  13.6 us (19%)
  waiting for transfers between devices  4.37 us (6%)
  local copies, waits for them, and re-layouts  2.61 us (4%)
  between operations  0.9 us (1%)
    pallas_call x5, Pallas kernels, run(): pl.pallas_call(kernel, out_shape=out_shape, in_specs=specs, out_specs=jax...  34.7 us
    all_to_all x1, blocking collectives, shards(): lax.all_to_all(slot_sums, 'dev', split_axis=0, concat_axis=0, tiled=True)  13.6 us
    all_to_all x1, starting transfers between devices, shards(): lax.all_to_all(packed, 'dev', split_axis=0, concat_axis=0, tiled=True)  7.3 us
    ppermute x2, starting transfers between devices, swap_edges(): got_in = lax.ppermute(jnp.where(odd, first, last), 'dev', inner)  5.06 us
    all_to_all x1, waiting for transfers between devices, shards(): lax.all_to_all(packed, 'dev', split_axis=0, concat_axis=0, tiled=True)  3.48 us
    ppermute x2, starting transfers between devices, swap_edges(): got_out = lax.ppermute(jnp.where(odd, last, first), 'dev', outer)  1.51 us
  transfers between devices with their start and end apart: 5, of which 2 were waited for; matrix products, arithmetic and copies ran while one was open for 2% of the time, Pallas kernels for 15%

profile of v3, /device:TPU:0, one launch (start us, length us, event | category | flops | bytes accessed | tf_op | source)
XLA Modules:
  0.0 70.1 jit_solution(8252112440099052416)
XLA Ops:
  0.6 2.9 %shard_map.122 = f32[256,128]{1,0:T(8,128)} custom-call(s32[1,2048]{1,0:T(1,128)} %rows_ref.3, f32[2,2048]{1,0:T(2,128)} %centres.3, f32[2,2048]{1,0:T(2,128)} %conic.3, f32[1,2048]{1,0:T(1,128)} %rho.3, f32[1,2048]{1,0:T(1,128)} %opacity.3, f32[3,2048]{1,0:T(4,128)} %colors.1), custom_call_target="tpu_custom_call" | custom-call | tf_op jit(solution)/shard_map/pallas_call | solution.py:421
  3.5 0.0 copy-start.1
  3.5 7.3 %all-to-all-start = ((f32[32,8,128]{2,1,0:T(8,128)}), f32[32,8,128]{2,1,0:T(8,128)S(1)}, u32[]{:S(2)}, u32[]{:S(2)}) async-start(f32[32,8,128]{2,1,0:T(8,128)} %bitcast.21), calls=%async_computation | async-start | bytes 262144 | tf_op jit(solution)/shard_map/all_to_all | solution.py:465
  10.9 0.0 copy-done.1
  10.9 0.0 copy-start.10
  10.9 0.7 collective-permute-start.3
  11.6 3.2 %collective-permute-start.2 = (f32[3,10,384]{2,1,0:T(8,128)S(1)}, f32[3,10,384]{2,1,0:T(8,128)S(1)}, u32[]{:S(2)}, u32[]{:S(2)}) collective-permute-start(f32[3,10,384]{2,1,0:T(8,128)S(1)} %get-tuple-element.13), channel_id=1, source_target_pairs={{0,1},{1,0},{2,3},{3,2},{4,5},{5,4},{6,7},{7,6},{8,9},{9,8},{10,11... | collective-permute-start | bytes 138248 | tf_op jit(solution)/shard_map/ppermute | solution.py:441
  14.8 0.0 copy-done.10
  14.8 0.1 reshape.26
  14.8 0.3 copy.16
  15.1 0.0 copy-start.5
  15.1 0.4 reshape.27.idx_ref
  15.5 0.1 pad_add_fusion.edge
  15.6 3.5 %all-to-all-done = f32[32,8,128]{2,1,0:T(8,128)S(1)} async-done(((f32[32,8,128]{2,1,0:T(8,128)}), f32[32,8,128]{2,1,0:T(8,128)S(1)}, u32[]{:S(2)}, u32[]{:S(2)}) %all-to-all-start) | async-done | bytes 131104 | tf_op jit(solution)/shard_map/all_to_all | solution.py:465
  19.1 0.0 copy-done.5
  19.1 10.4 %shard_map.123 = (f32[24,3,256]{2,1,0:T(4,128)S(1)}, bf16[24,32,512]{2,1,0:T(8,128)(2,1)S(1)}, f32[24,40,256]{2,1,0:T(8,128)S(1)}) custom-call(f32[256,128]{1,0:T(8,128)S(1)} %bitcast.16, s32[96,128]{1,0:T(8,128)S(1)} %reshape.27.idx_ref, bf16[32,640]{1,0:T(8,128)(2,1)S(1)} %copy-done.5), custom_call_target="tpu_custom_call" | custom-call | tf_op jit(solution)/shard_map/pallas_call | solution.py:421
  29.5 0.2 reshape.28
  29.7 0.2 copy.18
  29.9 0.2 reshape.29.ren
  30.1 0.0 copy-start
  30.2 0.8 %collective-permute-start.1 = (f32[3,10,384]{2,1,0:T(8,128)S(1)}, f32[3,10,384]{2,1,0:T(8,128)S(1)}, u32[]{:S(2)}, u32[]{:S(2)}) collective-permute-start(f32[3,10,384]{2,1,0:T(8,128)S(1)} %get-tuple-element.14), channel_id=1, source_target_pairs={{1,2},{3,4},{5,6},{7,8},{9,10},{11,12},{13,14},{15,16},{17,18},{19... | collective-permute-start | bytes 138248 | tf_op jit(solution)/shard_map/ppermute | solution.py:442
  31.0 1.9 %collective-permute-start = (f32[3,10,384]{2,1,0:T(8,128)S(1)}, f32[3,10,384]{2,1,0:T(8,128)S(1)}, u32[]{:S(2)}, u32[]{:S(2)}) collective-permute-start(f32[3,10,384]{2,1,0:T(8,128)S(1)} %get-tuple-element.15), channel_id=1, source_target_pairs={{0,1},{1,0},{2,3},{3,2},{4,5},{5,4},{6,7},{7,6},{8,9},{9,8},{10,11... | collective-permute-start | bytes 138248 | tf_op jit(solution)/shard_map/ppermute | solution.py:441
  32.9 0.0 collective-permute-done.3
  32.9 0.0 collective-permute-done.2
  32.9 0.0 collective-permute-done.1
  32.9 0.9 %collective-permute-done = f32[3,10,384]{2,1,0:T(8,128)S(1)} collective-permute-done((f32[3,10,384]{2,1,0:T(8,128)S(1)}, f32[3,10,384]{2,1,0:T(8,128)S(1)}, u32[]{:S(2)}, u32[]{:S(2)}) %collective-permute-start) | collective-permute-done | bytes 46112 | tf_op jit(solution)/shard_map/ppermute | solution.py:441
  33.8 0.0 copy-done
  33.8 4.0 %shard_map.124 = f32[3,16,384]{2,1,0:T(8,128)S(1)} custom-call(s32[2]{0:T(128)S(1)} %pad_add_fusion.edge, f32[3,16,384]{2,1,0:T(8,128)S(1)} %reshape.29.ren, f32[3,16,384]{2,1,0:T(8,128)S(1)} %copy-done.1, f32[3,10,384]{2,1,0:T(8,128)S(1)} %get-tuple-element.11.ren_b, f32[3,10,384]{2,1,0:T(8,128)S(1)} %get-tuple-element.9.tar_b, ...), custom_call_target="tpu_custom_call" | custom-call | tf_op jit(solution)/shard_map/pallas_call | solution.py:421
  37.8 0.2 reshape.30
  38.0 0.1 copy.21
  38.2 0.0 copy-start.2
  38.2 0.0 copy-start.6
  38.2 0.3 reshape.32.cot_ref
  38.5 0.6 copy-done.2
  39.1 0.0 copy-done.6
  39.1 16.2 %shard_map.125 = f32[256,128]{1,0:T(8,128)S(1)} custom-call(bf16[24,32,512]{2,1,0:T(8,128)(2,1)S(1)} %get-tuple-element.6.x_ref, s32[96,128]{1,0:T(8,128)S(1)} %reshape.27.idx_ref, f32[24,40,256]{2,1,0:T(8,128)S(1)} %get-tuple-element.7.seg_ref, f32[24,3,256]{2,1,0:T(4,128)S(1)} %reshape.32.cot_ref, bf16[64,256]{1,0:T(8,128)(2,1)S(1)} %copy-done.6, ...), custom_call_target="tpu_custom_call" | custom-call | tf_op jit(solution)/shard_map/pallas_call | solution.py:421
  55.2 0.0 copy-start.3
  55.2 0.0 copy-start.4
  55.3 0.0 copy-start.7
  55.3 0.0 copy-start.8
  55.3 0.0 copy-start.9
  55.3 13.6 %all_to_all.22 = f32[32,8,128]{2,1,0:T(8,128)S(1)} all-to-all(f32[32,8,128]{2,1,0:T(8,128)S(1)} %bitcast.15), channel_id=1, replica_groups=mesh['dev'=32] {'dev'}, dimensions={0} | all-to-all | bytes 262144 | tf_op jit(solution)/shard_map/all_to_all | solution.py:496
  68.9 0.0 copy-done.3
  68.9 0.0 copy-done.4
  68.9 0.0 copy-done.7
  68.9 0.0 copy-done.8
  68.9 0.0 copy-done.9
  68.9 1.2 %shard_map.126 = f32[9,2048]{1,0:T(8,128)} custom-call(f32[256,128]{1,0:T(8,128)S(1)} %bitcast.17, s32[1,2048]{1,0:T(1,128)S(1)} %copy-done.7, f32[2,2048]{1,0:T(2,128)S(1)} %copy-done.3, f32[2,2048]{1,0:T(2,128)S(1)} %copy-done.4, f32[1,2048]{1,0:T(1,128)S(1)} %copy-done.8, f32[1,2048]{1,0:T(1,128)S(1)} %copy-done.9), custom_call_target="tpu_custom_call" | custom-call | tf_op jit(solution)/shard_map/pallas_call | solution.py:421
  (5 shorter events, 0.1 us)
Async XLA Ops:
  3.5 7.3 %copy-start.1 = (f32[3,16,384]{2,1,0:T(8,128)S(1)}, f32[3,16,384]{2,1,0:T(8,128)}, u32[]{:S(2)}) copy-start(f32[3,16,384]{2,1,0:T(8,128)} %tar.1) | copy-start | bytes 221188
  3.5 15.5 %all-to-all-start = ((f32[32,8,128]{2,1,0:T(8,128)}), f32[32,8,128]{2,1,0:T(8,128)S(1)}, u32[]{:S(2)}, u32[]{:S(2)}) async-start(f32[32,8,128]{2,1,0:T(8,128)} %bitcast.21), calls=%async_computation | async-start | bytes 262144 | tf_op jit(solution)/shard_map/all_to_all | solution.py:465
  10.9 3.9 %copy-start.10 = (s32[24,512]{1,0:T(8,128)S(1)}, s32[24,512]{1,0:T(8,128)}, u32[]{:S(2)}) copy-start(s32[24,512]{1,0:T(8,128)} %param.11) | copy-start | bytes 147460
  10.9 22.0 %collective-permute-start.3 = (f32[3,10,384]{2,1,0:T(8,128)S(1)}, f32[3,10,384]{2,1,0:T(8,128)S(1)}, u32[]{:S(2)}, u32[]{:S(2)}) collective-permute-start(f32[3,10,384]{2,1,0:T(8,128)S(1)} %get-tuple-element.12), channel_id=1, source_target_pairs={{1,2},{3,4},{5,6},{7,8},{9,10},{11,12},{13,14},{15,16},{17,18},{19... | collective-permute-start | bytes 138248 | tf_op jit(solution)/shard_map/ppermute | solution.py:442
  11.6 21.3 %collective-permute-start.2 = (f32[3,10,384]{2,1,0:T(8,128)S(1)}, f32[3,10,384]{2,1,0:T(8,128)S(1)}, u32[]{:S(2)}, u32[]{:S(2)}) collective-permute-start(f32[3,10,384]{2,1,0:T(8,128)S(1)} %get-tuple-element.13), channel_id=1, source_target_pairs={{0,1},{1,0},{2,3},{3,2},{4,5},{5,4},{6,7},{7,6},{8,9},{9,8},{10,11... | collective-permute-start | bytes 138248 | tf_op jit(solution)/shard_map/ppermute | solution.py:441
  15.1 3.9 %copy-start.5 = (bf16[32,640]{1,0:T(8,128)(2,1)S(1)}, bf16[32,640]{1,0:T(8,128)(2,1)}, u32[]{:S(2)}) copy-start(bf16[32,640]{1,0:T(8,128)(2,1)} %constant.35.clone.basis) | copy-start | bytes 122884
  30.1 3.7 %copy-start = (f32[3,16,384]{2,1,0:T(8,128)}, f32[3,16,384]{2,1,0:T(8,128)S(1)}, u32[]{:S(2)}) copy-start(f32[3,16,384]{2,1,0:T(8,128)S(1)} %reshape.29.ren) | copy-start | bytes 221188
  30.2 2.7 %collective-permute-start.1 = (f32[3,10,384]{2,1,0:T(8,128)S(1)}, f32[3,10,384]{2,1,0:T(8,128)S(1)}, u32[]{:S(2)}, u32[]{:S(2)}) collective-permute-start(f32[3,10,384]{2,1,0:T(8,128)S(1)} %get-tuple-element.14), channel_id=1, source_target_pairs={{1,2},{3,4},{5,6},{7,8},{9,10},{11,12},{13,14},{15,16},{17,18},{19... | collective-permute-start | bytes 138248 | tf_op jit(solution)/shard_map/ppermute | solution.py:442
  31.0 2.8 %collective-permute-start = (f32[3,10,384]{2,1,0:T(8,128)S(1)}, f32[3,10,384]{2,1,0:T(8,128)S(1)}, u32[]{:S(2)}, u32[]{:S(2)}) collective-permute-start(f32[3,10,384]{2,1,0:T(8,128)S(1)} %get-tuple-element.15), channel_id=1, source_target_pairs={{0,1},{1,0},{2,3},{3,2},{4,5},{5,4},{6,7},{7,6},{8,9},{9,8},{10,11... | collective-permute-start | bytes 138248 | tf_op jit(solution)/shard_map/ppermute | solution.py:441
  38.2 0.9 %copy-start.2 = (bf16[512,128]{1,0:T(8,128)(2,1)S(1)}, bf16[512,128]{1,0:T(8,128)(2,1)}, u32[]{:S(2)}) copy-start(bf16[512,128]{1,0:T(8,128)(2,1)} %constant.37.clone.phi) | copy-start | bytes 393220
  38.2 0.9 %copy-start.6 = (bf16[64,256]{1,0:T(8,128)(2,1)S(1)}, bf16[64,256]{1,0:T(8,128)(2,1)}, u32[]{:S(2)}) copy-start(bf16[64,256]{1,0:T(8,128)(2,1)} %constant.36.clone.basis) | copy-start | bytes 98308
  55.2 13.6 %copy-start.3 = (f32[2,2048]{1,0:T(2,128)S(1)}, f32[2,2048]{1,0:T(2,128)}, u32[]{:S(2)}) copy-start(f32[2,2048]{1,0:T(2,128)} %centres.3) | copy-start | bytes 49156
  55.2 13.6 %copy-start.4 = (f32[2,2048]{1,0:T(2,128)S(1)}, f32[2,2048]{1,0:T(2,128)}, u32[]{:S(2)}) copy-start(f32[2,2048]{1,0:T(2,128)} %conic.3) | copy-start | bytes 49156
  55.3 13.6 %copy-start.7 = (s32[1,2048]{1,0:T(1,128)S(1)}, s32[1,2048]{1,0:T(1,128)}, u32[]{:S(2)}) copy-start(s32[1,2048]{1,0:T(1,128)} %rows_ref.3) | copy-start | bytes 24580
  55.3 13.6 %copy-start.8 = (f32[1,2048]{1,0:T(1,128)S(1)}, f32[1,2048]{1,0:T(1,128)}, u32[]{:S(2)}) copy-start(f32[1,2048]{1,0:T(1,128)} %rho.3) | copy-start | bytes 24580
  55.3 13.6 %copy-start.9 = (f32[1,2048]{1,0:T(1,128)S(1)}, f32[1,2048]{1,0:T(1,128)}, u32[]{:S(2)}) copy-start(f32[1,2048]{1,0:T(1,128)} %opacity.3) | copy-start | bytes 24580

commit v4 on v3

--- a/solution.py
+++ b/solution.py
@@ -12,6 +12,7 @@
 SUB = 8
 RIM = 5
 HALO = 2 * RIM
+BLOCK = 16
 LOG2E = 1.4426950408889634
 F32 = jnp.float32
 BF16 = jnp.bfloat16
@@ -97,41 +98,46 @@
     return pltpu.roll(x, by % SUB, 0)
 
 
-def forward_kernel(recv, idx_ref, basis, img_ref, x_ref, seg_ref, table, last):
-    chunks = table.shape[0]
+def forward_kernel(recv, idx_ref, basis, img_ref, x_ref, seg_ref, table):
     tiles, pixels = img_ref.shape[0], img_ref.shape[2]
     groups = x_ref.shape[2] // LANES
+    wide = table.shape[1]
     half = LANES // 2
     left = lanes_of((SUB, LANES)) < half
-    for c in range(chunks):
-        a = recv[2 * c * SUB : (2 * c + 1) * SUB]
-        b = recv[(2 * c + 1) * SUB : (2 * c + 2) * SUB]
-        table[c] = jnp.where(left, a, pltpu.roll(b, half, 1))
-        last[c : c + 1] = jnp.where(left, pltpu.roll(a, half, 1), b)[0:1]
-    first = rows_of((SUB, LANES)) == 0
-
+    r = rows_of((SUB, wide))
+    for c in range(table.shape[0] // 32):
+        eights, ninths = [], []
+        for j in range(wide // LANES):
+            at = (c * (wide // LANES) + j) * 2 * SUB
+            a, b = recv[at : at + SUB], recv[at + SUB : at + 2 * SUB]
+            eights.append(jnp.where(left, a, pltpu.roll(b, half, 1)))
+            n = jnp.where(left, pltpu.roll(a, half, 1), b)
+            ninths.append(jnp.broadcast_to(n[0:1], (SUB, LANES)))
+        p = [v.astype(F32) for v in pieces(jnp.concatenate(eights, axis=1), 3)]
+        n = [v.astype(F32) for v in pieces(jnp.concatenate(ninths, axis=1), 3)]
+        tail = jnp.where(r == 0, n[0], jnp.where(r == 1, n[1], jnp.where(r == 2, n[2], 0.0)))
+        table[c * 32 : (c + 1) * 32] = jnp.concatenate(p + [tail], axis=0).astype(BF16)
     row = rows_of((SUB, pixels))
 
-    def fetch(t, q):
-        idx = idx_ref[pl.ds(t * groups + q, 1), :]
-        live = idx >= 0
-        value, ninth = pick(table, last, jnp.maximum(idx, 0))
-        live8 = jnp.broadcast_to(live, (SUB, LANES))
-        value = jnp.where(live8, value, jnp.where(first, -1000.0, 0.0))
-        ninth = jnp.where(live8, jnp.broadcast_to(ninth, (SUB, LANES)), 0.0)
-        p0, p1, p2 = [p.astype(F32) for p in pieces(value, 3)]
-        n0, n1, n2 = [p.astype(F32) for p in pieces(ninth, 3)]
-        r = rows_of((SUB, LANES))
-        n = jnp.where(r == 0, n0, jnp.where(r == 1, n1, jnp.where(r == 2, n2, 0.0)))
-        return jnp.concatenate([p0, p1, p2, n], axis=0).astype(BF16)
+    def fetch(t):
+        per = wide // LANES
+        for q in range(0, groups, per):
+            idx = jnp.concatenate([idx_ref[pl.ds(t * groups + q + j, 1), :] for j in range(per)], axis=1)
+            low = jnp.broadcast_to(jnp.bitwise_and(idx, wide - 1), (wide, wide))
+            hot = (low == rows_of((wide, wide))).astype(F32).astype(BF16)
+            got = dot(table[...], hot, NN)
+            chunk = jnp.where(idx < 0, -1, jnp.right_shift(idx, wide.bit_length() - 1))
+            chunk = jnp.broadcast_to(chunk, (32, wide))
+            x = jnp.where(jnp.logical_and(chunk < 0, rows_of((32, wide)) == 0), -1000.0, 0.0)
+            for c in range(table.shape[0] // 32):
+                x = jnp.where(chunk == c, got[c * 32 : (c + 1) * 32], x)
+            x_ref[t, :, q * LANES : (q + per) * LANES] = x.astype(BF16)
 
     def composite(t):
         trans = jnp.ones((SUB, pixels), F32)
         acc = [jnp.zeros((SUB, pixels), F32) for _ in range(3)]
         for q in range(groups):
-            x = fetch(t, q)
-            x_ref[t, :, q * LANES : (q + 1) * LANES] = x
-            out = dot(x, basis[...], TN)
+            out = dot(x_ref[t, :, q * LANES : (q + 1) * LANES], basis[...], TN)
             for i in range(LANES // SUB):
                 at = slice(i * SUB, (i + 1) * SUB)
                 alpha = jnp.exp2(out[at, :pixels])
@@ -153,6 +159,8 @@
 
     def body(i, carry):
         for k in range(par):
+            fetch(i * par + k)
+        for k in range(par):
             composite(i * par + k)
         return carry
 
@@ -160,38 +168,44 @@
     lax.fori_loop(0, tiles // par, body, 0)
 
 
-def taps_of():
-    m = np.arange(-RIM, RIM + 1)
-    w = np.exp(-m * m / 4.5)
-    return [float(v) for v in w / w.sum()]
-
-
-def blur_rows(x, count):
-    taps = taps_of()
-    width = x.shape[1]
-    out = taps[RIM] * x[RIM : RIM + count]
-    for m in range(1, RIM + 1):
-        out = out + taps[RIM + m] * (x[RIM - m : RIM - m + count] + x[RIM + m : RIM + m + count])
-    lane = lanes_of(out.shape)
-    res = taps[RIM] * out
-    for m in range(1, RIM + 1):
-        up = jnp.where(lane >= m, pltpu.roll(out, m, 1), 0.0)
-        down = jnp.where(lane < width - m, pltpu.roll(out, width - m, 1), 0.0)
-        res = res + taps[RIM + m] * (up + down)
-    return res
-
-
-def ssim_kernel(edge, ren, tar, ren_b, tar_b, ren_a, tar_a, cot_ref):
-    rows = ren.shape[1]
-    width = ren.shape[2]
-    mid = rows + HALO
-    r_at = rows_of((mid, width))
+def exact(a, b):
+    return sum(dot(a[i], b[j], NN) for i in range(3) for j in range(3 - i))
+
+
+def blur(images, rows, cols):
+    height = rows.shape[0] // 3
+    done = []
+    for x in images:
+        got = dot(rows[...], jnp.concatenate(pieces(x, 3), axis=0), NN)
+        done.append(got[:height] + got[height : 2 * height] + got[2 * height :])
+    stacked = jnp.concatenate(done, axis=0)
+    out = exact(pieces(stacked, 3), [cols[k] for k in range(3)])
+    return [out[i * height : (i + 1) * height] for i in range(len(images))]
+
+
+def padded(own, before, after, ch):
+    fill = jnp.zeros((-HALO % SUB, own.shape[2]), F32)
+    return jnp.concatenate([own[ch], before[ch], fill, after[ch], fill], axis=0)
+
+
+def target_kernel(tar, tar_b, tar_a, rows, cols, out_ref):
+    channels = tar.shape[0]
+    images = [padded(tar, tar_b, tar_a, ch) for ch in range(channels)]
+    for i, v in enumerate(blur(images + [x * x for x in images], rows, cols)):
+        out_ref[i] = v
+
+
+def ssim_kernel(edge, ren, tar, ren_b, tar_b, ren_a, tar_a, known, rows, back, cols, cot_ref):
+    channels, height, width = ren.shape
+    r_at = rows_of((rows.shape[0] // 3, width))
     inside = jnp.logical_and(r_at >= edge[0], r_at < edge[1])
-    for ch in range(ren.shape[0]):
-        r = jnp.concatenate([ren_b[ch], ren[ch], ren_a[ch]], axis=0)
-        t = jnp.concatenate([tar_b[ch], tar[ch], tar_a[ch]], axis=0)
-        mr, mt = blur_rows(r, mid), blur_rows(t, mid)
-        er, et, ert = blur_rows(r * r, mid), blur_rows(t * t, mid), blur_rows(r * t, mid)
+    ren_s = [padded(ren, ren_b, ren_a, ch) for ch in range(channels)]
+    tar_s = [padded(tar, tar_b, tar_a, ch) for ch in range(channels)]
+    found = blur(ren_s + [x * x for x in ren_s] + [x * y for x, y in zip(ren_s, tar_s)], rows, cols)
+    fields = []
+    for ch in range(channels):
+        mr, er, ert = found[ch], found[channels + ch], found[2 * channels + ch]
+        mt, et = known[ch], known[channels + ch]
         a1 = 2.0 * mr * mt + 0.0001
         a2 = 2.0 * (ert - mr * mt) + 0.0009
         b1 = mr * mr + mt * mt + 0.0001
@@ -201,9 +215,51 @@
         d_mr = 2.0 * mt * (a2 - a1) * i1 * i2 - 2.0 * mr * s * (i1 - i2)
         d_er = -s * i2
         d_ert = 2.0 * a1 * i1 * i2
-        g0, g1, g2 = [blur_rows(jnp.where(inside, d, 0.0), rows) for d in (d_mr, d_er, d_ert)]
+        fields += [jnp.where(inside, d, 0.0) for d in (d_mr, d_er, d_ert)]
+    pulled = blur(fields, back, cols)
+    for ch in range(channels):
+        g0, g1, g2 = pulled[3 * ch : 3 * ch + 3]
         rc, tc = ren[ch], tar[ch]
         cot_ref[ch] = 1.6 * (rc - tc) - 0.2 * (g0 + 2.0 * rc * g1 + tc * g2)
+
+
+def parts_of(matrix):
+    out = []
+    rest = matrix.astype(np.float32)
+    for _ in range(3):
+        top = rest.astype(jnp.bfloat16)
+        out.append(top)
+        rest = rest - top.astype(np.float32)
+    return jnp.asarray(np.stack(out))
+
+
+def blur_tables(height, width):
+    m = np.arange(-RIM, RIM + 1)
+    taps = np.exp(-m * m / 4.5)
+    taps = taps / taps.sum()
+    side = HALO + (-HALO % SUB)
+    place = [height + i for i in range(HALO)] + list(range(height)) + [height + side + i for i in range(HALO)]
+    mid = height + HALO
+    tall = mid + (-mid % SUB)
+    rows = np.zeros((tall, height + 2 * side))
+    back = np.zeros((height, tall))
+    cols = np.zeros((width, width))
+    for k, tap in enumerate(taps):
+        for i in range(mid):
+            rows[i, place[i + k]] = tap
+        for i in range(height):
+            back[i, i + k] = tap
+        for i in range(width):
+            if 0 <= i + k - RIM < width:
+                cols[i + k - RIM, i] = tap
+
+    def stack(matrix):
+        p = parts_of(matrix)
+        none = jnp.zeros_like(p[0])
+        sides = [[p[i] if i + j < 3 else none for j in range(3)] for i in range(3)]
+        return jnp.concatenate([jnp.concatenate(side, axis=1) for side in sides], axis=0)
+
+    return stack(rows), stack(back), parts_of(cols)
 
 
 def spread(values, where, total):
@@ -228,9 +284,6 @@
         got[0:SUB] + got[SUB : 2 * SUB] + got[2 * SUB : 3 * SUB],
         got[24:25] + got[25:26] + got[26:27],
     )
-
-
-BLOCK = 16
 
 
 def backward_kernel(x_ref, idx_ref, seg_ref, cot_ref, basis, phi, out_ref, total, *buffers):
@@ -451,7 +504,6 @@
     size = lax.axis_size("dev")
     me = lax.axis_index("dev")
     pixels = tile * tile
-    chunks = slot_count // LANES
     wide = 2 * LANES
     basis, basis_back, phi = tables(tile, slot_count)
     sds = jax.ShapeDtypeStruct
@@ -467,6 +519,8 @@
     order = tile_lists.reshape(strip_tiles, SUB, list_len // SUB).transpose(0, 2, 1)
     order = order.reshape(strip_tiles * list_len // LANES, LANES)
     tar_b, tar_a = swap_edges(target)
+    rows, back, cols = blur_tables(tile, width)
+    known = call(target_kernel, sds((2 * channels, rows.shape[0] // 3, width), F32))(target, tar_b, tar_a, rows, cols)
 
     colour_tiles, coefs, segments = call(
         forward_kernel,
@@ -475,7 +529,7 @@
             sds((strip_tiles, 32, list_len), BF16),
             sds((strip_tiles, 5 * SUB, pixels), F32),
         ),
-        [pltpu.VMEM((chunks, SUB, LANES), F32), pltpu.VMEM((chunks, LANES), F32)],
+        [pltpu.VMEM((slot_count // wide * 32, wide), BF16)],
     )(received, order, basis)
     image = (
         colour_tiles.reshape(strip_tiles, channels, tile, tile).transpose(1, 2, 0, 3).reshape(channels, tile, width)
@@ -483,7 +537,7 @@
     ren_b, ren_a = swap_edges(image)
     edge = jnp.stack([jnp.where(me == 0, RIM, 0), jnp.where(me == size - 1, tile + RIM, tile + HALO)]).astype(jnp.int32)
     cot = call(ssim_kernel, sds((channels, tile, width), F32), smem=1)(
-        edge, image, target, ren_b, tar_b, ren_a, tar_a
+        edge, image, target, ren_b, tar_b, ren_a, tar_a, known, rows, back, cols
     )
     cot_tiles = (
         cot.reshape(channels, tile, strip_tiles, tile).transpose(2, 0, 1, 3).reshape(strip_tiles, channels, pixels)

time: 70.6 us -> 67.9 us (0.962)
  Pallas kernels: 34.7 us -> 31.9 us
  other arithmetic: 0.13 us -> 1.71 us
  waiting for transfers between devices: 4.37 us -> 2.87 us
  blocking collectives: 13.6 us -> 12.8 us
    pallas_call x5 -> x6, Pallas kernels: 34.7 us -> 31.9 us  [run(): pl.pallas_call(kernel, out_shape=out_shape, in_specs=specs, out_specs=jax...]
    select_n x2, other arithmetic: 0.03 us -> 0.95 us  [swap_edges(): return (jnp.where(odd, got_in, got_out), jnp.where(odd, got_out, got_in))]
    ppermute x2, waiting for transfers between devices: 0.88 us -> 0.01 us  [swap_edges(): got_in = lax.ppermute(jnp.where(odd, first, last), 'dev', inner)]
    all_to_all x1, blocking collectives: 13.6 us -> 12.8 us  [shards(): lax.all_to_all(slot_sums, 'dev', split_axis=0, concat_axis=0, tiled=True)]
  transfers between devices with their start and end apart: 5 -> 5, of which waited for: 2 -> 1; matrix products, arithmetic and copies ran while one was open for 2% -> 4% of each run, Pallas kernels for 15% -> 13%
where the time goes in v4:
time: 67.9 us; the launch traced here: 67.3 us
  Pallas kernels  31.9 us (47%)
  starting transfers between devices  13.8 us (20%)
  blocking collectives  12.8 us (19%)
  local copies, waits for them, and re-layouts  3.3 us (5%)
  waiting for transfers between devices  2.87 us (4%)
  other arithmetic  1.71 us (3%)
  between operations  0.94 us (1%)
    pallas_call x6, Pallas kernels, run(): pl.pallas_call(kernel, out_shape=out_shape, in_specs=specs, out_specs=jax...  31.9 us
    all_to_all x1, blocking collectives, shards(): lax.all_to_all(slot_sums, 'dev', split_axis=0, concat_axis=0, tiled=True)  12.8 us
    all_to_all x1, starting transfers between devices, shards(): lax.all_to_all(packed, 'dev', split_axis=0, concat_axis=0, tiled=True)  7.3 us
    ppermute x2, starting transfers between devices, swap_edges(): got_in = lax.ppermute(jnp.where(odd, first, last), 'dev', inner)  4.43 us
    all_to_all x1, waiting for transfers between devices, shards(): lax.all_to_all(packed, 'dev', split_axis=0, concat_axis=0, tiled=True)  2.86 us
    ppermute x2, starting transfers between devices, swap_edges(): got_out = lax.ppermute(jnp.where(odd, last, first), 'dev', outer)  2.07 us
  transfers between devices with their start and end apart: 5, of which 1 were waited for; matrix products, arithmetic and copies ran while one was open for 4% of the time, Pallas kernels for 13%

profile of v4, /device:TPU:0, one launch (start us, length us, event | category | flops | bytes accessed | tf_op | source)
XLA Modules:
  0.0 67.3 jit_solution(7886784935095024410)
XLA Ops:
  0.6 2.9 %shard_map.149 = f32[256,128]{1,0:T(8,128)} custom-call(s32[1,2048]{1,0:T(1,128)} %rows_ref.3, f32[2,2048]{1,0:T(2,128)} %centres.3, f32[2,2048]{1,0:T(2,128)} %conic.3, f32[1,2048]{1,0:T(1,128)} %rho.3, f32[1,2048]{1,0:T(1,128)} %opacity.3, f32[3,2048]{1,0:T(4,128)} %colors.1), custom_call_target="tpu_custom_call" | custom-call | tf_op jit(solution)/shard_map/pallas_call | solution.py:474
  3.5 0.0 copy-start.1
  3.5 7.3 %all-to-all-start = ((f32[32,8,128]{2,1,0:T(8,128)}), f32[32,8,128]{2,1,0:T(8,128)S(1)}, u32[]{:S(2)}, u32[]{:S(2)}) async-start(f32[32,8,128]{2,1,0:T(8,128)} %bitcast.21), calls=%async_computation | async-start | bytes 262144 | tf_op jit(solution)/shard_map/all_to_all | solution.py:517
  10.9 0.0 copy-done.1
  10.9 0.0 copy-start.13
  10.9 0.7 slice_select_fusion.2
  11.5 1.3 %collective-permute-start.3 = (f32[3,10,384]{2,1,0:T(8,128)}, f32[3,10,384]{2,1,0:T(8,128)}, u32[]{:S(2)}, u32[]{:S(2)}) collective-permute-start(f32[3,10,384]{2,1,0:T(8,128)} %get-tuple-element.12), channel_id=1, source_target_pairs={{1,2},{3,4},{5,6},{7,8},{9,10},{11,12},{13,14},{15,16},{17,18},{19... | collective-permute-start | bytes 138248 | tf_op jit(solution)/shard_map/ppermute | solution.py:495
  12.8 2.6 %collective-permute-start.2 = (f32[3,10,384]{2,1,0:T(8,128)}, f32[3,10,384]{2,1,0:T(8,128)}, u32[]{:S(2)}, u32[]{:S(2)}) collective-permute-start(f32[3,10,384]{2,1,0:T(8,128)} %get-tuple-element.13), channel_id=1, source_target_pairs={{0,1},{1,0},{2,3},{3,2},{4,5},{5,4},{6,7},{7,6},{8,9},{9,8},{10,11... | collective-permute-start | bytes 138248 | tf_op jit(solution)/shard_map/ppermute | solution.py:494
  15.4 0.0 copy-done.13
  15.4 0.1 reshape.26
  15.5 0.3 copy.19
  15.8 0.0 copy-start.7
  15.8 0.4 reshape.27.idx_ref
  16.1 0.1 pad_add_fusion.edge
  16.2 2.9 %all-to-all-done = f32[32,8,128]{2,1,0:T(8,128)S(1)} async-done(((f32[32,8,128]{2,1,0:T(8,128)}), f32[32,8,128]{2,1,0:T(8,128)S(1)}, u32[]{:S(2)}, u32[]{:S(2)}) %all-to-all-start) | async-done | bytes 131104 | tf_op jit(solution)/shard_map/all_to_all | solution.py:517
  19.1 0.0 copy-done.7
  19.1 7.6 %shard_map.150 = (f32[24,3,256]{2,1,0:T(4,128)S(1)}, bf16[24,32,512]{2,1,0:T(8,128)(2,1)S(1)}, f32[24,40,256]{2,1,0:T(8,128)S(1)}) custom-call(f32[256,128]{1,0:T(8,128)S(1)} %bitcast.16, s32[96,128]{1,0:T(8,128)S(1)} %reshape.27.idx_ref, bf16[32,640]{1,0:T(8,128)(2,1)S(1)} %copy-done.7), custom_call_target="tpu_custom_call" | custom-call | tf_op jit(solution)/shard_map/pallas_call | solution.py:474
  26.8 0.2 reshape.28
  27.0 0.2 copy.21
  27.2 0.0 copy-start
  27.2 0.2 reshape.29.ren
  27.4 0.0 copy-start.2
  27.4 0.8 %collective-permute-start.1 = (f32[3,10,384]{2,1,0:T(8,128)S(1)}, f32[3,10,384]{2,1,0:T(8,128)S(1)}, u32[]{:S(2)}, u32[]{:S(2)}) collective-permute-start(f32[3,10,384]{2,1,0:T(8,128)S(1)} %get-tuple-element.14), channel_id=1, source_target_pairs={{1,2},{3,4},{5,6},{7,8},{9,10},{11,12},{13,14},{15,16},{17,18},{19... | collective-permute-start | bytes 138248 | tf_op jit(solution)/shard_map/ppermute | solution.py:495
  28.2 0.0 copy-start.3
  28.2 1.9 %collective-permute-start = (f32[3,10,384]{2,1,0:T(8,128)S(1)}, f32[3,10,384]{2,1,0:T(8,128)S(1)}, u32[]{:S(2)}, u32[]{:S(2)}) collective-permute-start(f32[3,10,384]{2,1,0:T(8,128)S(1)} %get-tuple-element.15), channel_id=1, source_target_pairs={{0,1},{1,0},{2,3},{3,2},{4,5},{5,4},{6,7},{7,6},{8,9},{9,8},{10,11... | collective-permute-start | bytes 138248 | tf_op jit(solution)/shard_map/ppermute | solution.py:494
  30.1 0.0 collective-permute-done.3
  30.1 0.0 collective-permute-done.2
  30.1 0.9 %broadcast_select_fusion = (f32[3,10,384]{2,1,0:T(8,128)S(1)}, f32[3,10,384]{2,1,0:T(8,128)S(1)}) fusion(f32[3,10,384]{2,1,0:T(8,128)} %collective-permute-done.3, f32[3,10,384]{2,1,0:T(8,128)} %collective-permute-done.2, pred[]{:T(512)S(6)} %eq.15), kind=kLoop, calls=%fused_computation.4 | loop fusion | flops 23040 | bytes 184321 | tf_op jit(solution)/shard_map/jit(_where)/select_n | solution.py:496
  31.0 0.0 copy-done
  31.1 0.0 copy-done.3
  31.1 0.9 %shard_map.151.known = f32[6,32,384]{2,1,0:T(8,128)S(1)} custom-call(f32[3,16,384]{2,1,0:T(8,128)S(1)} %copy-done.1, f32[3,10,384]{2,1,0:T(8,128)S(1)} %get-tuple-element.9.tar_b, f32[3,10,384]{2,1,0:T(8,128)S(1)} %get-tuple-element.8.tar_a, bf16[96,144]{1,0:T(8,128)(2,1)S(1)} %copy-done.3, bf16[3,384,384]{2,1,0:T(8,128)(2,1)S(1)} %copy-done), custom_call_target="tpu_custom_call" | custom-call | tf_op jit(solution)/shard_map/pallas_call | solution.py:474
  32.0 0.0 collective-permute-done.1
  32.0 0.0 collective-permute-done
  32.0 0.0 copy-start.12
  32.1 0.0 copy-done.2
  32.1 0.7 copy-done.12
  32.7 3.0 %shard_map.152 = f32[3,16,384]{2,1,0:T(8,128)S(1)} custom-call(s32[2]{0:T(128)S(1)} %pad_add_fusion.edge, f32[3,16,384]{2,1,0:T(8,128)S(1)} %reshape.29.ren, f32[3,16,384]{2,1,0:T(8,128)S(1)} %copy-done.1, f32[3,10,384]{2,1,0:T(8,128)S(1)} %get-tuple-element.11.ren_b, f32[3,10,384]{2,1,0:T(8,128)S(1)} %get-tuple-element.9.tar_b, ...), custom_call_target="tpu_custom_call" | custom-call | tf_op jit(solution)/shard_map/pallas_call | solution.py:474
  35.8 0.2 reshape.30
  36.0 0.1 copy.24
  36.1 0.0 copy-start.4
  36.1 0.0 copy-start.8
  36.2 0.3 reshape.32.cot_ref
  36.5 0.6 copy-done.4
  37.0 0.0 copy-done.8
  37.0 16.2 %shard_map.153 = f32[256,128]{1,0:T(8,128)S(1)} custom-call(bf16[24,32,512]{2,1,0:T(8,128)(2,1)S(1)} %get-tuple-element.6.x_ref, s32[96,128]{1,0:T(8,128)S(1)} %reshape.27.idx_ref, f32[24,40,256]{2,1,0:T(8,128)S(1)} %get-tuple-element.7.seg_ref, f32[24,3,256]{2,1,0:T(4,128)S(1)} %reshape.32.cot_ref, bf16[64,256]{1,0:T(8,128)(2,1)S(1)} %copy-done.8, ...), custom_call_target="tpu_custom_call" | custom-call | tf_op jit(solution)/shard_map/pallas_call | solution.py:474
  53.2 0.0 copy-start.5
  53.2 0.0 copy-start.6
  53.2 0.0 copy-start.9
  53.3 0.0 copy-start.10
  53.3 0.0 copy-start.11
  53.3 12.8 %all_to_all.22 = f32[32,8,128]{2,1,0:T(8,128)S(1)} all-to-all(f32[32,8,128]{2,1,0:T(8,128)S(1)} %bitcast.15), channel_id=1, replica_groups=mesh['dev'=32] {'dev'}, dimensions={0} | all-to-all | bytes 262144 | tf_op jit(solution)/shard_map/all_to_all | solution.py:550
  66.0 0.0 copy-done.5
  66.0 0.0 copy-done.6
  66.0 0.0 copy-done.9
  66.1 0.0 copy-done.10
  66.1 0.0 copy-done.11
  66.1 1.2 %shard_map.154 = f32[9,2048]{1,0:T(8,128)} custom-call(f32[256,128]{1,0:T(8,128)S(1)} %bitcast.17, s32[1,2048]{1,0:T(1,128)S(1)} %copy-done.9, f32[2,2048]{1,0:T(2,128)S(1)} %copy-done.5, f32[2,2048]{1,0:T(2,128)S(1)} %copy-done.6, f32[1,2048]{1,0:T(1,128)S(1)} %copy-done.10, f32[1,2048]{1,0:T(1,128)S(1)} %copy-done.11), custom_call_target="tpu_custom_call" | custom-call | tf_op jit(solution)/shard_map/pallas_call | solution.py:474
  (3 shorter events, 0.0 us)
Async XLA Ops:
  3.5 7.3 %copy-start.1 = (f32[3,16,384]{2,1,0:T(8,128)S(1)}, f32[3,16,384]{2,1,0:T(8,128)}, u32[]{:S(2)}) copy-start(f32[3,16,384]{2,1,0:T(8,128)} %tar.3) | copy-start | bytes 221188
  3.5 15.5 %all-to-all-start = ((f32[32,8,128]{2,1,0:T(8,128)}), f32[32,8,128]{2,1,0:T(8,128)S(1)}, u32[]{:S(2)}, u32[]{:S(2)}) async-start(f32[32,8,128]{2,1,0:T(8,128)} %bitcast.21), calls=%async_computation | async-start | bytes 262144 | tf_op jit(solution)/shard_map/all_to_all | solution.py:517
  10.9 4.5 %copy-start.13 = (s32[24,512]{1,0:T(8,128)S(1)}, s32[24,512]{1,0:T(8,128)}, u32[]{:S(2)}) copy-start(s32[24,512]{1,0:T(8,128)} %param.14) | copy-start | bytes 147460
  11.5 18.6 %collective-permute-start.3 = (f32[3,10,384]{2,1,0:T(8,128)}, f32[3,10,384]{2,1,0:T(8,128)}, u32[]{:S(2)}, u32[]{:S(2)}) collective-permute-start(f32[3,10,384]{2,1,0:T(8,128)} %get-tuple-element.12), channel_id=1, source_target_pairs={{1,2},{3,4},{5,6},{7,8},{9,10},{11,12},{13,14},{15,16},{17,18},{19... | collective-permute-start | bytes 138248 | tf_op jit(solution)/shard_map/ppermute | solution.py:495
  12.8 17.3 %collective-permute-start.2 = (f32[3,10,384]{2,1,0:T(8,128)}, f32[3,10,384]{2,1,0:T(8,128)}, u32[]{:S(2)}, u32[]{:S(2)}) collective-permute-start(f32[3,10,384]{2,1,0:T(8,128)} %get-tuple-element.13), channel_id=1, source_target_pairs={{0,1},{1,0},{2,3},{3,2},{4,5},{5,4},{6,7},{7,6},{8,9},{9,8},{10,11... | collective-permute-start | bytes 138248 | tf_op jit(solution)/shard_map/ppermute | solution.py:494
  15.8 3.3 %copy-start.7 = (bf16[32,640]{1,0:T(8,128)(2,1)S(1)}, bf16[32,640]{1,0:T(8,128)(2,1)}, u32[]{:S(2)}) copy-start(bf16[32,640]{1,0:T(8,128)(2,1)} %constant.46.clone.basis) | copy-start | bytes 122884
  27.2 3.9 %copy-start = (bf16[3,384,384]{2,1,0:T(8,128)(2,1)S(1)}, bf16[3,384,384]{2,1,0:T(8,128)(2,1)}, u32[]{:S(2)}) copy-start(bf16[3,384,384]{2,1,0:T(8,128)(2,1)} %constant.51.clone.cols) | copy-start | bytes 2654212
  27.4 4.7 %copy-start.2 = (f32[3,16,384]{2,1,0:T(8,128)}, f32[3,16,384]{2,1,0:T(8,128)S(1)}, u32[]{:S(2)}) copy-start(f32[3,16,384]{2,1,0:T(8,128)S(1)} %reshape.29.ren) | copy-start | bytes 221188
  27.4 4.6 %collective-permute-start.1 = (f32[3,10,384]{2,1,0:T(8,128)S(1)}, f32[3,10,384]{2,1,0:T(8,128)S(1)}, u32[]{:S(2)}, u32[]{:S(2)}) collective-permute-start(f32[3,10,384]{2,1,0:T(8,128)S(1)} %get-tuple-element.14), channel_id=1, source_target_pairs={{1,2},{3,4},{5,6},{7,8},{9,10},{11,12},{13,14},{15,16},{17,18},{19... | collective-permute-start | bytes 138248 | tf_op jit(solution)/shard_map/ppermute | solution.py:495
  28.2 2.8 %copy-start.3 = (bf16[96,144]{1,0:T(8,128)(2,1)S(1)}, bf16[96,144]{1,0:T(8,128)(2,1)}, u32[]{:S(2)}) copy-start(bf16[96,144]{1,0:T(8,128)(2,1)} %constant.68.rows) | copy-start | bytes 82948
  28.2 3.8 %collective-permute-start = (f32[3,10,384]{2,1,0:T(8,128)S(1)}, f32[3,10,384]{2,1,0:T(8,128)S(1)}, u32[]{:S(2)}, u32[]{:S(2)}) collective-permute-start(f32[3,10,384]{2,1,0:T(8,128)S(1)} %get-tuple-element.15), channel_id=1, source_target_pairs={{0,1},{1,0},{2,3},{3,2},{4,5},{5,4},{6,7},{7,6},{8,9},{9,8},{10,11... | collective-permute-start | bytes 138248 | tf_op jit(solution)/shard_map/ppermute | solution.py:494
  32.0 0.7 %copy-start.12 = (bf16[48,96]{1,0:T(8,128)(2,1)S(1)}, bf16[48,96]{1,0:T(8,128)(2,1)}, u32[]{:S(2)}) copy-start(bf16[48,96]{1,0:T(8,128)(2,1)} %constant.78.back) | copy-start | bytes 27652
  36.1 0.9 %copy-start.4 = (bf16[512,128]{1,0:T(8,128)(2,1)S(1)}, bf16[512,128]{1,0:T(8,128)(2,1)}, u32[]{:S(2)}) copy-start(bf16[512,128]{1,0:T(8,128)(2,1)} %constant.48.clone.phi) | copy-start | bytes 393220
  36.1 0.9 %copy-start.8 = (bf16[64,256]{1,0:T(8,128)(2,1)S(1)}, bf16[64,256]{1,0:T(8,128)(2,1)}, u32[]{:S(2)}) copy-start(bf16[64,256]{1,0:T(8,128)(2,1)} %constant.47.clone.basis) | copy-start | bytes 98308
  53.2 12.8 %copy-start.5 = (f32[2,2048]{1,0:T(2,128)S(1)}, f32[2,2048]{1,0:T(2,128)}, u32[]{:S(2)}) copy-start(f32[2,2048]{1,0:T(2,128)} %centres.3) | copy-start | bytes 49156
  53.2 12.8 %copy-start.6 = (f32[2,2048]{1,0:T(2,128)S(1)}, f32[2,2048]{1,0:T(2,128)}, u32[]{:S(2)}) copy-start(f32[2,2048]{1,0:T(2,128)} %conic.3) | copy-start | bytes 49156
  53.2 12.8 %copy-start.9 = (s32[1,2048]{1,0:T(1,128)S(1)}, s32[1,2048]{1,0:T(1,128)}, u32[]{:S(2)}) copy-start(s32[1,2048]{1,0:T(1,128)} %rows_ref.3) | copy-start | bytes 24580
  53.3 12.8 %copy-start.10 = (f32[1,2048]{1,0:T(1,128)S(1)}, f32[1,2048]{1,0:T(1,128)}, u32[]{:S(2)}) copy-start(f32[1,2048]{1,0:T(1,128)} %rho.3) | copy-start | bytes 24580
  53.3 12.8 %copy-start.11 = (f32[1,2048]{1,0:T(1,128)S(1)}, f32[1,2048]{1,0:T(1,128)}, u32[]{:S(2)}) copy-start(f32[1,2048]{1,0:T(1,128)} %opacity.3) | copy-start | bytes 24580

commit v5 on v4

--- a/solution.py
+++ b/solution.py
@@ -43,28 +43,32 @@
     return lax.broadcasted_iota(jnp.int32, shape, len(shape) - 2)
 
 
-def pick(table, last, where):
-    chunks = table.shape[0]
-    lane = jnp.bitwise_and(where, LANES - 1)
-    chunk = jnp.right_shift(where, 7)
-    lane8 = jnp.broadcast_to(lane, (SUB, LANES))
-    chunk8 = jnp.broadcast_to(chunk, (SUB, LANES))
-    value = jnp.zeros((SUB, LANES), F32)
-    for c in range(chunks):
-        got = jnp.take_along_axis(table[c], lane8, axis=1, mode="promise_in_bounds")
-        value = jnp.where(chunk8 == c, got, value)
-    total = jnp.zeros((SUB, LANES), F32)
-    for c in range(0, chunks, SUB):
-        got = jnp.take_along_axis(last[c : c + SUB], lane8, axis=1, mode="promise_in_bounds")
-        total = total + jnp.where(chunk8 == rows_of((SUB, LANES)) + c, got, 0.0)
-    return value, jnp.sum(total, axis=0, keepdims=True)
-
-
-def pack_kernel(rows_ref, centres, conic, rho, opacity, colors, out_ref, table, last):
-    chunks = table.shape[0]
+def fill(table, c, eight, ninth):
+    p = [v.astype(F32) for v in pieces(eight, 3)]
+    n = [v.astype(F32) for v in pieces(jnp.broadcast_to(ninth, eight.shape), 3)]
+    r = rows_of(eight.shape)
+    tail = jnp.where(r == 0, n[0], jnp.where(r == 1, n[1], jnp.where(r == 2, n[2], 0.0)))
+    table[c * 32 : (c + 1) * 32] = jnp.concatenate(p + [tail], axis=0).astype(BF16)
+
+
+def choose(table, idx, none):
+    wide = table.shape[1]
+    low = jnp.broadcast_to(jnp.bitwise_and(idx, wide - 1), (wide, wide))
+    hot = (low == rows_of((wide, wide))).astype(F32).astype(BF16)
+    got = dot(table[...], hot, NN)
+    chunk = jnp.where(idx < 0, -1, jnp.right_shift(idx, wide.bit_length() - 1))
+    chunk = jnp.broadcast_to(chunk, (32, wide))
+    x = none
+    for c in range(table.shape[0] // 32):
+        x = jnp.where(chunk == c, got[c * 32 : (c + 1) * 32], x)
+    return x
+
+
+def pack_kernel(rows_ref, centres, conic, rho, opacity, colors, out_ref, table):
+    wide = table.shape[1]
     s = -0.5 * LOG2E
-    for c in range(chunks):
-        at = slice(c * LANES, (c + 1) * LANES)
+    for c in range(table.shape[0] // 32):
+        at = slice(c * wide, (c + 1) * wide)
         x, y = centres[0:1, at], centres[1:2, at]
         a, d = conic[0:1, at], conic[1:2, at]
         b = rho[0:1, at] * jnp.sqrt(a * d)
@@ -78,16 +82,19 @@
             colors[0:1, at],
             colors[1:2, at],
         ]
-        table[c] = jnp.concatenate(rows, axis=0)
-        last[c : c + 1] = colors[2:3, at]
+        fill(table, c, jnp.concatenate(rows, axis=0), colors[2:3, at])
     half = LANES // 2
     left = lanes_of((SUB, LANES)) < half
-    for g in range(rows_ref.shape[1] // LANES):
-        where = jnp.maximum(rows_ref[0:1, g * LANES : (g + 1) * LANES], 0)
-        value, ninth = pick(table, last, where)
-        ninth = jnp.broadcast_to(ninth, (SUB, LANES))
-        out_ref[2 * g * SUB : (2 * g + 1) * SUB] = jnp.where(left, value, pltpu.roll(ninth, half, 1))
-        out_ref[(2 * g + 1) * SUB : (2 * g + 2) * SUB] = jnp.where(left, pltpu.roll(value, half, 1), ninth)
+    none = jnp.zeros((32, wide), F32)
+    for g in range(rows_ref.shape[1] // wide):
+        x = choose(table, rows_ref[0:1, g * wide : (g + 1) * wide], none)
+        eight = x[0:SUB] + x[SUB : 2 * SUB] + x[2 * SUB : 3 * SUB]
+        ninth = jnp.broadcast_to(x[24:25] + x[25:26] + x[26:27], (SUB, wide))
+        for j in range(wide // LANES):
+            e, n = [v[:, j * LANES : (j + 1) * LANES] for v in (eight, ninth)]
+            at = (g * (wide // LANES) + j) * 2 * SUB
+            out_ref[at : at + SUB] = jnp.where(left, e, pltpu.roll(n, half, 1))
+            out_ref[at + SUB : at + 2 * SUB] = jnp.where(left, pltpu.roll(e, half, 1), n)
 
 
 def part_of(count, most):
@@ -104,7 +111,6 @@
     wide = table.shape[1]
     half = LANES // 2
     left = lanes_of((SUB, LANES)) < half
-    r = rows_of((SUB, wide))
     for c in range(table.shape[0] // 32):
         eights, ninths = [], []
         for j in range(wide // LANES):
@@ -112,25 +118,16 @@
             a, b = recv[at : at + SUB], recv[at + SUB : at + 2 * SUB]
             eights.append(jnp.where(left, a, pltpu.roll(b, half, 1)))
             n = jnp.where(left, pltpu.roll(a, half, 1), b)
-            ninths.append(jnp.broadcast_to(n[0:1], (SUB, LANES)))
-        p = [v.astype(F32) for v in pieces(jnp.concatenate(eights, axis=1), 3)]
-        n = [v.astype(F32) for v in pieces(jnp.concatenate(ninths, axis=1), 3)]
-        tail = jnp.where(r == 0, n[0], jnp.where(r == 1, n[1], jnp.where(r == 2, n[2], 0.0)))
-        table[c * 32 : (c + 1) * 32] = jnp.concatenate(p + [tail], axis=0).astype(BF16)
+            ninths.append(n[0:1])
+        fill(table, c, jnp.concatenate(eights, axis=1), jnp.concatenate(ninths, axis=1))
+    none = jnp.where(rows_of((32, wide)) == 0, -1000.0, 0.0)
     row = rows_of((SUB, pixels))
 
     def fetch(t):
         per = wide // LANES
         for q in range(0, groups, per):
             idx = jnp.concatenate([idx_ref[pl.ds(t * groups + q + j, 1), :] for j in range(per)], axis=1)
-            low = jnp.broadcast_to(jnp.bitwise_and(idx, wide - 1), (wide, wide))
-            hot = (low == rows_of((wide, wide))).astype(F32).astype(BF16)
-            got = dot(table[...], hot, NN)
-            chunk = jnp.where(idx < 0, -1, jnp.right_shift(idx, wide.bit_length() - 1))
-            chunk = jnp.broadcast_to(chunk, (32, wide))
-            x = jnp.where(jnp.logical_and(chunk < 0, rows_of((32, wide)) == 0), -1000.0, 0.0)
-            for c in range(table.shape[0] // 32):
-                x = jnp.where(chunk == c, got[c * 32 : (c + 1) * 32], x)
+            x = choose(table, idx, none)
             x_ref[t, :, q * LANES : (q + per) * LANES] = x.astype(BF16)
 
     def composite(t):
@@ -176,7 +173,7 @@
     height = rows.shape[0] // 3
     done = []
     for x in images:
-        got = dot(rows[...], jnp.concatenate(pieces(x, 3), axis=0), NN)
+        got = dot(rows, jnp.concatenate(pieces(x, 3), axis=0), NN)
         done.append(got[:height] + got[height : 2 * height] + got[2 * height :])
     stacked = jnp.concatenate(done, axis=0)
     out = exact(pieces(stacked, 3), [cols[k] for k in range(3)])
@@ -188,16 +185,20 @@
     return jnp.concatenate([own[ch], before[ch], fill, after[ch], fill], axis=0)
 
 
-def target_kernel(tar, tar_b, tar_a, rows, cols, out_ref):
+def target_kernel(tar, tar_b, tar_a, rows_back, cols, out_ref):
+    rows = rows_back[: 3 * out_ref.shape[1]]
     channels = tar.shape[0]
     images = [padded(tar, tar_b, tar_a, ch) for ch in range(channels)]
     for i, v in enumerate(blur(images + [x * x for x in images], rows, cols)):
         out_ref[i] = v
 
 
-def ssim_kernel(edge, ren, tar, ren_b, tar_b, ren_a, tar_a, known, rows, back, cols, cot_ref):
+def ssim_kernel(edge, ren, tar, ren_b, tar_b, ren_a, tar_a, known, rows_back, cols, cot_ref):
     channels, height, width = ren.shape
-    r_at = rows_of((rows.shape[0] // 3, width))
+    tall = known.shape[1]
+    rows = rows_back[: 3 * tall]
+    back = rows_back[3 * tall :, : 3 * tall]
+    r_at = rows_of((tall, width))
     inside = jnp.logical_and(r_at >= edge[0], r_at < edge[1])
     ren_s = [padded(ren, ren_b, ren_a, ch) for ch in range(channels)]
     tar_s = [padded(tar, tar_b, tar_a, ch) for ch in range(channels)]
@@ -259,7 +260,9 @@
         sides = [[p[i] if i + j < 3 else none for j in range(3)] for i in range(3)]
         return jnp.concatenate([jnp.concatenate(side, axis=1) for side in sides], axis=0)
 
-    return stack(rows), stack(back), parts_of(cols)
+    down, up = stack(rows), stack(back)
+    up = jnp.pad(up, ((0, 0), (0, down.shape[1] - up.shape[1])))
+    return jnp.concatenate([down, up], axis=0), parts_of(cols)
 
 
 def spread(values, where, total):
@@ -286,7 +289,7 @@
     )
 
 
-def backward_kernel(x_ref, idx_ref, seg_ref, cot_ref, basis, phi, out_ref, total, *buffers):
+def backward_kernel(x_ref, idx_ref, seg_ref, cot_ref, ahead, out_ref, total, phi, *buffers):
     tiles, pixels = cot_ref.shape[0], cot_ref.shape[2]
     count = x_ref.shape[2]
     groups = count // LANES
@@ -297,6 +300,18 @@
     each = 3
     columns = total.shape[1] // 2
     field = jnp.bitwise_and(lanes_of((SUB, LANES)), BLOCK - 1)
+    basis = jnp.concatenate([ahead[:, :pixels], jnp.zeros((32, pixels), BF16)], axis=0)
+    side = int(pixels**0.5)
+    kind = jnp.bitwise_and(lanes_of((pixels, LANES)), BLOCK - 1)
+    spot = rows_of((pixels, LANES))
+    down = jnp.right_shift(spot, side.bit_length() - 1)
+    u = (spot - down * side).astype(F32) - (side - 1) / 2.0
+    v = down.astype(F32) - (side - 1) / 2.0
+    six = jnp.zeros((pixels, LANES), F32)
+    for i, f in enumerate((jnp.ones_like(u), u, v, u * u, u * v, v * v)):
+        six = jnp.where(kind == i, f, six)
+    phi[:pixels] = six.astype(BF16)
+    phi[pixels:] = six.astype(BF16)
     moment = jnp.bitwise_and(lanes_of((count, LANES)), BLOCK - 1) < 6
     block = jnp.right_shift(lanes_of((LANES, LANES)), BLOCK.bit_length() - 1)
 
@@ -310,7 +325,7 @@
             return [body, body, body, jnp.where(row < 3, v[2], 0.0)]
 
         rhs = jnp.concatenate(place(hi) + place(lo), axis=0).astype(BF16)
-        rhs = jnp.concatenate([basis[...], rhs], axis=1)
+        rhs = jnp.concatenate([basis, rhs], axis=1)
         trans = seg_ref[t, 0:SUB]
         rest = trans * (cot[0] * seg_ref[t, 2 * SUB : 3 * SUB] + cot[1] * seg_ref[t, 3 * SUB : 4 * SUB] + cot[2] * seg_ref[t, 4 * SUB : 5 * SUB])
         for by in (1, 2, 4):
@@ -432,28 +447,19 @@
             out_ref[i : i + 1, at] = v
 
 
-def tables(tile, slots):
+def tables(tile):
     pixels = tile * tile
-    wide = 2 * LANES
     p = np.arange(pixels)
     v = (p // tile) - (tile - 1) / 2.0
     u = (p % tile) - (tile - 1) / 2.0
     six = np.stack([np.ones(pixels), u, v, u * u, u * v, v * v])
     ahead = np.zeros((32, pixels + 3 * LANES), np.float32)
-    back = np.zeros((64, pixels), np.float32)
     for k in range(3):
         ahead[8 * k : 8 * k + 6, :pixels] = six
-        back[8 * k : 8 * k + 6, :pixels] = six
         ahead[8 * k + 6, pixels : pixels + LANES] = 1.0
         ahead[8 * k + 7, pixels + LANES : pixels + 2 * LANES] = 1.0
         ahead[24 + k, pixels + 2 * LANES :] = 1.0
-    phi = np.zeros((2 * pixels, LANES), np.float32)
-    for lane in range(LANES):
-        field = lane % BLOCK
-        if field < 6:
-            phi[:pixels, lane] = six[field]
-            phi[pixels:, lane] = six[field]
-    return jnp.asarray(ahead, BF16), jnp.asarray(back, BF16), jnp.asarray(phi, BF16)
+    return jnp.asarray(ahead, BF16)
 
 
 def back_scratch(list_len, pixels, slots, par):
@@ -463,7 +469,7 @@
         pltpu.VMEM((list_len, LANES), F32),
         pltpu.VMEM((list_len, 2 * columns), BF16),
     ]
-    return [pltpu.VMEM((2 * LANES, 2 * columns), F32)] + one * par
+    return [pltpu.VMEM((2 * LANES, 2 * columns), F32), pltpu.VMEM((2 * pixels, LANES), BF16)] + one * par
 
 
 def call(kernel, out_shape, scratch=(), smem=0, mib=48):
@@ -505,13 +511,13 @@
     me = lax.axis_index("dev")
     pixels = tile * tile
     wide = 2 * LANES
-    basis, basis_back, phi = tables(tile, slot_count)
+    basis = tables(tile)
     sds = jax.ShapeDtypeStruct
 
     packed = call(
         pack_kernel,
         sds((size * SUB, LANES), F32),
-        [pltpu.VMEM((owned_count // LANES, SUB, LANES), F32), pltpu.VMEM((owned_count // LANES, LANES), F32)],
+        [pltpu.VMEM((owned_count // wide * 32, wide), BF16)],
         mib=63,
     )(send_rows, centres, conic, rho, opacity, colors)
     received = lax.all_to_all(packed, "dev", split_axis=0, concat_axis=0, tiled=True)
@@ -519,8 +525,9 @@
     order = tile_lists.reshape(strip_tiles, SUB, list_len // SUB).transpose(0, 2, 1)
     order = order.reshape(strip_tiles * list_len // LANES, LANES)
     tar_b, tar_a = swap_edges(target)
-    rows, back, cols = blur_tables(tile, width)
-    known = call(target_kernel, sds((2 * channels, rows.shape[0] // 3, width), F32))(target, tar_b, tar_a, rows, cols)
+    rows_back, cols = blur_tables(tile, width)
+    tall = rows_back.shape[0] // 3 - tile
+    known = call(target_kernel, sds((2 * channels, tall, width), F32))(target, tar_b, tar_a, rows_back, cols)
 
     colour_tiles, coefs, segments = call(
         forward_kernel,
@@ -537,7 +544,7 @@
     ren_b, ren_a = swap_edges(image)
     edge = jnp.stack([jnp.where(me == 0, RIM, 0), jnp.where(me == size - 1, tile + RIM, tile + HALO)]).astype(jnp.int32)
     cot = call(ssim_kernel, sds((channels, tile, width), F32), smem=1)(
-        edge, image, target, ren_b, tar_b, ren_a, tar_a, known, rows, back, cols
+        edge, image, target, ren_b, tar_b, ren_a, tar_a, known, rows_back, cols
     )
     cot_tiles = (
         cot.reshape(channels, tile, strip_tiles, tile).transpose(2, 0, 1, 3).reshape(strip_tiles, channels, pixels)
@@ -546,7 +553,7 @@
         backward_kernel,
         sds((size * SUB, LANES), F32),
         back_scratch(list_len, pixels, slot_count, part_of(strip_tiles, 6)),
-    )(coefs, order, segments, cot_tiles, basis_back, phi)
+    )(coefs, order, segments, cot_tiles, basis)
     returned = lax.all_to_all(slot_sums, "dev", split_axis=0, concat_axis=0, tiled=True)
     grads = call(
         home_kernel,

time: 67.9 us -> 65.7 us (0.968)
  local copies, waits for them, and re-layouts: 3.3 us -> 2.05 us
  Pallas kernels: 31.9 us -> 31.2 us
    unnamed x28 -> x22, local copies, waits for them, and re-layouts: 1.32 us -> 0.07 us
    pallas_call x6, Pallas kernels: 31.9 us -> 31.2 us  [run(): pl.pallas_call(kernel, out_shape=out_shape, in_specs=specs, out_specs=jax...]
  transfers between devices with their start and end apart: 5 -> 5, of which waited for: 1 -> 1; matrix products, arithmetic and copies ran while one was open for 4% -> 5% of each run, Pallas kernels for 13% -> 13%
where the time goes in v5:
time: 65.7 us; the launch traced here: 65.3 us
  Pallas kernels  31.2 us (47%)
  starting transfers between devices  13.8 us (21%)
  blocking collectives  12.8 us (19%)
  waiting for transfers between devices  2.87 us (4%)
  local copies, waits for them, and re-layouts  2.05 us (3%)
  other arithmetic  1.72 us (3%)
  between operations  0.92 us (1%)
    pallas_call x6, Pallas kernels, run(): pl.pallas_call(kernel, out_shape=out_shape, in_specs=specs, out_specs=jax...  31.2 us
    all_to_all x1, blocking collectives, shards(): lax.all_to_all(slot_sums, 'dev', split_axis=0, concat_axis=0, tiled=True)  12.8 us
    all_to_all x1, starting transfers between devices, shards(): lax.all_to_all(packed, 'dev', split_axis=0, concat_axis=0, tiled=True)  7.3 us
    ppermute x2, starting transfers between devices, swap_edges(): got_in = lax.ppermute(jnp.where(odd, first, last), 'dev', inner)  4.4 us
    all_to_all x1, waiting for transfers between devices, shards(): lax.all_to_all(packed, 'dev', split_axis=0, concat_axis=0, tiled=True)  2.86 us
    ppermute x2, starting transfers between devices, swap_edges(): got_out = lax.ppermute(jnp.where(odd, last, first), 'dev', outer)  2.09 us
  transfers between devices with their start and end apart: 5, of which 1 were waited for; matrix products, arithmetic and copies ran while one was open for 5% of the time, Pallas kernels for 13%

profile of v5, /device:TPU:0, one launch (start us, length us, event | category | flops | bytes accessed | tf_op | source)
XLA Modules:
  0.0 65.3 jit_solution(14076380943548671361)
XLA Ops:
  0.6 2.2 %shard_map.131 = f32[256,128]{1,0:T(8,128)} custom-call(s32[1,2048]{1,0:T(1,128)} %rows_ref.3, f32[2,2048]{1,0:T(2,128)} %centres.3, f32[2,2048]{1,0:T(2,128)} %conic.3, f32[1,2048]{1,0:T(1,128)} %rho.3, f32[1,2048]{1,0:T(1,128)} %opacity.3, f32[3,2048]{1,0:T(4,128)} %colors.1), custom_call_target="tpu_custom_call" | custom-call | tf_op jit(solution)/shard_map/pallas_call | solution.py:480
  2.8 0.0 copy-start.1
  2.8 7.3 %all-to-all-start = ((f32[32,8,128]{2,1,0:T(8,128)}), f32[32,8,128]{2,1,0:T(8,128)S(1)}, u32[]{:S(2)}, u32[]{:S(2)}) async-start(f32[32,8,128]{2,1,0:T(8,128)} %bitcast.21), calls=%async_computation | async-start | bytes 262144 | tf_op jit(solution)/shard_map/all_to_all | solution.py:523
  10.1 0.0 copy-done.1
  10.1 0.0 copy-start.10
  10.1 0.7 %slice_select_fusion.2 = (f32[3,10,384]{2,1,0:T(8,128)}, f32[3,10,384]{2,1,0:T(8,128)}) fusion(f32[3,16,384]{2,1,0:T(8,128)S(1)} %copy-done.1, pred[]{:T(512)S(6)} %eq.15), kind=kLoop, calls=%fused_computation.2 | loop fusion | flops 23040 | bytes 184321 | tf_op jit(solution)/shard_map/jit(_where)/select_n | solution.py:501
  10.8 1.3 %collective-permute-start.3 = (f32[3,10,384]{2,1,0:T(8,128)}, f32[3,10,384]{2,1,0:T(8,128)}, u32[]{:S(2)}, u32[]{:S(2)}) collective-permute-start(f32[3,10,384]{2,1,0:T(8,128)} %get-tuple-element.12), channel_id=1, source_target_pairs={{1,2},{3,4},{5,6},{7,8},{9,10},{11,12},{13,14},{15,16},{17,18},{19... | collective-permute-start | bytes 138248 | tf_op jit(solution)/shard_map/ppermute | solution.py:501
  12.1 2.6 %collective-permute-start.2 = (f32[3,10,384]{2,1,0:T(8,128)}, f32[3,10,384]{2,1,0:T(8,128)}, u32[]{:S(2)}, u32[]{:S(2)}) collective-permute-start(f32[3,10,384]{2,1,0:T(8,128)} %get-tuple-element.13), channel_id=1, source_target_pairs={{0,1},{1,0},{2,3},{3,2},{4,5},{5,4},{6,7},{7,6},{8,9},{9,8},{10,11... | collective-permute-start | bytes 138248 | tf_op jit(solution)/shard_map/ppermute | solution.py:500
  14.7 0.0 copy-done.10
  14.7 0.1 reshape.26
  14.8 0.3 copy.17
  15.0 0.0 copy-start.4
  15.1 0.4 reshape.27.idx_ref
  15.4 0.1 pad_add_fusion.edge
  15.5 2.9 %all-to-all-done = f32[32,8,128]{2,1,0:T(8,128)S(1)} async-done(((f32[32,8,128]{2,1,0:T(8,128)}), f32[32,8,128]{2,1,0:T(8,128)S(1)}, u32[]{:S(2)}, u32[]{:S(2)}) %all-to-all-start) | async-done | bytes 131104 | tf_op jit(solution)/shard_map/all_to_all | solution.py:523
  18.4 0.0 copy-done.4
  18.4 7.7 %shard_map.132 = (f32[24,3,256]{2,1,0:T(4,128)S(1)}, bf16[24,32,512]{2,1,0:T(8,128)(2,1)S(1)}, f32[24,40,256]{2,1,0:T(8,128)S(1)}) custom-call(f32[256,128]{1,0:T(8,128)S(1)} %bitcast.16, s32[96,128]{1,0:T(8,128)S(1)} %reshape.27.idx_ref, bf16[32,640]{1,0:T(8,128)(2,1)S(1)} %copy-done.4), custom_call_target="tpu_custom_call" | custom-call | tf_op jit(solution)/shard_map/pallas_call | solution.py:480
  26.0 0.2 reshape.28
  26.3 0.2 copy.19
  26.5 0.0 copy-start
  26.5 0.2 reshape.29.ren
  26.7 0.0 copy-start.2
  26.7 0.8 %collective-permute-start.1 = (f32[3,10,384]{2,1,0:T(8,128)S(1)}, f32[3,10,384]{2,1,0:T(8,128)S(1)}, u32[]{:S(2)}, u32[]{:S(2)}) collective-permute-start(f32[3,10,384]{2,1,0:T(8,128)S(1)} %get-tuple-element.14), channel_id=1, source_target_pairs={{1,2},{3,4},{5,6},{7,8},{9,10},{11,12},{13,14},{15,16},{17,18},{19... | collective-permute-start | bytes 138248 | tf_op jit(solution)/shard_map/ppermute | solution.py:501
  27.5 0.0 copy-start.3
  27.5 1.8 %collective-permute-start = (f32[3,10,384]{2,1,0:T(8,128)S(1)}, f32[3,10,384]{2,1,0:T(8,128)S(1)}, u32[]{:S(2)}, u32[]{:S(2)}) collective-permute-start(f32[3,10,384]{2,1,0:T(8,128)S(1)} %get-tuple-element.15), channel_id=1, source_target_pairs={{0,1},{1,0},{2,3},{3,2},{4,5},{5,4},{6,7},{7,6},{8,9},{9,8},{10,11... | collective-permute-start | bytes 138248 | tf_op jit(solution)/shard_map/ppermute | solution.py:500
  29.4 0.0 collective-permute-done.3
  29.4 0.0 collective-permute-done.2
  29.4 0.9 %broadcast_select_fusion = (f32[3,10,384]{2,1,0:T(8,128)S(1)}, f32[3,10,384]{2,1,0:T(8,128)S(1)}) fusion(f32[3,10,384]{2,1,0:T(8,128)} %collective-permute-done.3, f32[3,10,384]{2,1,0:T(8,128)} %collective-permute-done.2, pred[]{:T(512)S(6)} %eq.15), kind=kLoop, calls=%fused_computation.4 | loop fusion | flops 23040 | bytes 184321 | tf_op jit(solution)/shard_map/jit(_where)/select_n | solution.py:502
  30.3 0.0 copy-done
  30.3 0.0 copy-done.3
  30.3 0.9 %shard_map.133.known = f32[6,32,384]{2,1,0:T(8,128)S(1)} custom-call(f32[3,16,384]{2,1,0:T(8,128)S(1)} %copy-done.1, f32[3,10,384]{2,1,0:T(8,128)S(1)} %get-tuple-element.9.tar_b, f32[3,10,384]{2,1,0:T(8,128)S(1)} %get-tuple-element.8.tar_a, bf16[144,144]{1,0:T(8,128)(2,1)S(1)} %copy-done.3, bf16[3,384,384]{2,1,0:T(8,128)(2,1)S(1)} %copy-done), custom_call_target="tpu_custom_call" | custom-call | tf_op jit(solution)/shard_map/pallas_call | solution.py:480
  31.3 0.0 collective-permute-done.1
  31.3 0.0 collective-permute-done
  31.3 0.0 copy-done.2
  31.3 3.0 %shard_map.134 = f32[3,16,384]{2,1,0:T(8,128)S(1)} custom-call(s32[2]{0:T(128)S(1)} %pad_add_fusion.edge, f32[3,16,384]{2,1,0:T(8,128)S(1)} %reshape.29.ren, f32[3,16,384]{2,1,0:T(8,128)S(1)} %copy-done.1, f32[3,10,384]{2,1,0:T(8,128)S(1)} %get-tuple-element.11.ren_b, f32[3,10,384]{2,1,0:T(8,128)S(1)} %get-tuple-element.9.tar_b, ...), custom_call_target="tpu_custom_call" | custom-call | tf_op jit(solution)/shard_map/pallas_call | solution.py:480
  34.4 0.2 reshape.30
  34.6 0.1 copy.22
  34.7 0.3 reshape.32.cot_ref
  35.0 16.1 %shard_map.135 = f32[256,128]{1,0:T(8,128)S(1)} custom-call(bf16[24,32,512]{2,1,0:T(8,128)(2,1)S(1)} %get-tuple-element.6.x_ref, s32[96,128]{1,0:T(8,128)S(1)} %reshape.27.idx_ref, f32[24,40,256]{2,1,0:T(8,128)S(1)} %get-tuple-element.7.seg_ref, f32[24,3,256]{2,1,0:T(4,128)S(1)} %reshape.32.cot_ref, bf16[32,640]{1,0:T(8,128)(2,1)S(1)} %copy-done.4), custom_call_target="tpu_custom_call" | custom-call | tf_op jit(solution)/shard_map/pallas_call | solution.py:480
  51.2 0.0 copy-start.5
  51.2 0.0 copy-start.6
  51.2 0.0 copy-start.7
  51.2 0.0 copy-start.8
  51.2 0.0 copy-start.9
  51.2 12.8 %all_to_all.22 = f32[32,8,128]{2,1,0:T(8,128)S(1)} all-to-all(f32[32,8,128]{2,1,0:T(8,128)S(1)} %bitcast.15), channel_id=1, replica_groups=mesh['dev'=32] {'dev'}, dimensions={0} | all-to-all | bytes 262144 | tf_op jit(solution)/shard_map/all_to_all | solution.py:557
  64.0 0.0 copy-done.5
  64.0 0.0 copy-done.6
  64.0 0.0 copy-done.7
  64.0 0.0 copy-done.8
  64.0 0.0 copy-done.9
  64.0 1.2 %shard_map.136 = f32[9,2048]{1,0:T(8,128)} custom-call(f32[256,128]{1,0:T(8,128)S(1)} %bitcast.17, s32[1,2048]{1,0:T(1,128)S(1)} %copy-done.7, f32[2,2048]{1,0:T(2,128)S(1)} %copy-done.5, f32[2,2048]{1,0:T(2,128)S(1)} %copy-done.6, f32[1,2048]{1,0:T(1,128)S(1)} %copy-done.8, f32[1,2048]{1,0:T(1,128)S(1)} %copy-done.9), custom_call_target="tpu_custom_call" | custom-call | tf_op jit(solution)/shard_map/pallas_call | solution.py:480
  (3 shorter events, 0.0 us)
Async XLA Ops:
  2.8 7.3 %copy-start.1 = (f32[3,16,384]{2,1,0:T(8,128)S(1)}, f32[3,16,384]{2,1,0:T(8,128)}, u32[]{:S(2)}) copy-start(f32[3,16,384]{2,1,0:T(8,128)} %tar.3) | copy-start | bytes 221188
  2.8 15.6 %all-to-all-start = ((f32[32,8,128]{2,1,0:T(8,128)}), f32[32,8,128]{2,1,0:T(8,128)S(1)}, u32[]{:S(2)}, u32[]{:S(2)}) async-start(f32[32,8,128]{2,1,0:T(8,128)} %bitcast.21), calls=%async_computation | async-start | bytes 262144 | tf_op jit(solution)/shard_map/all_to_all | solution.py:523
  10.1 4.5 %copy-start.10 = (s32[24,512]{1,0:T(8,128)S(1)}, s32[24,512]{1,0:T(8,128)}, u32[]{:S(2)}) copy-start(s32[24,512]{1,0:T(8,128)} %param.12) | copy-start | bytes 147460
  10.8 18.5 %collective-permute-start.3 = (f32[3,10,384]{2,1,0:T(8,128)}, f32[3,10,384]{2,1,0:T(8,128)}, u32[]{:S(2)}, u32[]{:S(2)}) collective-permute-start(f32[3,10,384]{2,1,0:T(8,128)} %get-tuple-element.12), channel_id=1, source_target_pairs={{1,2},{3,4},{5,6},{7,8},{9,10},{11,12},{13,14},{15,16},{17,18},{19... | collective-permute-start | bytes 138248 | tf_op jit(solution)/shard_map/ppermute | solution.py:501
  12.1 17.3 %collective-permute-start.2 = (f32[3,10,384]{2,1,0:T(8,128)}, f32[3,10,384]{2,1,0:T(8,128)}, u32[]{:S(2)}, u32[]{:S(2)}) collective-permute-start(f32[3,10,384]{2,1,0:T(8,128)} %get-tuple-element.13), channel_id=1, source_target_pairs={{0,1},{1,0},{2,3},{3,2},{4,5},{5,4},{6,7},{7,6},{8,9},{9,8},{10,11... | collective-permute-start | bytes 138248 | tf_op jit(solution)/shard_map/ppermute | solution.py:500
  15.0 3.3 %copy-start.4 = (bf16[32,640]{1,0:T(8,128)(2,1)S(1)}, bf16[32,640]{1,0:T(8,128)(2,1)}, u32[]{:S(2)}) copy-start(bf16[32,640]{1,0:T(8,128)(2,1)} %constant.43.clone.basis.ahead) | copy-start | bytes 122884
  26.5 3.9 %copy-start = (bf16[3,384,384]{2,1,0:T(8,128)(2,1)S(1)}, bf16[3,384,384]{2,1,0:T(8,128)(2,1)}, u32[]{:S(2)}) copy-start(bf16[3,384,384]{2,1,0:T(8,128)(2,1)} %constant.46.clone.cols) | copy-start | bytes 2654212
  26.7 4.6 %copy-start.2 = (f32[3,16,384]{2,1,0:T(8,128)}, f32[3,16,384]{2,1,0:T(8,128)S(1)}, u32[]{:S(2)}) copy-start(f32[3,16,384]{2,1,0:T(8,128)S(1)} %reshape.29.ren) | copy-start | bytes 221188
  26.7 4.6 %collective-permute-start.1 = (f32[3,10,384]{2,1,0:T(8,128)S(1)}, f32[3,10,384]{2,1,0:T(8,128)S(1)}, u32[]{:S(2)}, u32[]{:S(2)}) collective-permute-start(f32[3,10,384]{2,1,0:T(8,128)S(1)} %get-tuple-element.14), channel_id=1, source_target_pairs={{1,2},{3,4},{5,6},{7,8},{9,10},{11,12},{13,14},{15,16},{17,18},{19... | collective-permute-start | bytes 138248 | tf_op jit(solution)/shard_map/ppermute | solution.py:501
  27.5 2.8 %copy-start.3 = (bf16[144,144]{1,0:T(8,128)(2,1)S(1)}, bf16[144,144]{1,0:T(8,128)(2,1)}, u32[]{:S(2)}) copy-start(bf16[144,144]{1,0:T(8,128)(2,1)} %constant.76.rows_back) | copy-start | bytes 124420
  27.5 3.8 %collective-permute-start = (f32[3,10,384]{2,1,0:T(8,128)S(1)}, f32[3,10,384]{2,1,0:T(8,128)S(1)}, u32[]{:S(2)}, u32[]{:S(2)}) collective-permute-start(f32[3,10,384]{2,1,0:T(8,128)S(1)} %get-tuple-element.15), channel_id=1, source_target_pairs={{0,1},{1,0},{2,3},{3,2},{4,5},{5,4},{6,7},{7,6},{8,9},{9,8},{10,11... | collective-permute-start | bytes 138248 | tf_op jit(solution)/shard_map/ppermute | solution.py:500
  51.2 12.8 %copy-start.5 = (f32[2,2048]{1,0:T(2,128)S(1)}, f32[2,2048]{1,0:T(2,128)}, u32[]{:S(2)}) copy-start(f32[2,2048]{1,0:T(2,128)} %centres.3) | copy-start | bytes 49156
  51.2 12.8 %copy-start.6 = (f32[2,2048]{1,0:T(2,128)S(1)}, f32[2,2048]{1,0:T(2,128)}, u32[]{:S(2)}) copy-start(f32[2,2048]{1,0:T(2,128)} %conic.3) | copy-start | bytes 49156
  51.2 12.8 %copy-start.7 = (s32[1,2048]{1,0:T(1,128)S(1)}, s32[1,2048]{1,0:T(1,128)}, u32[]{:S(2)}) copy-start(s32[1,2048]{1,0:T(1,128)} %rows_ref.3) | copy-start | bytes 24580
  51.2 12.8 %copy-start.8 = (f32[1,2048]{1,0:T(1,128)S(1)}, f32[1,2048]{1,0:T(1,128)}, u32[]{:S(2)}) copy-start(f32[1,2048]{1,0:T(1,128)} %rho.3) | copy-start | bytes 24580
  51.2 12.8 %copy-start.9 = (f32[1,2048]{1,0:T(1,128)S(1)}, f32[1,2048]{1,0:T(1,128)}, u32[]{:S(2)}) copy-start(f32[1,2048]{1,0:T(1,128)} %opacity.3) | copy-start | bytes 24580

commit v6 on v5

--- a/solution.py
+++ b/solution.py
@@ -161,7 +161,7 @@
             composite(i * par + k)
         return carry
 
-    par = part_of(tiles, 4)
+    par = part_of(tiles, 6)
     lax.fori_loop(0, tiles // par, body, 0)
 
 
@@ -176,7 +176,15 @@
         got = dot(rows, jnp.concatenate(pieces(x, 3), axis=0), NN)
         done.append(got[:height] + got[height : 2 * height] + got[2 * height :])
     stacked = jnp.concatenate(done, axis=0)
-    out = exact(pieces(stacked, 3), [cols[k] for k in range(3)])
+    parts = pieces(stacked, 3)
+    width = stacked.shape[1]
+    out = []
+    for low in range(0, width, 2 * LANES):
+        high = min(low + 2 * LANES, width)
+        first = max(low - RIM, 0) // LANES * LANES
+        end = min(-(-(high + RIM) // LANES) * LANES, width)
+        out.append(exact([p[:, first:end] for p in parts], [cols[k, first:end, low:high] for k in range(3)]))
+    out = jnp.concatenate(out, axis=1)
     return [out[i * height : (i + 1) * height] for i in range(len(images))]
 
 
@@ -353,13 +361,19 @@
     def sums(t, factors, tints_ref, split):
         got = jnp.where(moment, dot(factors[...], phi[...], NN), tints_ref[...])
         where = [idx_ref[pl.ds(t * groups + q, 1), :] for q in range(groups)]
-        where = jnp.concatenate(where + [where[0]] * (SUB - groups), axis=0)
-        chunk = jnp.transpose(jnp.where(where < 0, -1, jnp.right_shift(where, 8)))
+        words = []
+        for q, idx in enumerate(where):
+            if q % 4 == 0:
+                words.append(jnp.zeros((1, LANES), jnp.int32))
+            words[-1] = words[-1] | jnp.left_shift(jnp.where(idx < 0, 255, jnp.right_shift(idx, 8)), 8 * (q % 4))
+        words = jnp.transpose(jnp.concatenate(words + [words[0]] * (SUB - len(words)), axis=0))
         for q in range(groups):
             at = slice(q * LANES, (q + 1) * LANES)
-            mine = jnp.broadcast_to(chunk[:, q : q + 1], (LANES, LANES))
+            if q % 4 == 0:
+                word = jnp.broadcast_to(words[:, q // 4 : q // 4 + 1], (LANES, LANES))
+            mine = word & jnp.left_shift(jnp.full((LANES, LANES), 255, jnp.int32), 8 * (q % 4))
             for base in range(0, columns, LANES):
-                kept = jnp.where(mine == block + base // BLOCK, got[at], 0.0)
+                kept = jnp.where(mine == jnp.left_shift(block + base // BLOCK, 8 * (q % 4)), got[at], 0.0)
                 top, rest = pieces(kept, 2)
                 split[at, base : base + LANES] = top
                 split[at, columns + base : columns + base + LANES] = rest

time: 65.7 us -> 64.7 us (0.985)
  Pallas kernels: 31.2 us -> 30 us
    pallas_call x6, Pallas kernels: 31.2 us -> 30 us  [run(): pl.pallas_call(kernel, out_shape=out_shape, in_specs=specs, out_specs=jax...]
where the time goes in v6:
time: 64.7 us; the launch traced here: 64.2 us
  Pallas kernels  30 us (46%)
  starting transfers between devices  13.8 us (21%)
  blocking collectives  12.8 us (20%)
  waiting for transfers between devices  2.87 us (4%)
  local copies, waits for them, and re-layouts  2.05 us (3%)
  other arithmetic  1.72 us (3%)
  between operations  0.91 us (1%)
    pallas_call x6, Pallas kernels, run(): pl.pallas_call(kernel, out_shape=out_shape, in_specs=specs, out_specs=jax...  30 us
    all_to_all x1, blocking collectives, shards(): lax.all_to_all(slot_sums, 'dev', split_axis=0, concat_axis=0, tiled=True)  12.8 us
    all_to_all x1, starting transfers between devices, shards(): lax.all_to_all(packed, 'dev', split_axis=0, concat_axis=0, tiled=True)  7.3 us
    ppermute x2, starting transfers between devices, swap_edges(): got_in = lax.ppermute(jnp.where(odd, first, last), 'dev', inner)  4.42 us
    all_to_all x1, waiting for transfers between devices, shards(): lax.all_to_all(packed, 'dev', split_axis=0, concat_axis=0, tiled=True)  2.86 us
    ppermute x2, starting transfers between devices, swap_edges(): got_out = lax.ppermute(jnp.where(odd, last, first), 'dev', outer)  2.09 us
  transfers between devices with their start and end apart: 5, of which 1 were waited for; matrix products, arithmetic and copies ran while one was open for 5% of the time, Pallas kernels for 13%

profile of v6, /device:TPU:0, one launch (start us, length us, event | category | flops | bytes accessed | tf_op | source)
XLA Modules:
  0.0 64.2 jit_solution(18257305133326676611)
XLA Ops:
  0.6 2.2 %shard_map.131 = f32[256,128]{1,0:T(8,128)} custom-call(s32[1,2048]{1,0:T(1,128)} %rows_ref.3, f32[2,2048]{1,0:T(2,128)} %centres.3, f32[2,2048]{1,0:T(2,128)} %conic.3, f32[1,2048]{1,0:T(1,128)} %rho.3, f32[1,2048]{1,0:T(1,128)} %opacity.3, f32[3,2048]{1,0:T(4,128)} %colors.1), custom_call_target="tpu_custom_call" | custom-call | tf_op jit(solution)/shard_map/pallas_call | solution.py:494
  2.8 0.0 copy-start.1
  2.8 7.3 %all-to-all-start = ((f32[32,8,128]{2,1,0:T(8,128)}), f32[32,8,128]{2,1,0:T(8,128)S(1)}, u32[]{:S(2)}, u32[]{:S(2)}) async-start(f32[32,8,128]{2,1,0:T(8,128)} %bitcast.21), calls=%async_computation | async-start | bytes 262144 | tf_op jit(solution)/shard_map/all_to_all | solution.py:537
  10.1 0.0 copy-done.1
  10.1 0.0 copy-start.10
  10.1 0.7 %slice_select_fusion.2 = (f32[3,10,384]{2,1,0:T(8,128)}, f32[3,10,384]{2,1,0:T(8,128)}) fusion(f32[3,16,384]{2,1,0:T(8,128)S(1)} %copy-done.1, pred[]{:T(512)S(6)} %eq.15), kind=kLoop, calls=%fused_computation.2 | loop fusion | flops 23040 | bytes 184321 | tf_op jit(solution)/shard_map/jit(_where)/select_n | solution.py:515
  10.8 1.3 %collective-permute-start.3 = (f32[3,10,384]{2,1,0:T(8,128)}, f32[3,10,384]{2,1,0:T(8,128)}, u32[]{:S(2)}, u32[]{:S(2)}) collective-permute-start(f32[3,10,384]{2,1,0:T(8,128)} %get-tuple-element.12), channel_id=1, source_target_pairs={{1,2},{3,4},{5,6},{7,8},{9,10},{11,12},{13,14},{15,16},{17,18},{19... | collective-permute-start | bytes 138248 | tf_op jit(solution)/shard_map/ppermute | solution.py:515
  12.1 2.6 %collective-permute-start.2 = (f32[3,10,384]{2,1,0:T(8,128)}, f32[3,10,384]{2,1,0:T(8,128)}, u32[]{:S(2)}, u32[]{:S(2)}) collective-permute-start(f32[3,10,384]{2,1,0:T(8,128)} %get-tuple-element.13), channel_id=1, source_target_pairs={{0,1},{1,0},{2,3},{3,2},{4,5},{5,4},{6,7},{7,6},{8,9},{9,8},{10,11... | collective-permute-start | bytes 138248 | tf_op jit(solution)/shard_map/ppermute | solution.py:514
  14.7 0.0 copy-done.10
  14.7 0.1 reshape.26
  14.8 0.3 copy.17
  15.0 0.0 copy-start.4
  15.1 0.4 reshape.27.idx_ref
  15.4 0.1 pad_add_fusion.edge
  15.5 2.9 %all-to-all-done = f32[32,8,128]{2,1,0:T(8,128)S(1)} async-done(((f32[32,8,128]{2,1,0:T(8,128)}), f32[32,8,128]{2,1,0:T(8,128)S(1)}, u32[]{:S(2)}, u32[]{:S(2)}) %all-to-all-start) | async-done | bytes 131104 | tf_op jit(solution)/shard_map/all_to_all | solution.py:537
  18.4 0.0 copy-done.4
  18.4 7.4 %shard_map.132 = (f32[24,3,256]{2,1,0:T(4,128)S(1)}, bf16[24,32,512]{2,1,0:T(8,128)(2,1)S(1)}, f32[24,40,256]{2,1,0:T(8,128)S(1)}) custom-call(f32[256,128]{1,0:T(8,128)S(1)} %bitcast.16, s32[96,128]{1,0:T(8,128)S(1)} %reshape.27.idx_ref, bf16[32,640]{1,0:T(8,128)(2,1)S(1)} %copy-done.4), custom_call_target="tpu_custom_call" | custom-call | tf_op jit(solution)/shard_map/pallas_call | solution.py:494
  25.8 0.2 reshape.28
  26.0 0.2 copy.19
  26.2 0.0 copy-start
  26.2 0.2 reshape.29.ren
  26.5 0.0 copy-start.2
  26.5 0.8 %collective-permute-start.1 = (f32[3,10,384]{2,1,0:T(8,128)S(1)}, f32[3,10,384]{2,1,0:T(8,128)S(1)}, u32[]{:S(2)}, u32[]{:S(2)}) collective-permute-start(f32[3,10,384]{2,1,0:T(8,128)S(1)} %get-tuple-element.14), channel_id=1, source_target_pairs={{1,2},{3,4},{5,6},{7,8},{9,10},{11,12},{13,14},{15,16},{17,18},{19... | collective-permute-start | bytes 138248 | tf_op jit(solution)/shard_map/ppermute | solution.py:515
  27.3 0.0 copy-start.3
  27.3 1.9 %collective-permute-start = (f32[3,10,384]{2,1,0:T(8,128)S(1)}, f32[3,10,384]{2,1,0:T(8,128)S(1)}, u32[]{:S(2)}, u32[]{:S(2)}) collective-permute-start(f32[3,10,384]{2,1,0:T(8,128)S(1)} %get-tuple-element.15), channel_id=1, source_target_pairs={{0,1},{1,0},{2,3},{3,2},{4,5},{5,4},{6,7},{7,6},{8,9},{9,8},{10,11... | collective-permute-start | bytes 138248 | tf_op jit(solution)/shard_map/ppermute | solution.py:514
  29.2 0.0 collective-permute-done.3
  29.2 0.0 collective-permute-done.2
  29.2 0.9 %broadcast_select_fusion = (f32[3,10,384]{2,1,0:T(8,128)S(1)}, f32[3,10,384]{2,1,0:T(8,128)S(1)}) fusion(f32[3,10,384]{2,1,0:T(8,128)} %collective-permute-done.3, f32[3,10,384]{2,1,0:T(8,128)} %collective-permute-done.2, pred[]{:T(512)S(6)} %eq.15), kind=kLoop, calls=%fused_computation.4 | loop fusion | flops 23040 | bytes 184321 | tf_op jit(solution)/shard_map/jit(_where)/select_n | solution.py:516
  30.1 0.0 copy-done
  30.1 0.0 copy-done.3
  30.1 0.9 %shard_map.133.known = f32[6,32,384]{2,1,0:T(8,128)S(1)} custom-call(f32[3,16,384]{2,1,0:T(8,128)S(1)} %copy-done.1, f32[3,10,384]{2,1,0:T(8,128)S(1)} %get-tuple-element.9.tar_b, f32[3,10,384]{2,1,0:T(8,128)S(1)} %get-tuple-element.8.tar_a, bf16[144,144]{1,0:T(8,128)(2,1)S(1)} %copy-done.3, bf16[3,384,384]{2,1,0:T(8,128)(2,1)S(1)} %copy-done), custom_call_target="tpu_custom_call" | custom-call | tf_op jit(solution)/shard_map/pallas_call | solution.py:494
  31.0 0.0 collective-permute-done.1
  31.0 0.0 collective-permute-done
  31.1 0.0 copy-done.2
  31.1 3.0 %shard_map.134 = f32[3,16,384]{2,1,0:T(8,128)S(1)} custom-call(s32[2]{0:T(128)S(1)} %pad_add_fusion.edge, f32[3,16,384]{2,1,0:T(8,128)S(1)} %reshape.29.ren, f32[3,16,384]{2,1,0:T(8,128)S(1)} %copy-done.1, f32[3,10,384]{2,1,0:T(8,128)S(1)} %get-tuple-element.11.ren_b, f32[3,10,384]{2,1,0:T(8,128)S(1)} %get-tuple-element.9.tar_b, ...), custom_call_target="tpu_custom_call" | custom-call | tf_op jit(solution)/shard_map/pallas_call | solution.py:494
  34.0 0.2 reshape.30
  34.3 0.1 copy.22
  34.4 0.3 reshape.32.cot_ref
  34.7 15.3 %shard_map.135 = f32[256,128]{1,0:T(8,128)S(1)} custom-call(bf16[24,32,512]{2,1,0:T(8,128)(2,1)S(1)} %get-tuple-element.6.x_ref, s32[96,128]{1,0:T(8,128)S(1)} %reshape.27.idx_ref, f32[24,40,256]{2,1,0:T(8,128)S(1)} %get-tuple-element.7.seg_ref, f32[24,3,256]{2,1,0:T(4,128)S(1)} %reshape.32.cot_ref, bf16[32,640]{1,0:T(8,128)(2,1)S(1)} %copy-done.4), custom_call_target="tpu_custom_call" | custom-call | tf_op jit(solution)/shard_map/pallas_call | solution.py:494
  50.0 0.0 copy-start.5
  50.0 0.0 copy-start.6
  50.1 0.0 copy-start.7
  50.1 0.0 copy-start.8
  50.1 0.0 copy-start.9
  50.1 12.8 %all_to_all.22 = f32[32,8,128]{2,1,0:T(8,128)S(1)} all-to-all(f32[32,8,128]{2,1,0:T(8,128)S(1)} %bitcast.15), channel_id=1, replica_groups=mesh['dev'=32] {'dev'}, dimensions={0} | all-to-all | bytes 262144 | tf_op jit(solution)/shard_map/all_to_all | solution.py:571
  62.9 0.0 copy-done.5
  62.9 0.0 copy-done.6
  62.9 0.0 copy-done.7
  62.9 0.0 copy-done.8
  62.9 0.0 copy-done.9
  62.9 1.2 %shard_map.136 = f32[9,2048]{1,0:T(8,128)} custom-call(f32[256,128]{1,0:T(8,128)S(1)} %bitcast.17, s32[1,2048]{1,0:T(1,128)S(1)} %copy-done.7, f32[2,2048]{1,0:T(2,128)S(1)} %copy-done.5, f32[2,2048]{1,0:T(2,128)S(1)} %copy-done.6, f32[1,2048]{1,0:T(1,128)S(1)} %copy-done.8, f32[1,2048]{1,0:T(1,128)S(1)} %copy-done.9), custom_call_target="tpu_custom_call" | custom-call | tf_op jit(solution)/shard_map/pallas_call | solution.py:494
  (3 shorter events, 0.0 us)
Async XLA Ops:
  2.8 7.3 %copy-start.1 = (f32[3,16,384]{2,1,0:T(8,128)S(1)}, f32[3,16,384]{2,1,0:T(8,128)}, u32[]{:S(2)}) copy-start(f32[3,16,384]{2,1,0:T(8,128)} %tar.3) | copy-start | bytes 221188
  2.8 15.6 %all-to-all-start = ((f32[32,8,128]{2,1,0:T(8,128)}), f32[32,8,128]{2,1,0:T(8,128)S(1)}, u32[]{:S(2)}, u32[]{:S(2)}) async-start(f32[32,8,128]{2,1,0:T(8,128)} %bitcast.21), calls=%async_computation | async-start | bytes 262144 | tf_op jit(solution)/shard_map/all_to_all | solution.py:537
  10.1 4.5 %copy-start.10 = (s32[24,512]{1,0:T(8,128)S(1)}, s32[24,512]{1,0:T(8,128)}, u32[]{:S(2)}) copy-start(s32[24,512]{1,0:T(8,128)} %param.12) | copy-start | bytes 147460
  10.8 18.3 %collective-permute-start.3 = (f32[3,10,384]{2,1,0:T(8,128)}, f32[3,10,384]{2,1,0:T(8,128)}, u32[]{:S(2)}, u32[]{:S(2)}) collective-permute-start(f32[3,10,384]{2,1,0:T(8,128)} %get-tuple-element.12), channel_id=1, source_target_pairs={{1,2},{3,4},{5,6},{7,8},{9,10},{11,12},{13,14},{15,16},{17,18},{19... | collective-permute-start | bytes 138248 | tf_op jit(solution)/shard_map/ppermute | solution.py:515
  12.1 17.1 %collective-permute-start.2 = (f32[3,10,384]{2,1,0:T(8,128)}, f32[3,10,384]{2,1,0:T(8,128)}, u32[]{:S(2)}, u32[]{:S(2)}) collective-permute-start(f32[3,10,384]{2,1,0:T(8,128)} %get-tuple-element.13), channel_id=1, source_target_pairs={{0,1},{1,0},{2,3},{3,2},{4,5},{5,4},{6,7},{7,6},{8,9},{9,8},{10,11... | collective-permute-start | bytes 138248 | tf_op jit(solution)/shard_map/ppermute | solution.py:514
  15.0 3.3 %copy-start.4 = (bf16[32,640]{1,0:T(8,128)(2,1)S(1)}, bf16[32,640]{1,0:T(8,128)(2,1)}, u32[]{:S(2)}) copy-start(bf16[32,640]{1,0:T(8,128)(2,1)} %constant.43.clone.basis.ahead) | copy-start | bytes 122884
  26.2 3.9 %copy-start = (bf16[3,384,384]{2,1,0:T(8,128)(2,1)S(1)}, bf16[3,384,384]{2,1,0:T(8,128)(2,1)}, u32[]{:S(2)}) copy-start(bf16[3,384,384]{2,1,0:T(8,128)(2,1)} %constant.46.clone.cols) | copy-start | bytes 2654212
  26.5 4.6 %copy-start.2 = (f32[3,16,384]{2,1,0:T(8,128)}, f32[3,16,384]{2,1,0:T(8,128)S(1)}, u32[]{:S(2)}) copy-start(f32[3,16,384]{2,1,0:T(8,128)S(1)} %reshape.29.ren) | copy-start | bytes 221188
  26.5 4.5 %collective-permute-start.1 = (f32[3,10,384]{2,1,0:T(8,128)S(1)}, f32[3,10,384]{2,1,0:T(8,128)S(1)}, u32[]{:S(2)}, u32[]{:S(2)}) collective-permute-start(f32[3,10,384]{2,1,0:T(8,128)S(1)} %get-tuple-element.14), channel_id=1, source_target_pairs={{1,2},{3,4},{5,6},{7,8},{9,10},{11,12},{13,14},{15,16},{17,18},{19... | collective-permute-start | bytes 138248 | tf_op jit(solution)/shard_map/ppermute | solution.py:515
  27.3 2.8 %copy-start.3 = (bf16[144,144]{1,0:T(8,128)(2,1)S(1)}, bf16[144,144]{1,0:T(8,128)(2,1)}, u32[]{:S(2)}) copy-start(bf16[144,144]{1,0:T(8,128)(2,1)} %constant.76.rows_back) | copy-start | bytes 124420
  27.3 3.7 %collective-permute-start = (f32[3,10,384]{2,1,0:T(8,128)S(1)}, f32[3,10,384]{2,1,0:T(8,128)S(1)}, u32[]{:S(2)}, u32[]{:S(2)}) collective-permute-start(f32[3,10,384]{2,1,0:T(8,128)S(1)} %get-tuple-element.15), channel_id=1, source_target_pairs={{0,1},{1,0},{2,3},{3,2},{4,5},{5,4},{6,7},{7,6},{8,9},{9,8},{10,11... | collective-permute-start | bytes 138248 | tf_op jit(solution)/shard_map/ppermute | solution.py:514
  50.0 12.9 %copy-start.5 = (f32[2,2048]{1,0:T(2,128)S(1)}, f32[2,2048]{1,0:T(2,128)}, u32[]{:S(2)}) copy-start(f32[2,2048]{1,0:T(2,128)} %centres.3) | copy-start | bytes 49156
  50.0 12.9 %copy-start.6 = (f32[2,2048]{1,0:T(2,128)S(1)}, f32[2,2048]{1,0:T(2,128)}, u32[]{:S(2)}) copy-start(f32[2,2048]{1,0:T(2,128)} %conic.3) | copy-start | bytes 49156
  50.1 12.9 %copy-start.7 = (s32[1,2048]{1,0:T(1,128)S(1)}, s32[1,2048]{1,0:T(1,128)}, u32[]{:S(2)}) copy-start(s32[1,2048]{1,0:T(1,128)} %rows_ref.3) | copy-start | bytes 24580
  50.1 12.9 %copy-start.8 = (f32[1,2048]{1,0:T(1,128)S(1)}, f32[1,2048]{1,0:T(1,128)}, u32[]{:S(2)}) copy-start(f32[1,2048]{1,0:T(1,128)} %rho.3) | copy-start | bytes 24580
  50.1 12.9 %copy-start.9 = (f32[1,2048]{1,0:T(1,128)S(1)}, f32[1,2048]{1,0:T(1,128)}, u32[]{:S(2)}) copy-start(f32[1,2048]{1,0:T(1,128)} %opacity.3) | copy-start | bytes 24580

commit v7 on v6

--- a/solution.py
+++ b/solution.py
@@ -105,7 +105,23 @@
     return pltpu.roll(x, by % SUB, 0)
 
 
-def forward_kernel(recv, idx_ref, basis, img_ref, x_ref, seg_ref, table):
+def six_of(kind, spot, side):
+    down = jnp.right_shift(spot, side.bit_length() - 1)
+    u = (spot - down * side).astype(F32) - (side - 1) / 2.0
+    v = down.astype(F32) - (side - 1) / 2.0
+    six = jnp.zeros(kind.shape, F32)
+    for i, f in enumerate((jnp.ones_like(u), u, v, u * u, u * v, v * v)):
+        six = jnp.where(kind == i, f, six)
+    return six
+
+
+def terms(pixels):
+    r = rows_of((32, pixels))
+    kind = jnp.where(r < 24, jnp.bitwise_and(r, SUB - 1), SUB)
+    return six_of(kind, lanes_of((32, pixels)), int(pixels**0.5))
+
+
+def forward_kernel(recv, idx_ref, img_ref, x_ref, seg_ref, table, basis):
     tiles, pixels = img_ref.shape[0], img_ref.shape[2]
     groups = x_ref.shape[2] // LANES
     wide = table.shape[1]
@@ -121,6 +137,11 @@
             ninths.append(n[0:1])
         fill(table, c, jnp.concatenate(eights, axis=1), jnp.concatenate(ninths, axis=1))
     none = jnp.where(rows_of((32, wide)) == 0, -1000.0, 0.0)
+    basis[:, :pixels] = terms(pixels).astype(BF16)
+    r = rows_of((32, LANES))
+    for ch in range(3):
+        spread_it = jnp.logical_and(r < 24, jnp.bitwise_and(r, SUB - 1) == 6 + ch) if ch < 2 else jnp.logical_and(r >= 24, r < 27)
+        basis[:, pixels + ch * LANES : pixels + (ch + 1) * LANES] = jnp.where(spread_it, 1.0, 0.0).astype(BF16)
     row = rows_of((SUB, pixels))
 
     def fetch(t):
@@ -161,7 +182,7 @@
             composite(i * par + k)
         return carry
 
-    par = part_of(tiles, 6)
+    par = part_of(tiles, 8)
     lax.fori_loop(0, tiles // par, body, 0)
 
 
@@ -297,7 +318,7 @@
     )
 
 
-def backward_kernel(x_ref, idx_ref, seg_ref, cot_ref, ahead, out_ref, total, phi, *buffers):
+def backward_kernel(x_ref, idx_ref, seg_ref, cot_ref, out_ref, total, phi, *buffers):
     tiles, pixels = cot_ref.shape[0], cot_ref.shape[2]
     count = x_ref.shape[2]
     groups = count // LANES
@@ -308,16 +329,9 @@
     each = 3
     columns = total.shape[1] // 2
     field = jnp.bitwise_and(lanes_of((SUB, LANES)), BLOCK - 1)
-    basis = jnp.concatenate([ahead[:, :pixels], jnp.zeros((32, pixels), BF16)], axis=0)
-    side = int(pixels**0.5)
+    basis = jnp.concatenate([terms(pixels), jnp.zeros((32, pixels), F32)], axis=0).astype(BF16)
     kind = jnp.bitwise_and(lanes_of((pixels, LANES)), BLOCK - 1)
-    spot = rows_of((pixels, LANES))
-    down = jnp.right_shift(spot, side.bit_length() - 1)
-    u = (spot - down * side).astype(F32) - (side - 1) / 2.0
-    v = down.astype(F32) - (side - 1) / 2.0
-    six = jnp.zeros((pixels, LANES), F32)
-    for i, f in enumerate((jnp.ones_like(u), u, v, u * u, u * v, v * v)):
-        six = jnp.where(kind == i, f, six)
+    six = six_of(kind, rows_of((pixels, LANES)), int(pixels**0.5))
     phi[:pixels] = six.astype(BF16)
     phi[pixels:] = six.astype(BF16)
     moment = jnp.bitwise_and(lanes_of((count, LANES)), BLOCK - 1) < 6
@@ -461,21 +475,6 @@
             out_ref[i : i + 1, at] = v
 
 
-def tables(tile):
-    pixels = tile * tile
-    p = np.arange(pixels)
-    v = (p // tile) - (tile - 1) / 2.0
-    u = (p % tile) - (tile - 1) / 2.0
-    six = np.stack([np.ones(pixels), u, v, u * u, u * v, v * v])
-    ahead = np.zeros((32, pixels + 3 * LANES), np.float32)
-    for k in range(3):
-        ahead[8 * k : 8 * k + 6, :pixels] = six
-        ahead[8 * k + 6, pixels : pixels + LANES] = 1.0
-        ahead[8 * k + 7, pixels + LANES : pixels + 2 * LANES] = 1.0
-        ahead[24 + k, pixels + 2 * LANES :] = 1.0
-    return jnp.asarray(ahead, BF16)
-
-
 def back_scratch(list_len, pixels, slots, par):
     columns = slots // (2 * LANES) * BLOCK
     one = [
@@ -525,7 +524,6 @@
     me = lax.axis_index("dev")
     pixels = tile * tile
     wide = 2 * LANES
-    basis = tables(tile)
     sds = jax.ShapeDtypeStruct
 
     packed = call(
@@ -550,8 +548,8 @@
             sds((strip_tiles, 32, list_len), BF16),
             sds((strip_tiles, 5 * SUB, pixels), F32),
         ),
-        [pltpu.VMEM((slot_count // wide * 32, wide), BF16)],
-    )(received, order, basis)
+        [pltpu.VMEM((slot_count // wide * 32, wide), BF16), pltpu.VMEM((32, pixels + 3 * LANES), BF16)],
+    )(received, order)
     image = (
         colour_tiles.reshape(strip_tiles, channels, tile, tile).transpose(1, 2, 0, 3).reshape(channels, tile, width)
     )
@@ -566,8 +564,8 @@
     slot_sums = call(
         backward_kernel,
         sds((size * SUB, LANES), F32),
-        back_scratch(list_len, pixels, slot_count, part_of(strip_tiles, 6)),
-    )(coefs, order, segments, cot_tiles, basis)
+        back_scratch(list_len, pixels, slot_count, part_of(strip_tiles, 8)),
+    )(coefs, order, segments, cot_tiles)
     returned = lax.all_to_all(slot_sums, "dev", split_axis=0, concat_axis=0, tiled=True)
     grads = call(
         home_kernel,

time: 64.7 us -> 64 us (0.989)
  no operation moved by 1% of the time
where the time goes in v7:
time: 64 us; the launch traced here: 63.6 us
  Pallas kernels  29.5 us (46%)
  starting transfers between devices  14 us (22%)
  blocking collectives  12.6 us (20%)
  waiting for transfers between devices  2.88 us (4%)
  local copies, waits for them, and re-layouts  2.04 us (3%)
  other arithmetic  1.67 us (3%)
  between operations  0.92 us (1%)
    pallas_call x6, Pallas kernels, run(): pl.pallas_call(kernel, out_shape=out_shape, in_specs=specs, out_specs=jax...  29.5 us
    all_to_all x1, blocking collectives, shards(): lax.all_to_all(slot_sums, 'dev', split_axis=0, concat_axis=0, tiled=True)  12.6 us
    all_to_all x1, starting transfers between devices, shards(): lax.all_to_all(packed, 'dev', split_axis=0, concat_axis=0, tiled=True)  7.3 us
    ppermute x2, starting transfers between devices, swap_edges(): got_in = lax.ppermute(jnp.where(odd, first, last), 'dev', inner)  5.04 us
    all_to_all x1, waiting for transfers between devices, shards(): lax.all_to_all(packed, 'dev', split_axis=0, concat_axis=0, tiled=True)  2.87 us
    ppermute x2, starting transfers between devices, swap_edges(): got_out = lax.ppermute(jnp.where(odd, last, first), 'dev', outer)  1.63 us
  transfers between devices with their start and end apart: 5, of which 1 were waited for; matrix products, arithmetic and copies ran while one was open for 5% of the time, Pallas kernels for 13%

profile of v7, /device:TPU:0, one launch (start us, length us, event | category | flops | bytes accessed | tf_op | source)
XLA Modules:
  0.0 63.6 jit_solution(13402131771471118357)
XLA Ops:
  0.6 2.2 %shard_map.122 = f32[256,128]{1,0:T(8,128)} custom-call(s32[1,2048]{1,0:T(1,128)} %rows_ref.3, f32[2,2048]{1,0:T(2,128)} %centres.3, f32[2,2048]{1,0:T(2,128)} %conic.3, f32[1,2048]{1,0:T(1,128)} %rho.3, f32[1,2048]{1,0:T(1,128)} %opacity.3, f32[3,2048]{1,0:T(4,128)} %colors.1), custom_call_target="tpu_custom_call" | custom-call | tf_op jit(solution)/shard_map/pallas_call | solution.py:493
  2.8 0.0 copy-start.1
  2.8 7.3 %all-to-all-start = ((f32[32,8,128]{2,1,0:T(8,128)}), f32[32,8,128]{2,1,0:T(8,128)S(1)}, u32[]{:S(2)}, u32[]{:S(2)}) async-start(f32[32,8,128]{2,1,0:T(8,128)} %bitcast.21), calls=%async_computation | async-start | bytes 262144 | tf_op jit(solution)/shard_map/all_to_all | solution.py:535
  10.1 0.0 copy-done.1
  10.1 0.0 copy-start.9
  10.1 0.7 %slice_select_fusion.2 = (f32[3,10,384]{2,1,0:T(8,128)}, f32[3,10,384]{2,1,0:T(8,128)}) fusion(f32[3,16,384]{2,1,0:T(8,128)S(1)} %copy-done.1, pred[]{:T(512)S(6)} %eq.15), kind=kLoop, calls=%fused_computation.2 | loop fusion | flops 23040 | bytes 184321 | tf_op jit(solution)/shard_map/jit(_where)/select_n | solution.py:514
  10.8 0.7 %collective-permute-start.3 = (f32[3,10,384]{2,1,0:T(8,128)}, f32[3,10,384]{2,1,0:T(8,128)S(1)}, u32[]{:S(2)}, u32[]{:S(2)}) collective-permute-start(f32[3,10,384]{2,1,0:T(8,128)} %get-tuple-element.12), channel_id=1, source_target_pairs={{1,2},{3,4},{5,6},{7,8},{9,10},{11,12},{13,14},{15,16},{17,18},{19... | collective-permute-start | bytes 138248 | tf_op jit(solution)/shard_map/ppermute | solution.py:514
  11.5 3.2 %collective-permute-start.2 = (f32[3,10,384]{2,1,0:T(8,128)}, f32[3,10,384]{2,1,0:T(8,128)}, u32[]{:S(2)}, u32[]{:S(2)}) collective-permute-start(f32[3,10,384]{2,1,0:T(8,128)} %get-tuple-element.13), channel_id=1, source_target_pairs={{0,1},{1,0},{2,3},{3,2},{4,5},{5,4},{6,7},{7,6},{8,9},{9,8},{10,11... | collective-permute-start | bytes 138248 | tf_op jit(solution)/shard_map/ppermute | solution.py:513
  14.7 0.0 copy-done.9
  14.7 0.1 reshape.26
  14.7 0.3 copy.16
  15.0 0.4 reshape.27.idx_ref
  15.4 0.1 pad_add_fusion.edge
  15.5 2.9 %all-to-all-done = f32[32,8,128]{2,1,0:T(8,128)S(1)} async-done(((f32[32,8,128]{2,1,0:T(8,128)}), f32[32,8,128]{2,1,0:T(8,128)S(1)}, u32[]{:S(2)}, u32[]{:S(2)}) %all-to-all-start) | async-done | bytes 131104 | tf_op jit(solution)/shard_map/all_to_all | solution.py:535
  18.3 7.3 %shard_map.123 = (f32[24,3,256]{2,1,0:T(4,128)S(1)}, bf16[24,32,512]{2,1,0:T(8,128)(2,1)S(1)}, f32[24,40,256]{2,1,0:T(8,128)S(1)}) custom-call(f32[256,128]{1,0:T(8,128)S(1)} %bitcast.16, s32[96,128]{1,0:T(8,128)S(1)} %reshape.27.idx_ref), custom_call_target="tpu_custom_call" | custom-call | tf_op jit(solution)/shard_map/pallas_call | solution.py:493
  25.6 0.2 reshape.28
  25.9 0.2 copy.18
  26.1 0.0 copy-start
  26.1 0.2 reshape.29.ren
  26.3 0.0 copy-start.2
  26.3 1.0 %collective-permute-start.1 = (f32[3,10,384]{2,1,0:T(8,128)S(1)}, f32[3,10,384]{2,1,0:T(8,128)S(1)}, u32[]{:S(2)}, u32[]{:S(2)}) collective-permute-start(f32[3,10,384]{2,1,0:T(8,128)S(1)} %get-tuple-element.14), channel_id=1, source_target_pairs={{1,2},{3,4},{5,6},{7,8},{9,10},{11,12},{13,14},{15,16},{17,18},{19... | collective-permute-start | bytes 138248 | tf_op jit(solution)/shard_map/ppermute | solution.py:514
  27.3 0.0 copy-start.3
  27.3 1.8 %collective-permute-start = (f32[3,10,384]{2,1,0:T(8,128)S(1)}, f32[3,10,384]{2,1,0:T(8,128)S(1)}, u32[]{:S(2)}, u32[]{:S(2)}) collective-permute-start(f32[3,10,384]{2,1,0:T(8,128)S(1)} %get-tuple-element.15), channel_id=1, source_target_pairs={{0,1},{1,0},{2,3},{3,2},{4,5},{5,4},{6,7},{7,6},{8,9},{9,8},{10,11... | collective-permute-start | bytes 138248 | tf_op jit(solution)/shard_map/ppermute | solution.py:513
  29.2 0.0 collective-permute-done.3
  29.2 0.0 collective-permute-done.2
  29.2 0.9 %broadcast_select_fusion = (f32[3,10,384]{2,1,0:T(8,128)S(1)}, f32[3,10,384]{2,1,0:T(8,128)S(1)}) fusion(f32[3,10,384]{2,1,0:T(8,128)S(1)} %collective-permute-done.3, f32[3,10,384]{2,1,0:T(8,128)} %collective-permute-done.2, pred[]{:T(512)S(6)} %eq.15), kind=kLoop, calls=%fused_computation.4 | loop fusion | flops 23040 | bytes 184321 | tf_op jit(solution)/shard_map/jit(_where)/select_n | solution.py:515
  30.1 0.0 copy-done
  30.1 0.0 copy-done.3
  30.1 0.9 %shard_map.124.known = f32[6,32,384]{2,1,0:T(8,128)S(1)} custom-call(f32[3,16,384]{2,1,0:T(8,128)S(1)} %copy-done.1, f32[3,10,384]{2,1,0:T(8,128)S(1)} %get-tuple-element.9.tar_b, f32[3,10,384]{2,1,0:T(8,128)S(1)} %get-tuple-element.8.tar_a, bf16[144,144]{1,0:T(8,128)(2,1)S(1)} %copy-done.3, bf16[3,384,384]{2,1,0:T(8,128)(2,1)S(1)} %copy-done), custom_call_target="tpu_custom_call" | custom-call | tf_op jit(solution)/shard_map/pallas_call | solution.py:493
  31.0 0.0 collective-permute-done.1
  31.0 0.0 collective-permute-done
  31.0 0.0 copy-done.2
  31.0 2.9 %shard_map.125 = f32[3,16,384]{2,1,0:T(8,128)S(1)} custom-call(s32[2]{0:T(128)S(1)} %pad_add_fusion.edge, f32[3,16,384]{2,1,0:T(8,128)S(1)} %reshape.29.ren, f32[3,16,384]{2,1,0:T(8,128)S(1)} %copy-done.1, f32[3,10,384]{2,1,0:T(8,128)S(1)} %get-tuple-element.11.ren_b, f32[3,10,384]{2,1,0:T(8,128)S(1)} %get-tuple-element.9.tar_b, ...), custom_call_target="tpu_custom_call" | custom-call | tf_op jit(solution)/shard_map/pallas_call | solution.py:493
  34.0 0.2 reshape.30
  34.2 0.1 copy.21
  34.3 0.3 reshape.32.cot_ref
  34.6 15.0 %shard_map.126 = f32[256,128]{1,0:T(8,128)S(1)} custom-call(bf16[24,32,512]{2,1,0:T(8,128)(2,1)S(1)} %get-tuple-element.6.x_ref, s32[96,128]{1,0:T(8,128)S(1)} %reshape.27.idx_ref, f32[24,40,256]{2,1,0:T(8,128)S(1)} %get-tuple-element.7.seg_ref, f32[24,3,256]{2,1,0:T(4,128)S(1)} %reshape.32.cot_ref), custom_call_target="tpu_custom_call" | custom-call | tf_op jit(solution)/shard_map/pallas_call | solution.py:493
  49.6 0.0 copy-start.4
  49.6 0.0 copy-start.5
  49.6 0.0 copy-start.6
  49.6 0.0 copy-start.7
  49.7 0.0 copy-start.8
  49.7 12.6 %all_to_all.22 = f32[32,8,128]{2,1,0:T(8,128)S(1)} all-to-all(f32[32,8,128]{2,1,0:T(8,128)S(1)} %bitcast.15), channel_id=1, replica_groups=mesh['dev'=32] {'dev'}, dimensions={0} | all-to-all | bytes 262144 | tf_op jit(solution)/shard_map/all_to_all | solution.py:569
  62.3 0.0 copy-done.4
  62.3 0.0 copy-done.5
  62.3 0.0 copy-done.6
  62.3 0.0 copy-done.7
  62.3 0.0 copy-done.8
  62.3 1.2 %shard_map.127 = f32[9,2048]{1,0:T(8,128)} custom-call(f32[256,128]{1,0:T(8,128)S(1)} %bitcast.17, s32[1,2048]{1,0:T(1,128)S(1)} %copy-done.6, f32[2,2048]{1,0:T(2,128)S(1)} %copy-done.4, f32[2,2048]{1,0:T(2,128)S(1)} %copy-done.5, f32[1,2048]{1,0:T(1,128)S(1)} %copy-done.7, f32[1,2048]{1,0:T(1,128)S(1)} %copy-done.8), custom_call_target="tpu_custom_call" | custom-call | tf_op jit(solution)/shard_map/pallas_call | solution.py:493
  (3 shorter events, 0.0 us)
Async XLA Ops:
  2.8 7.3 %copy-start.1 = (f32[3,16,384]{2,1,0:T(8,128)S(1)}, f32[3,16,384]{2,1,0:T(8,128)}, u32[]{:S(2)}) copy-start(f32[3,16,384]{2,1,0:T(8,128)} %tar.3) | copy-start | bytes 221188
  2.8 15.5 %all-to-all-start = ((f32[32,8,128]{2,1,0:T(8,128)}), f32[32,8,128]{2,1,0:T(8,128)S(1)}, u32[]{:S(2)}, u32[]{:S(2)}) async-start(f32[32,8,128]{2,1,0:T(8,128)} %bitcast.21), calls=%async_computation | async-start | bytes 262144 | tf_op jit(solution)/shard_map/all_to_all | solution.py:535
  10.1 4.5 %copy-start.9 = (s32[24,512]{1,0:T(8,128)S(1)}, s32[24,512]{1,0:T(8,128)}, u32[]{:S(2)}) copy-start(s32[24,512]{1,0:T(8,128)} %param.11) | copy-start | bytes 147460
  10.8 18.4 %collective-permute-start.3 = (f32[3,10,384]{2,1,0:T(8,128)}, f32[3,10,384]{2,1,0:T(8,128)S(1)}, u32[]{:S(2)}, u32[]{:S(2)}) collective-permute-start(f32[3,10,384]{2,1,0:T(8,128)} %get-tuple-element.12), channel_id=1, source_target_pairs={{1,2},{3,4},{5,6},{7,8},{9,10},{11,12},{13,14},{15,16},{17,18},{19... | collective-permute-start | bytes 138248 | tf_op jit(solution)/shard_map/ppermute | solution.py:514
  11.5 17.7 %collective-permute-start.2 = (f32[3,10,384]{2,1,0:T(8,128)}, f32[3,10,384]{2,1,0:T(8,128)}, u32[]{:S(2)}, u32[]{:S(2)}) collective-permute-start(f32[3,10,384]{2,1,0:T(8,128)} %get-tuple-element.13), channel_id=1, source_target_pairs={{0,1},{1,0},{2,3},{3,2},{4,5},{5,4},{6,7},{7,6},{8,9},{9,8},{10,11... | collective-permute-start | bytes 138248 | tf_op jit(solution)/shard_map/ppermute | solution.py:513
  26.1 4.0 %copy-start = (bf16[3,384,384]{2,1,0:T(8,128)(2,1)S(1)}, bf16[3,384,384]{2,1,0:T(8,128)(2,1)}, u32[]{:S(2)}) copy-start(bf16[3,384,384]{2,1,0:T(8,128)(2,1)} %constant.43.clone.cols) | copy-start | bytes 2654212
  26.3 4.7 %copy-start.2 = (f32[3,16,384]{2,1,0:T(8,128)}, f32[3,16,384]{2,1,0:T(8,128)S(1)}, u32[]{:S(2)}) copy-start(f32[3,16,384]{2,1,0:T(8,128)S(1)} %reshape.29.ren) | copy-start | bytes 221188
  26.3 4.7 %collective-permute-start.1 = (f32[3,10,384]{2,1,0:T(8,128)S(1)}, f32[3,10,384]{2,1,0:T(8,128)S(1)}, u32[]{:S(2)}, u32[]{:S(2)}) collective-permute-start(f32[3,10,384]{2,1,0:T(8,128)S(1)} %get-tuple-element.14), channel_id=1, source_target_pairs={{1,2},{3,4},{5,6},{7,8},{9,10},{11,12},{13,14},{15,16},{17,18},{19... | collective-permute-start | bytes 138248 | tf_op jit(solution)/shard_map/ppermute | solution.py:514
  27.3 2.8 %copy-start.3 = (bf16[144,144]{1,0:T(8,128)(2,1)S(1)}, bf16[144,144]{1,0:T(8,128)(2,1)}, u32[]{:S(2)}) copy-start(bf16[144,144]{1,0:T(8,128)(2,1)} %constant.73.rows_back) | copy-start | bytes 124420
  27.3 3.7 %collective-permute-start = (f32[3,10,384]{2,1,0:T(8,128)S(1)}, f32[3,10,384]{2,1,0:T(8,128)S(1)}, u32[]{:S(2)}, u32[]{:S(2)}) collective-permute-start(f32[3,10,384]{2,1,0:T(8,128)S(1)} %get-tuple-element.15), channel_id=1, source_target_pairs={{0,1},{1,0},{2,3},{3,2},{4,5},{5,4},{6,7},{7,6},{8,9},{9,8},{10,11... | collective-permute-start | bytes 138248 | tf_op jit(solution)/shard_map/ppermute | solution.py:513
  49.6 12.7 %copy-start.4 = (f32[2,2048]{1,0:T(2,128)S(1)}, f32[2,2048]{1,0:T(2,128)}, u32[]{:S(2)}) copy-start(f32[2,2048]{1,0:T(2,128)} %centres.3) | copy-start | bytes 49156
  49.6 12.7 %copy-start.5 = (f32[2,2048]{1,0:T(2,128)S(1)}, f32[2,2048]{1,0:T(2,128)}, u32[]{:S(2)}) copy-start(f32[2,2048]{1,0:T(2,128)} %conic.3) | copy-start | bytes 49156
  49.6 12.7 %copy-start.6 = (s32[1,2048]{1,0:T(1,128)S(1)}, s32[1,2048]{1,0:T(1,128)}, u32[]{:S(2)}) copy-start(s32[1,2048]{1,0:T(1,128)} %rows_ref.3) | copy-start | bytes 24580
  49.6 12.7 %copy-start.7 = (f32[1,2048]{1,0:T(1,128)S(1)}, f32[1,2048]{1,0:T(1,128)}, u32[]{:S(2)}) copy-start(f32[1,2048]{1,0:T(1,128)} %rho.3) | copy-start | bytes 24580
  49.7 12.7 %copy-start.8 = (f32[1,2048]{1,0:T(1,128)S(1)}, f32[1,2048]{1,0:T(1,128)}, u32[]{:S(2)}) copy-start(f32[1,2048]{1,0:T(1,128)} %opacity.3) | copy-start | bytes 24580

commit v8 on v7

--- a/solution.py
+++ b/solution.py
@@ -168,10 +168,9 @@
         for by in (1, 2, 4):
             before = before * jnp.where(row >= by, shifted(before, by), 1.0)
         seg_ref[t, 0:SUB] = before
-        seg_ref[t, SUB : 2 * SUB] = trans
         image = []
         for ch in range(3):
-            seg_ref[t, (2 + ch) * SUB : (3 + ch) * SUB] = acc[ch]
+            seg_ref[t, (1 + ch) * SUB : (2 + ch) * SUB] = acc[ch]
             image.append(jnp.sum(acc[ch] * before, axis=0, keepdims=True))
         img_ref[t] = jnp.concatenate(image, axis=0)
 
@@ -349,7 +348,7 @@
         rhs = jnp.concatenate(place(hi) + place(lo), axis=0).astype(BF16)
         rhs = jnp.concatenate([basis, rhs], axis=1)
         trans = seg_ref[t, 0:SUB]
-        rest = trans * (cot[0] * seg_ref[t, 2 * SUB : 3 * SUB] + cot[1] * seg_ref[t, 3 * SUB : 4 * SUB] + cot[2] * seg_ref[t, 4 * SUB : 5 * SUB])
+        rest = trans * (cot[0] * seg_ref[t, SUB : 2 * SUB] + cot[1] * seg_ref[t, 2 * SUB : 3 * SUB] + cot[2] * seg_ref[t, 3 * SUB : 4 * SUB])
         for by in (1, 2, 4):
             rest = rest + jnp.where(row < SUB - by, shifted(rest, -by), 0.0)
         for q in range(groups):
@@ -436,7 +435,7 @@
     half = LANES // 2
     left = lanes_of((SUB, LANES)) < half
     total[...] = jnp.zeros_like(total)
-    step = 4
+    step = 8
     for g in range(0, rows_ref.shape[1] // LANES, step):
         eights, ninths = [], []
         for k in range(g, g + step):
@@ -546,7 +545,7 @@
         (
             sds((strip_tiles, channels, pixels), F32),
             sds((strip_tiles, 32, list_len), BF16),
-            sds((strip_tiles, 5 * SUB, pixels), F32),
+            sds((strip_tiles, 4 * SUB, pixels), F32),
         ),
         [pltpu.VMEM((slot_count // wide * 32, wide), BF16), pltpu.VMEM((32, pixels + 3 * LANES), BF16)],
     )(received, order)

time: 64 us -> 64.1 us (level)
  other arithmetic: 1.67 us -> 0.14 us
  blocking collectives: 12.6 us -> 13.5 us
    select_n x2, other arithmetic: 0.92 us -> 0.03 us  [swap_edges(): return (jnp.where(odd, got_in, got_out), jnp.where(odd, got_out, got_in))]
    all_to_all x1, blocking collectives: 12.6 us -> 13.5 us  [shards(): lax.all_to_all(slot_sums, 'dev', split_axis=0, concat_axis=0, tiled=True)]
    select_n x2, other arithmetic: 0.68 us -> 0.03 us  [swap_edges(): got_out = lax.ppermute(jnp.where(odd, last, first), 'dev', outer)]
  transfers between devices with their start and end apart: 5 -> 5, of which waited for: 1 -> 1; matrix products, arithmetic and copies ran while one was open for 5% -> 2% of each run, Pallas kernels for 13% -> 13%
where the time goes in v8:
time: 64.1 us; the launch traced here: 63.6 us
  Pallas kernels  29.5 us (46%)
  starting transfers between devices  14 us (22%)
  blocking collectives  13.5 us (21%)
  waiting for transfers between devices  3.5 us (5%)
  local copies, waits for them, and re-layouts  2.04 us (3%)
  between operations  0.93 us (1%)
    pallas_call x6, Pallas kernels, run(): pl.pallas_call(kernel, out_shape=out_shape, in_specs=specs, out_specs=jax...  29.5 us
    all_to_all x1, blocking collectives, shards(): lax.all_to_all(slot_sums, 'dev', split_axis=0, concat_axis=0, tiled=True)  13.5 us
    all_to_all x1, starting transfers between devices, shards(): lax.all_to_all(packed, 'dev', split_axis=0, concat_axis=0, tiled=True)  7.3 us
    ppermute x2, starting transfers between devices, swap_edges(): got_in = lax.ppermute(jnp.where(odd, first, last), 'dev', inner)  5.06 us
    all_to_all x1, waiting for transfers between devices, shards(): lax.all_to_all(packed, 'dev', split_axis=0, concat_axis=0, tiled=True)  3.49 us
    ppermute x2, starting transfers between devices, swap_edges(): got_out = lax.ppermute(jnp.where(odd, last, first), 'dev', outer)  1.64 us
  transfers between devices with their start and end apart: 5, of which 1 were waited for; matrix products, arithmetic and copies ran while one was open for 2% of the time, Pallas kernels for 13%

profile of v8, /device:TPU:0, one launch (start us, length us, event | category | flops | bytes accessed | tf_op | source)
XLA Modules:
  0.0 63.6 jit_solution(2141499804753134517)
XLA Ops:
  0.6 2.2 %shard_map.122 = f32[256,128]{1,0:T(8,128)} custom-call(s32[1,2048]{1,0:T(1,128)} %rows_ref.3, f32[2,2048]{1,0:T(2,128)} %centres.3, f32[2,2048]{1,0:T(2,128)} %conic.3, f32[1,2048]{1,0:T(1,128)} %rho.3, f32[1,2048]{1,0:T(1,128)} %opacity.3, f32[3,2048]{1,0:T(4,128)} %colors.1), custom_call_target="tpu_custom_call" | custom-call | tf_op jit(solution)/shard_map/pallas_call | solution.py:492
  2.8 0.0 copy-start.1
  2.8 7.3 %all-to-all-start = ((f32[32,8,128]{2,1,0:T(8,128)}), f32[32,8,128]{2,1,0:T(8,128)S(1)}, u32[]{:S(2)}, u32[]{:S(2)}) async-start(f32[32,8,128]{2,1,0:T(8,128)} %bitcast.21), calls=%async_computation | async-start | bytes 262144 | tf_op jit(solution)/shard_map/all_to_all | solution.py:534
  10.1 0.0 copy-done.1
  10.1 0.0 copy-start.9
  10.2 0.7 %collective-permute-start.3 = (f32[3,10,384]{2,1,0:T(8,128)S(1)}, f32[3,10,384]{2,1,0:T(8,128)S(1)}, u32[]{:S(2)}, u32[]{:S(2)}) collective-permute-start(f32[3,10,384]{2,1,0:T(8,128)S(1)} %get-tuple-element.12), channel_id=1, source_target_pairs={{1,2},{3,4},{5,6},{7,8},{9,10},{11,12},{13,14},{15,16},{17,18},{19... | collective-permute-start | bytes 138248 | tf_op jit(solution)/shard_map/ppermute | solution.py:513
  10.8 3.2 %collective-permute-start.2 = (f32[3,10,384]{2,1,0:T(8,128)S(1)}, f32[3,10,384]{2,1,0:T(8,128)S(1)}, u32[]{:S(2)}, u32[]{:S(2)}) collective-permute-start(f32[3,10,384]{2,1,0:T(8,128)S(1)} %get-tuple-element.13), channel_id=1, source_target_pairs={{0,1},{1,0},{2,3},{3,2},{4,5},{5,4},{6,7},{7,6},{8,9},{9,8},{10,11... | collective-permute-start | bytes 138248 | tf_op jit(solution)/shard_map/ppermute | solution.py:512
  14.0 0.0 copy-done.9
  14.0 0.1 reshape.26
  14.1 0.3 copy.16
  14.4 0.4 reshape.27.idx_ref
  14.8 0.1 pad_add_fusion.edge
  14.8 3.5 %all-to-all-done = f32[32,8,128]{2,1,0:T(8,128)S(1)} async-done(((f32[32,8,128]{2,1,0:T(8,128)}), f32[32,8,128]{2,1,0:T(8,128)S(1)}, u32[]{:S(2)}, u32[]{:S(2)}) %all-to-all-start) | async-done | bytes 131104 | tf_op jit(solution)/shard_map/all_to_all | solution.py:534
  18.3 7.3 %shard_map.123 = (f32[24,3,256]{2,1,0:T(4,128)S(1)}, bf16[24,32,512]{2,1,0:T(8,128)(2,1)S(1)}, f32[24,32,256]{2,1,0:T(8,128)S(1)}) custom-call(f32[256,128]{1,0:T(8,128)S(1)} %bitcast.16, s32[96,128]{1,0:T(8,128)S(1)} %reshape.27.idx_ref), custom_call_target="tpu_custom_call" | custom-call | tf_op jit(solution)/shard_map/pallas_call | solution.py:492
  25.7 0.2 reshape.28
  25.9 0.2 copy.18
  26.1 0.0 copy-start
  26.1 0.2 reshape.29.ren
  26.3 0.0 copy-start.2
  26.3 1.0 %collective-permute-start.1 = (f32[3,10,384]{2,1,0:T(8,128)S(1)}, f32[3,10,384]{2,1,0:T(8,128)S(1)}, u32[]{:S(2)}, u32[]{:S(2)}) collective-permute-start(f32[3,10,384]{2,1,0:T(8,128)S(1)} %get-tuple-element.14), channel_id=1, source_target_pairs={{1,2},{3,4},{5,6},{7,8},{9,10},{11,12},{13,14},{15,16},{17,18},{19... | collective-permute-start | bytes 138248 | tf_op jit(solution)/shard_map/ppermute | solution.py:513
  27.3 0.0 copy-start.3
  27.3 1.9 %collective-permute-start = (f32[3,10,384]{2,1,0:T(8,128)S(1)}, f32[3,10,384]{2,1,0:T(8,128)S(1)}, u32[]{:S(2)}, u32[]{:S(2)}) collective-permute-start(f32[3,10,384]{2,1,0:T(8,128)S(1)} %get-tuple-element.15), channel_id=1, source_target_pairs={{0,1},{1,0},{2,3},{3,2},{4,5},{5,4},{6,7},{7,6},{8,9},{9,8},{10,11... | collective-permute-start | bytes 138248 | tf_op jit(solution)/shard_map/ppermute | solution.py:512
  29.2 0.0 collective-permute-done.3
  29.2 0.0 collective-permute-done.2
  29.2 0.0 copy-done
  29.2 0.0 copy-done.3
  29.2 0.9 %shard_map.124.known = f32[6,32,384]{2,1,0:T(8,128)S(1)} custom-call(f32[3,16,384]{2,1,0:T(8,128)S(1)} %copy-done.1, f32[3,10,384]{2,1,0:T(8,128)S(1)} %get-tuple-element.9.tar_b, f32[3,10,384]{2,1,0:T(8,128)S(1)} %get-tuple-element.8.tar_a, bf16[144,144]{1,0:T(8,128)(2,1)S(1)} %copy-done.3, bf16[3,384,384]{2,1,0:T(8,128)(2,1)S(1)} %copy-done), custom_call_target="tpu_custom_call" | custom-call | tf_op jit(solution)/shard_map/pallas_call | solution.py:492
  30.1 0.0 collective-permute-done.1
  30.1 0.0 collective-permute-done
  30.2 0.0 copy-done.2
  30.2 2.9 %shard_map.125 = f32[3,16,384]{2,1,0:T(8,128)S(1)} custom-call(s32[2]{0:T(128)S(1)} %pad_add_fusion.edge, f32[3,16,384]{2,1,0:T(8,128)S(1)} %reshape.29.ren, f32[3,16,384]{2,1,0:T(8,128)S(1)} %copy-done.1, f32[3,10,384]{2,1,0:T(8,128)S(1)} %get-tuple-element.11.ren_b, f32[3,10,384]{2,1,0:T(8,128)S(1)} %get-tuple-element.9.tar_b, ...), custom_call_target="tpu_custom_call" | custom-call | tf_op jit(solution)/shard_map/pallas_call | solution.py:492
  33.1 0.2 reshape.30
  33.4 0.1 copy.21
  33.5 0.3 reshape.32.cot_ref
  33.8 15.0 %shard_map.126 = f32[256,128]{1,0:T(8,128)S(1)} custom-call(bf16[24,32,512]{2,1,0:T(8,128)(2,1)S(1)} %get-tuple-element.6.x_ref, s32[96,128]{1,0:T(8,128)S(1)} %reshape.27.idx_ref, f32[24,32,256]{2,1,0:T(8,128)S(1)} %get-tuple-element.7.seg_ref, f32[24,3,256]{2,1,0:T(4,128)S(1)} %reshape.32.cot_ref), custom_call_target="tpu_custom_call" | custom-call | tf_op jit(solution)/shard_map/pallas_call | solution.py:492
  48.8 0.0 copy-start.4
  48.8 0.0 copy-start.5
  48.8 0.0 copy-start.6
  48.8 0.0 copy-start.7
  48.8 0.0 copy-start.8
  48.8 13.5 %all_to_all.22 = f32[32,8,128]{2,1,0:T(8,128)S(1)} all-to-all(f32[32,8,128]{2,1,0:T(8,128)S(1)} %bitcast.15), channel_id=1, replica_groups=mesh['dev'=32] {'dev'}, dimensions={0} | all-to-all | bytes 262144 | tf_op jit(solution)/shard_map/all_to_all | solution.py:568
  62.4 0.0 copy-done.4
  62.4 0.0 copy-done.5
  62.4 0.0 copy-done.6
  62.4 0.0 copy-done.7
  62.4 0.0 copy-done.8
  62.4 1.2 %shard_map.127 = f32[9,2048]{1,0:T(8,128)} custom-call(f32[256,128]{1,0:T(8,128)S(1)} %bitcast.17, s32[1,2048]{1,0:T(1,128)S(1)} %copy-done.6, f32[2,2048]{1,0:T(2,128)S(1)} %copy-done.4, f32[2,2048]{1,0:T(2,128)S(1)} %copy-done.5, f32[1,2048]{1,0:T(1,128)S(1)} %copy-done.7, f32[1,2048]{1,0:T(1,128)S(1)} %copy-done.8), custom_call_target="tpu_custom_call" | custom-call | tf_op jit(solution)/shard_map/pallas_call | solution.py:492
  (5 shorter events, 0.1 us)
Async XLA Ops:
  2.8 7.3 %copy-start.1 = (f32[3,16,384]{2,1,0:T(8,128)S(1)}, f32[3,16,384]{2,1,0:T(8,128)}, u32[]{:S(2)}) copy-start(f32[3,16,384]{2,1,0:T(8,128)} %tar.3) | copy-start | bytes 221188
  2.8 15.5 %all-to-all-start = ((f32[32,8,128]{2,1,0:T(8,128)}), f32[32,8,128]{2,1,0:T(8,128)S(1)}, u32[]{:S(2)}, u32[]{:S(2)}) async-start(f32[32,8,128]{2,1,0:T(8,128)} %bitcast.21), calls=%async_computation | async-start | bytes 262144 | tf_op jit(solution)/shard_map/all_to_all | solution.py:534
  10.1 3.9 %copy-start.9 = (s32[24,512]{1,0:T(8,128)S(1)}, s32[24,512]{1,0:T(8,128)}, u32[]{:S(2)}) copy-start(s32[24,512]{1,0:T(8,128)} %param.11) | copy-start | bytes 147460
  10.2 19.0 %collective-permute-start.3 = (f32[3,10,384]{2,1,0:T(8,128)S(1)}, f32[3,10,384]{2,1,0:T(8,128)S(1)}, u32[]{:S(2)}, u32[]{:S(2)}) collective-permute-start(f32[3,10,384]{2,1,0:T(8,128)S(1)} %get-tuple-element.12), channel_id=1, source_target_pairs={{1,2},{3,4},{5,6},{7,8},{9,10},{11,12},{13,14},{15,16},{17,18},{19... | collective-permute-start | bytes 138248 | tf_op jit(solution)/shard_map/ppermute | solution.py:513
  10.8 18.4 %collective-permute-start.2 = (f32[3,10,384]{2,1,0:T(8,128)S(1)}, f32[3,10,384]{2,1,0:T(8,128)S(1)}, u32[]{:S(2)}, u32[]{:S(2)}) collective-permute-start(f32[3,10,384]{2,1,0:T(8,128)S(1)} %get-tuple-element.13), channel_id=1, source_target_pairs={{0,1},{1,0},{2,3},{3,2},{4,5},{5,4},{6,7},{7,6},{8,9},{9,8},{10,11... | collective-permute-start | bytes 138248 | tf_op jit(solution)/shard_map/ppermute | solution.py:512
  26.1 3.2 %copy-start = (bf16[3,384,384]{2,1,0:T(8,128)(2,1)S(1)}, bf16[3,384,384]{2,1,0:T(8,128)(2,1)}, u32[]{:S(2)}) copy-start(bf16[3,384,384]{2,1,0:T(8,128)(2,1)} %constant.43.clone.cols) | copy-start | bytes 2654212
  26.3 3.9 %copy-start.2 = (f32[3,16,384]{2,1,0:T(8,128)}, f32[3,16,384]{2,1,0:T(8,128)S(1)}, u32[]{:S(2)}) copy-start(f32[3,16,384]{2,1,0:T(8,128)S(1)} %reshape.29.ren) | copy-start | bytes 221188
  26.3 3.8 %collective-permute-start.1 = (f32[3,10,384]{2,1,0:T(8,128)S(1)}, f32[3,10,384]{2,1,0:T(8,128)S(1)}, u32[]{:S(2)}, u32[]{:S(2)}) collective-permute-start(f32[3,10,384]{2,1,0:T(8,128)S(1)} %get-tuple-element.14), channel_id=1, source_target_pairs={{1,2},{3,4},{5,6},{7,8},{9,10},{11,12},{13,14},{15,16},{17,18},{19... | collective-permute-start | bytes 138248 | tf_op jit(solution)/shard_map/ppermute | solution.py:513
  27.3 1.9 %copy-start.3 = (bf16[144,144]{1,0:T(8,128)(2,1)S(1)}, bf16[144,144]{1,0:T(8,128)(2,1)}, u32[]{:S(2)}) copy-start(bf16[144,144]{1,0:T(8,128)(2,1)} %constant.73.rows_back) | copy-start | bytes 124420
  27.3 2.8 %collective-permute-start = (f32[3,10,384]{2,1,0:T(8,128)S(1)}, f32[3,10,384]{2,1,0:T(8,128)S(1)}, u32[]{:S(2)}, u32[]{:S(2)}) collective-permute-start(f32[3,10,384]{2,1,0:T(8,128)S(1)} %get-tuple-element.15), channel_id=1, source_target_pairs={{0,1},{1,0},{2,3},{3,2},{4,5},{5,4},{6,7},{7,6},{8,9},{9,8},{10,11... | collective-permute-start | bytes 138248 | tf_op jit(solution)/shard_map/ppermute | solution.py:512
  48.8 13.6 %copy-start.4 = (f32[2,2048]{1,0:T(2,128)S(1)}, f32[2,2048]{1,0:T(2,128)}, u32[]{:S(2)}) copy-start(f32[2,2048]{1,0:T(2,128)} %centres.3) | copy-start | bytes 49156
  48.8 13.6 %copy-start.5 = (f32[2,2048]{1,0:T(2,128)S(1)}, f32[2,2048]{1,0:T(2,128)}, u32[]{:S(2)}) copy-start(f32[2,2048]{1,0:T(2,128)} %conic.3) | copy-start | bytes 49156
  48.8 13.6 %copy-start.6 = (s32[1,2048]{1,0:T(1,128)S(1)}, s32[1,2048]{1,0:T(1,128)}, u32[]{:S(2)}) copy-start(s32[1,2048]{1,0:T(1,128)} %rows_ref.3) | copy-start | bytes 24580
  48.8 13.6 %copy-start.7 = (f32[1,2048]{1,0:T(1,128)S(1)}, f32[1,2048]{1,0:T(1,128)}, u32[]{:S(2)}) copy-start(f32[1,2048]{1,0:T(1,128)} %rho.3) | copy-start | bytes 24580
  48.8 13.6 %copy-start.8 = (f32[1,2048]{1,0:T(1,128)S(1)}, f32[1,2048]{1,0:T(1,128)}, u32[]{:S(2)}) copy-start(f32[1,2048]{1,0:T(1,128)} %opacity.3) | copy-start | bytes 24580

commit v9 on v8

--- a/solution.py
+++ b/solution.py
@@ -563,7 +563,7 @@
     slot_sums = call(
         backward_kernel,
         sds((size * SUB, LANES), F32),
-        back_scratch(list_len, pixels, slot_count, part_of(strip_tiles, 8)),
+        back_scratch(list_len, pixels, slot_count, part_of(strip_tiles, 12)),
     )(coefs, order, segments, cot_tiles)
     returned = lax.all_to_all(slot_sums, "dev", split_axis=0, concat_axis=0, tiled=True)
     grads = call(

time: 64.1 us -> 63.9 us (level)
  no operation moved by 1% of the time
where the time goes in v9:
time: 63.9 us; the launch traced here: 63.5 us
  Pallas kernels  29.4 us (46%)
  starting transfers between devices  14 us (22%)
  blocking collectives  13.5 us (21%)
  waiting for transfers between devices  3.5 us (5%)
  local copies, waits for them, and re-layouts  2.04 us (3%)
  between operations  0.93 us (1%)
    pallas_call x6, Pallas kernels, run(): pl.pallas_call(kernel, out_shape=out_shape, in_specs=specs, out_specs=jax...  29.4 us
    all_to_all x1, blocking collectives, shards(): lax.all_to_all(slot_sums, 'dev', split_axis=0, concat_axis=0, tiled=True)  13.5 us
    all_to_all x1, starting transfers between devices, shards(): lax.all_to_all(packed, 'dev', split_axis=0, concat_axis=0, tiled=True)  7.3 us
    ppermute x2, starting transfers between devices, swap_edges(): got_in = lax.ppermute(jnp.where(odd, first, last), 'dev', inner)  5.06 us
    all_to_all x1, waiting for transfers between devices, shards(): lax.all_to_all(packed, 'dev', split_axis=0, concat_axis=0, tiled=True)  3.49 us
    ppermute x2, starting transfers between devices, swap_edges(): got_out = lax.ppermute(jnp.where(odd, last, first), 'dev', outer)  1.64 us
  transfers between devices with their start and end apart: 5, of which 1 were waited for; matrix products, arithmetic and copies ran while one was open for 2% of the time, Pallas kernels for 13%

profile of v9, /device:TPU:0, one launch (start us, length us, event | category | flops | bytes accessed | tf_op | source)
XLA Modules:
  0.0 63.5 jit_solution(18172509095138916694)
XLA Ops:
  0.6 2.2 %shard_map.122 = f32[256,128]{1,0:T(8,128)} custom-call(s32[1,2048]{1,0:T(1,128)} %rows_ref.3, f32[2,2048]{1,0:T(2,128)} %centres.3, f32[2,2048]{1,0:T(2,128)} %conic.3, f32[1,2048]{1,0:T(1,128)} %rho.3, f32[1,2048]{1,0:T(1,128)} %opacity.3, f32[3,2048]{1,0:T(4,128)} %colors.1), custom_call_target="tpu_custom_call" | custom-call | tf_op jit(solution)/shard_map/pallas_call | solution.py:492
  2.8 0.0 copy-start.1
  2.8 7.3 %all-to-all-start = ((f32[32,8,128]{2,1,0:T(8,128)}), f32[32,8,128]{2,1,0:T(8,128)S(1)}, u32[]{:S(2)}, u32[]{:S(2)}) async-start(f32[32,8,128]{2,1,0:T(8,128)} %bitcast.21), calls=%async_computation | async-start | bytes 262144 | tf_op jit(solution)/shard_map/all_to_all | solution.py:534
  10.1 0.0 copy-done.1
  10.1 0.0 copy-start.9
  10.2 0.7 %collective-permute-start.3 = (f32[3,10,384]{2,1,0:T(8,128)S(1)}, f32[3,10,384]{2,1,0:T(8,128)S(1)}, u32[]{:S(2)}, u32[]{:S(2)}) collective-permute-start(f32[3,10,384]{2,1,0:T(8,128)S(1)} %get-tuple-element.12), channel_id=1, source_target_pairs={{1,2},{3,4},{5,6},{7,8},{9,10},{11,12},{13,14},{15,16},{17,18},{19... | collective-permute-start | bytes 138248 | tf_op jit(solution)/shard_map/ppermute | solution.py:513
  10.8 3.2 %collective-permute-start.2 = (f32[3,10,384]{2,1,0:T(8,128)S(1)}, f32[3,10,384]{2,1,0:T(8,128)S(1)}, u32[]{:S(2)}, u32[]{:S(2)}) collective-permute-start(f32[3,10,384]{2,1,0:T(8,128)S(1)} %get-tuple-element.13), channel_id=1, source_target_pairs={{0,1},{1,0},{2,3},{3,2},{4,5},{5,4},{6,7},{7,6},{8,9},{9,8},{10,11... | collective-permute-start | bytes 138248 | tf_op jit(solution)/shard_map/ppermute | solution.py:512
  14.0 0.0 copy-done.9
  14.0 0.1 reshape.26
  14.1 0.3 copy.16
  14.4 0.4 reshape.27.idx_ref
  14.8 0.1 pad_add_fusion.edge
  14.8 3.5 %all-to-all-done = f32[32,8,128]{2,1,0:T(8,128)S(1)} async-done(((f32[32,8,128]{2,1,0:T(8,128)}), f32[32,8,128]{2,1,0:T(8,128)S(1)}, u32[]{:S(2)}, u32[]{:S(2)}) %all-to-all-start) | async-done | bytes 131104 | tf_op jit(solution)/shard_map/all_to_all | solution.py:534
  18.3 7.3 %shard_map.123 = (f32[24,3,256]{2,1,0:T(4,128)S(1)}, bf16[24,32,512]{2,1,0:T(8,128)(2,1)S(1)}, f32[24,32,256]{2,1,0:T(8,128)S(1)}) custom-call(f32[256,128]{1,0:T(8,128)S(1)} %bitcast.16, s32[96,128]{1,0:T(8,128)S(1)} %reshape.27.idx_ref), custom_call_target="tpu_custom_call" | custom-call | tf_op jit(solution)/shard_map/pallas_call | solution.py:492
  25.7 0.2 reshape.28
  25.9 0.2 copy.18
  26.1 0.0 copy-start
  26.1 0.2 reshape.29.ren
  26.3 0.0 copy-start.2
  26.3 1.0 %collective-permute-start.1 = (f32[3,10,384]{2,1,0:T(8,128)S(1)}, f32[3,10,384]{2,1,0:T(8,128)S(1)}, u32[]{:S(2)}, u32[]{:S(2)}) collective-permute-start(f32[3,10,384]{2,1,0:T(8,128)S(1)} %get-tuple-element.14), channel_id=1, source_target_pairs={{1,2},{3,4},{5,6},{7,8},{9,10},{11,12},{13,14},{15,16},{17,18},{19... | collective-permute-start | bytes 138248 | tf_op jit(solution)/shard_map/ppermute | solution.py:513
  27.3 0.0 copy-start.3
  27.3 1.9 %collective-permute-start = (f32[3,10,384]{2,1,0:T(8,128)S(1)}, f32[3,10,384]{2,1,0:T(8,128)S(1)}, u32[]{:S(2)}, u32[]{:S(2)}) collective-permute-start(f32[3,10,384]{2,1,0:T(8,128)S(1)} %get-tuple-element.15), channel_id=1, source_target_pairs={{0,1},{1,0},{2,3},{3,2},{4,5},{5,4},{6,7},{7,6},{8,9},{9,8},{10,11... | collective-permute-start | bytes 138248 | tf_op jit(solution)/shard_map/ppermute | solution.py:512
  29.2 0.0 collective-permute-done.3
  29.2 0.0 collective-permute-done.2
  29.2 0.0 copy-done
  29.2 0.0 copy-done.3
  29.2 0.9 %shard_map.124.known = f32[6,32,384]{2,1,0:T(8,128)S(1)} custom-call(f32[3,16,384]{2,1,0:T(8,128)S(1)} %copy-done.1, f32[3,10,384]{2,1,0:T(8,128)S(1)} %get-tuple-element.9.tar_b, f32[3,10,384]{2,1,0:T(8,128)S(1)} %get-tuple-element.8.tar_a, bf16[144,144]{1,0:T(8,128)(2,1)S(1)} %copy-done.3, bf16[3,384,384]{2,1,0:T(8,128)(2,1)S(1)} %copy-done), custom_call_target="tpu_custom_call" | custom-call | tf_op jit(solution)/shard_map/pallas_call | solution.py:492
  30.1 0.0 collective-permute-done.1
  30.1 0.0 collective-permute-done
  30.2 0.0 copy-done.2
  30.2 2.9 %shard_map.125 = f32[3,16,384]{2,1,0:T(8,128)S(1)} custom-call(s32[2]{0:T(128)S(1)} %pad_add_fusion.edge, f32[3,16,384]{2,1,0:T(8,128)S(1)} %reshape.29.ren, f32[3,16,384]{2,1,0:T(8,128)S(1)} %copy-done.1, f32[3,10,384]{2,1,0:T(8,128)S(1)} %get-tuple-element.11.ren_b, f32[3,10,384]{2,1,0:T(8,128)S(1)} %get-tuple-element.9.tar_b, ...), custom_call_target="tpu_custom_call" | custom-call | tf_op jit(solution)/shard_map/pallas_call | solution.py:492
  33.1 0.2 reshape.30
  33.4 0.1 copy.21
  33.5 0.3 reshape.32.cot_ref
  33.8 14.8 %shard_map.126 = f32[256,128]{1,0:T(8,128)S(1)} custom-call(bf16[24,32,512]{2,1,0:T(8,128)(2,1)S(1)} %get-tuple-element.6.x_ref, s32[96,128]{1,0:T(8,128)S(1)} %reshape.27.idx_ref, f32[24,32,256]{2,1,0:T(8,128)S(1)} %get-tuple-element.7.seg_ref, f32[24,3,256]{2,1,0:T(4,128)S(1)} %reshape.32.cot_ref), custom_call_target="tpu_custom_call" | custom-call | tf_op jit(solution)/shard_map/pallas_call | solution.py:492
  48.6 0.0 copy-start.4
  48.6 0.0 copy-start.5
  48.7 0.0 copy-start.6
  48.7 0.0 copy-start.7
  48.7 0.0 copy-start.8
  48.7 13.5 %all_to_all.22 = f32[32,8,128]{2,1,0:T(8,128)S(1)} all-to-all(f32[32,8,128]{2,1,0:T(8,128)S(1)} %bitcast.15), channel_id=1, replica_groups=mesh['dev'=32] {'dev'}, dimensions={0} | all-to-all | bytes 262144 | tf_op jit(solution)/shard_map/all_to_all | solution.py:568
  62.2 0.0 copy-done.4
  62.2 0.0 copy-done.5
  62.2 0.0 copy-done.6
  62.2 0.0 copy-done.7
  62.2 0.0 copy-done.8
  62.2 1.2 %shard_map.127 = f32[9,2048]{1,0:T(8,128)} custom-call(f32[256,128]{1,0:T(8,128)S(1)} %bitcast.17, s32[1,2048]{1,0:T(1,128)S(1)} %copy-done.6, f32[2,2048]{1,0:T(2,128)S(1)} %copy-done.4, f32[2,2048]{1,0:T(2,128)S(1)} %copy-done.5, f32[1,2048]{1,0:T(1,128)S(1)} %copy-done.7, f32[1,2048]{1,0:T(1,128)S(1)} %copy-done.8), custom_call_target="tpu_custom_call" | custom-call | tf_op jit(solution)/shard_map/pallas_call | solution.py:492
  (5 shorter events, 0.1 us)
Async XLA Ops:
  2.8 7.3 %copy-start.1 = (f32[3,16,384]{2,1,0:T(8,128)S(1)}, f32[3,16,384]{2,1,0:T(8,128)}, u32[]{:S(2)}) copy-start(f32[3,16,384]{2,1,0:T(8,128)} %tar.3) | copy-start | bytes 221188
  2.8 15.5 %all-to-all-start = ((f32[32,8,128]{2,1,0:T(8,128)}), f32[32,8,128]{2,1,0:T(8,128)S(1)}, u32[]{:S(2)}, u32[]{:S(2)}) async-start(f32[32,8,128]{2,1,0:T(8,128)} %bitcast.21), calls=%async_computation | async-start | bytes 262144 | tf_op jit(solution)/shard_map/all_to_all | solution.py:534
  10.1 3.9 %copy-start.9 = (s32[24,512]{1,0:T(8,128)S(1)}, s32[24,512]{1,0:T(8,128)}, u32[]{:S(2)}) copy-start(s32[24,512]{1,0:T(8,128)} %param.11) | copy-start | bytes 147460
  10.2 19.0 %collective-permute-start.3 = (f32[3,10,384]{2,1,0:T(8,128)S(1)}, f32[3,10,384]{2,1,0:T(8,128)S(1)}, u32[]{:S(2)}, u32[]{:S(2)}) collective-permute-start(f32[3,10,384]{2,1,0:T(8,128)S(1)} %get-tuple-element.12), channel_id=1, source_target_pairs={{1,2},{3,4},{5,6},{7,8},{9,10},{11,12},{13,14},{15,16},{17,18},{19... | collective-permute-start | bytes 138248 | tf_op jit(solution)/shard_map/ppermute | solution.py:513
  10.8 18.4 %collective-permute-start.2 = (f32[3,10,384]{2,1,0:T(8,128)S(1)}, f32[3,10,384]{2,1,0:T(8,128)S(1)}, u32[]{:S(2)}, u32[]{:S(2)}) collective-permute-start(f32[3,10,384]{2,1,0:T(8,128)S(1)} %get-tuple-element.13), channel_id=1, source_target_pairs={{0,1},{1,0},{2,3},{3,2},{4,5},{5,4},{6,7},{7,6},{8,9},{9,8},{10,11... | collective-permute-start | bytes 138248 | tf_op jit(solution)/shard_map/ppermute | solution.py:512
  26.1 3.2 %copy-start = (bf16[3,384,384]{2,1,0:T(8,128)(2,1)S(1)}, bf16[3,384,384]{2,1,0:T(8,128)(2,1)}, u32[]{:S(2)}) copy-start(bf16[3,384,384]{2,1,0:T(8,128)(2,1)} %constant.43.clone.cols) | copy-start | bytes 2654212
  26.3 3.9 %copy-start.2 = (f32[3,16,384]{2,1,0:T(8,128)}, f32[3,16,384]{2,1,0:T(8,128)S(1)}, u32[]{:S(2)}) copy-start(f32[3,16,384]{2,1,0:T(8,128)S(1)} %reshape.29.ren) | copy-start | bytes 221188
  26.3 3.8 %collective-permute-start.1 = (f32[3,10,384]{2,1,0:T(8,128)S(1)}, f32[3,10,384]{2,1,0:T(8,128)S(1)}, u32[]{:S(2)}, u32[]{:S(2)}) collective-permute-start(f32[3,10,384]{2,1,0:T(8,128)S(1)} %get-tuple-element.14), channel_id=1, source_target_pairs={{1,2},{3,4},{5,6},{7,8},{9,10},{11,12},{13,14},{15,16},{17,18},{19... | collective-permute-start | bytes 138248 | tf_op jit(solution)/shard_map/ppermute | solution.py:513
  27.3 1.9 %copy-start.3 = (bf16[144,144]{1,0:T(8,128)(2,1)S(1)}, bf16[144,144]{1,0:T(8,128)(2,1)}, u32[]{:S(2)}) copy-start(bf16[144,144]{1,0:T(8,128)(2,1)} %constant.73.rows_back) | copy-start | bytes 124420
  27.3 2.8 %collective-permute-start = (f32[3,10,384]{2,1,0:T(8,128)S(1)}, f32[3,10,384]{2,1,0:T(8,128)S(1)}, u32[]{:S(2)}, u32[]{:S(2)}) collective-permute-start(f32[3,10,384]{2,1,0:T(8,128)S(1)} %get-tuple-element.15), channel_id=1, source_target_pairs={{0,1},{1,0},{2,3},{3,2},{4,5},{5,4},{6,7},{7,6},{8,9},{9,8},{10,11... | collective-permute-start | bytes 138248 | tf_op jit(solution)/shard_map/ppermute | solution.py:512
  48.6 13.6 %copy-start.4 = (f32[2,2048]{1,0:T(2,128)S(1)}, f32[2,2048]{1,0:T(2,128)}, u32[]{:S(2)}) copy-start(f32[2,2048]{1,0:T(2,128)} %centres.3) | copy-start | bytes 49156
  48.6 13.6 %copy-start.5 = (f32[2,2048]{1,0:T(2,128)S(1)}, f32[2,2048]{1,0:T(2,128)}, u32[]{:S(2)}) copy-start(f32[2,2048]{1,0:T(2,128)} %conic.3) | copy-start | bytes 49156
  48.7 13.6 %copy-start.6 = (s32[1,2048]{1,0:T(1,128)S(1)}, s32[1,2048]{1,0:T(1,128)}, u32[]{:S(2)}) copy-start(s32[1,2048]{1,0:T(1,128)} %rows_ref.3) | copy-start | bytes 24580
  48.7 13.6 %copy-start.7 = (f32[1,2048]{1,0:T(1,128)S(1)}, f32[1,2048]{1,0:T(1,128)}, u32[]{:S(2)}) copy-start(f32[1,2048]{1,0:T(1,128)} %rho.3) | copy-start | bytes 24580
  48.7 13.6 %copy-start.8 = (f32[1,2048]{1,0:T(1,128)S(1)}, f32[1,2048]{1,0:T(1,128)}, u32[]{:S(2)}) copy-start(f32[1,2048]{1,0:T(1,128)} %opacity.3) | copy-start | bytes 24580
